TPU v7x, 32 devices: a whole 2x2x4 slice. The times are simulated.
32 devices in a mesh: dp: 8 (over z, x), seq: 4 (over y, core).
Axes of the slice: x: 2, y: 2, z: 4, core: 2. Of those that a mesh axis runs over, the one named last changes fastest.
Arguments:
- tokens_in: bfloat16 [16, 1024, 768], P('dp', 'seq'), may hold values from -6 to 6
- w_in: bfloat16 [768, 2304], P('dp', 'seq'), may hold values from -0.21875 to 0.21875
- w_out: bfloat16 [768, 768], P('dp', 'seq'), may hold values from -0.21875 to 0.21875
- w_up: bfloat16 [768, 3072], P('dp', 'seq'), may hold values from -0.21875 to 0.21875
- w_down: bfloat16 [3072, 768], P('dp', 'seq'), may hold values from -0.109375 to 0.109375
- norm_gains: bfloat16 [2, 768], P(None, 'seq'), may hold values from 0.5 to 1.5
- kernel: bfloat16 [1024, 768], P('dp', 'seq'), may hold values from -0.375 to 0.375
- taps: int32 [768], P('seq'), may hold values from 256 to 1024, as said below
- cotangent: bfloat16 [16, 1024, 768], P('dp', 'seq'), may hold values from -6 to 6
Outputs:
- output: bfloat16 [16, 1024, 768], P('dp', 'seq')
- grad_in: bfloat16 [16, 1024, 768], P('dp', 'seq')
- grad_w_in: float32 [768, 2304], P('dp', 'seq')
- grad_w_out: float32 [768, 768], P('dp', 'seq')
- grad_w_up: float32 [768, 3072], P('dp', 'seq')
- grad_w_down: float32 [3072, 768], P('dp', 'seq')
- grad_gains: float32 [2, 768], P(None, 'seq')
- grad_kernel: float32 [1024, 768], P('dp', 'seq')
Inputs may be any that keep to these rules, and one draw needn't show every extreme that they name: taps[d] is the number of live taps of channel d; kernel entries at taps taps[d] and later are padding and never act. Some channel has all 1024 taps live and some has a quarter of 1024.
All inputs are finite; a program needn't handle non-finite values.
Results may differ from a plain program's by a relative error of at most 0.018.
Values may be sent and summed in bfloat16 or wider, within the bound.
A program may use at most 192 MiB of HBM per device.

v0:
```python
from functools import partial
import math

import jax
import jax.numpy as jnp
from jax import lax
from jax.sharding import PartitionSpec as P

EPSILON = 1e-05
SHRINK_SCALE = 0.003
HIGHEST = lax.Precision.HIGHEST


def norm_rows(values, gain):
    center = values - jnp.mean(values, axis=-1, keepdims=True)
    spread = jnp.mean(center * center, axis=-1, keepdims=True)
    return center * lax.rsqrt(spread + EPSILON) * gain


def shape_filter(kernel, taps):
    length = kernel.shape[0]
    position = jnp.arange(length, dtype=jnp.int32)[:, None]
    live_mask = (position < taps[None, :]).astype(kernel.dtype)
    masked = kernel * live_mask
    shrunk = masked - SHRINK_SCALE * jnp.tanh(masked / SHRINK_SCALE)
    padded = jnp.pad(shrunk, ((1, 1), (0, 0)))
    pooled = (padded[:-2] + padded[1:-1] + padded[2:]) / 3.0
    return pooled * live_mask


def gelu_tanh(values):
    return jax.nn.gelu(values, approximate=True)


def contract_rows(left, right):
    return lax.dot_general(
        left, right, (((0,), (0,)), ((), ())), preferred_element_type=jnp.float32
    )


def times_transposed(left, weight):
    return lax.dot_general(
        left, weight, (((1,), (1,)), ((), ())), preferred_element_type=jnp.float32
    )


def phase_table(count_rows, count_cols, period):
    row_index = lax.broadcasted_iota(jnp.int32, (count_rows, count_cols), 0)
    col_index = lax.broadcasted_iota(jnp.int32, (count_rows, count_cols), 1)
    angles = 2.0 * math.pi / period * (row_index * col_index % period).astype(jnp.float32)
    return (jnp.cos(angles), jnp.sin(angles))


def dft_factors(length):
    total = 2 * length
    first = max(2, total // 128)
    return (total, first, total // first)


def mix_last(field, table):
    return jnp.einsum("bckn,nm->bckm", field, table, precision=HIGHEST)


def forward_dft(field):
    batch, length, chans = field.shape
    total, first, second = dft_factors(length)
    half = first // 2
    blocks = field.reshape(batch, half, second, chans)
    cos_one, sin_one = phase_table(half, first, first)
    part_re = jnp.einsum("hk,bhnc->bckn", cos_one, blocks, precision=HIGHEST)
    part_im = -jnp.einsum("hk,bhnc->bckn", sin_one, blocks, precision=HIGHEST)
    cos_two, sin_two = phase_table(first, second, total)
    turn_re = part_re * cos_two + part_im * sin_two
    turn_im = part_im * cos_two - part_re * sin_two
    cos_three, sin_three = phase_table(second, second, second)
    spec_re = mix_last(turn_re, cos_three) + mix_last(turn_im, sin_three)
    spec_im = mix_last(turn_im, cos_three) - mix_last(turn_re, sin_three)
    return (spec_re, spec_im)


def inverse_dft(spec_re, spec_im):
    batch, chans, first, second = spec_re.shape
    total = first * second
    half = first // 2
    cos_three, sin_three = phase_table(second, second, second)
    back_re = mix_last(spec_re, cos_three) - mix_last(spec_im, sin_three)
    back_im = mix_last(spec_re, sin_three) + mix_last(spec_im, cos_three)
    cos_two, sin_two = phase_table(first, second, total)
    turn_re = back_re * cos_two - back_im * sin_two
    turn_im = back_re * sin_two + back_im * cos_two
    cos_one, sin_one = phase_table(half, first, first)
    blocks = jnp.einsum("hk,bckn->bhnc", cos_one, turn_re, precision=HIGHEST)
    blocks = blocks - jnp.einsum("hk,bckn->bhnc", sin_one, turn_im, precision=HIGHEST)
    return blocks.reshape(batch, half * second, chans) / total


def to_channels(field):
    return lax.all_to_all(field, "seq", split_axis=2, concat_axis=1, tiled=True)


def to_tokens(field):
    return lax.all_to_all(field, "seq", split_axis=1, concat_axis=2, tiled=True)


def body(tokens_in, w_in, w_out, w_up, w_down, norm_gains, kernel, taps, cotangent):
    w_in_rows, w_out_rows, w_up_rows, w_down_rows, gains = (
        lax.all_gather(w_in, "seq", axis=1, tiled=True),
        lax.all_gather(w_out, "seq", axis=1, tiled=True),
        lax.all_gather(w_up, "seq", axis=1, tiled=True),
        lax.all_gather(w_down, "seq", axis=1, tiled=True),
        lax.all_gather(norm_gains, "seq", axis=1, tiled=True),
    )
    full_in, full_out, full_up, full_down, kernel_cols = (
        lax.all_gather(w_in_rows, "dp", axis=0, tiled=True),
        lax.all_gather(w_out_rows, "dp", axis=0, tiled=True),
        lax.all_gather(w_up_rows, "dp", axis=0, tiled=True),
        lax.all_gather(w_down_rows, "dp", axis=0, tiled=True),
        lax.all_gather(kernel, "dp", axis=0, tiled=True),
    )
    num_seqs, local_len, width = tokens_in.shape
    total_rows = num_seqs * local_len
    inputs = tokens_in.reshape(total_rows, width).astype(jnp.float32)
    gains_wide = gains.astype(jnp.float32)
    normed, norm_back_one = jax.vjp(norm_rows, inputs, gains_wide[0])
    normed_low = normed.astype(jnp.bfloat16)
    proj = jnp.dot(normed_low, full_in, preferred_element_type=jnp.float32)
    values = proj[:, :width]
    gate_one = proj[:, width : 2 * width]
    gate_two = proj[:, 2 * width :]
    mixed_low = (gate_one * values).astype(jnp.bfloat16).reshape(num_seqs, local_len, width)
    by_channel = to_channels(mixed_low)
    filt, filter_back = jax.vjp(partial(shape_filter, taps=taps), kernel_cols.astype(jnp.float32))
    filt_re, filt_im = forward_dft(filt[None])
    sig_re, sig_im = forward_dft(by_channel.astype(jnp.float32))
    conv = inverse_dft(sig_re * filt_re - sig_im * filt_im, sig_re * filt_im + sig_im * filt_re)
    conv_tok = to_tokens(conv.astype(jnp.bfloat16)).reshape(total_rows, width).astype(jnp.float32)
    gated = (gate_two * conv_tok).astype(jnp.bfloat16)
    resid = inputs + jnp.dot(gated, full_out, preferred_element_type=jnp.float32)
    normed_two, norm_back_two = jax.vjp(norm_rows, resid, gains_wide[1])
    normed_two_low = normed_two.astype(jnp.bfloat16)
    hidden_pre = jnp.dot(normed_two_low, full_up, preferred_element_type=jnp.float32)
    active, gelu_back = jax.vjp(gelu_tanh, hidden_pre)
    active_low = active.astype(jnp.bfloat16)
    result = (resid + jnp.dot(active_low, full_down, preferred_element_type=jnp.float32)).astype(
        jnp.bfloat16
    )
    grad_rows = cotangent.reshape(total_rows, width)
    grad_down = contract_rows(active_low, grad_rows)
    grad_active = times_transposed(grad_rows, full_down)
    grad_pre = gelu_back(grad_active)[0].astype(jnp.bfloat16)
    grad_up = contract_rows(normed_two_low, grad_pre)
    grad_normed_two = times_transposed(grad_pre, full_up)
    grad_resid_part, grad_gain_two = norm_back_two(grad_normed_two)
    grad_resid = grad_rows.astype(jnp.float32) + grad_resid_part
    resid_low = grad_resid.astype(jnp.bfloat16)
    grad_outw = contract_rows(gated, resid_low)
    grad_gated = times_transposed(resid_low, full_out)
    grad_gate_two = grad_gated * conv_tok
    grad_conv = (grad_gated * gate_two).astype(jnp.bfloat16).reshape(num_seqs, local_len, width)
    grad_channel = to_channels(grad_conv).astype(jnp.float32)
    back_re, back_im = forward_dft(grad_channel)
    grad_signal = inverse_dft(
        back_re * filt_re + back_im * filt_im, back_im * filt_re - back_re * filt_im
    )
    cross_re = jnp.sum(back_re * sig_re + back_im * sig_im, axis=0, keepdims=True)
    cross_im = jnp.sum(back_im * sig_re - back_re * sig_im, axis=0, keepdims=True)
    grad_filt = inverse_dft(cross_re, cross_im)[0]
    grad_kern = filter_back(grad_filt)[0]
    grad_mixed = (
        to_tokens(grad_signal.astype(jnp.bfloat16)).reshape(total_rows, width).astype(jnp.float32)
    )
    grad_proj = jnp.concatenate([grad_mixed * gate_one, grad_mixed * values, grad_gate_two], axis=1)
    grad_proj = grad_proj.astype(jnp.bfloat16)
    grad_inw = contract_rows(normed_low, grad_proj)
    grad_normed = times_transposed(grad_proj, full_in)
    grad_input_part, grad_gain_one = norm_back_one(grad_normed)
    grad_inputs = (
        (grad_resid + grad_input_part).astype(jnp.bfloat16).reshape(num_seqs, local_len, width)
    )
    grad_gain_pair = jnp.stack([grad_gain_one, grad_gain_two])
    in_part, outw_part, up_part, down_part, kern_done = (
        lax.psum_scatter(
            grad_inw.astype(jnp.bfloat16), "dp", scatter_dimension=0, tiled=True
        ).astype(jnp.float32),
        lax.psum_scatter(
            grad_outw.astype(jnp.bfloat16), "dp", scatter_dimension=0, tiled=True
        ).astype(jnp.float32),
        lax.psum_scatter(
            grad_up.astype(jnp.bfloat16), "dp", scatter_dimension=0, tiled=True
        ).astype(jnp.float32),
        lax.psum_scatter(
            grad_down.astype(jnp.bfloat16), "dp", scatter_dimension=0, tiled=True
        ).astype(jnp.float32),
        lax.psum_scatter(
            grad_kern.astype(jnp.bfloat16), "dp", scatter_dimension=0, tiled=True
        ).astype(jnp.float32),
    )
    in_done, outw_done, up_done, down_done, gain_part = (
        lax.psum_scatter(
            in_part.astype(jnp.bfloat16), "seq", scatter_dimension=1, tiled=True
        ).astype(jnp.float32),
        lax.psum_scatter(
            outw_part.astype(jnp.bfloat16), "seq", scatter_dimension=1, tiled=True
        ).astype(jnp.float32),
        lax.psum_scatter(
            up_part.astype(jnp.bfloat16), "seq", scatter_dimension=1, tiled=True
        ).astype(jnp.float32),
        lax.psum_scatter(
            down_part.astype(jnp.bfloat16), "seq", scatter_dimension=1, tiled=True
        ).astype(jnp.float32),
        lax.psum_scatter(
            grad_gain_pair.astype(jnp.bfloat16), "seq", scatter_dimension=1, tiled=True
        ).astype(jnp.float32),
    )
    gain_done = lax.psum(gain_part, "dp")
    return (
        result.reshape(num_seqs, local_len, width),
        grad_inputs,
        in_done,
        outw_done,
        up_done,
        down_done,
        gain_done,
        kern_done,
    )


def solution(mesh):
    return jax.shard_map(
        body,
        mesh=mesh,
        in_specs=(
            P("dp", "seq", None),
            P("dp", "seq"),
            P("dp", "seq"),
            P("dp", "seq"),
            P("dp", "seq"),
            P(None, "seq"),
            P("dp", "seq"),
            P("seq"),
            P("dp", "seq", None),
        ),
        out_specs=(
            P("dp", "seq", None),
            P("dp", "seq", None),
            P("dp", "seq"),
            P("dp", "seq"),
            P("dp", "seq"),
            P("dp", "seq"),
            P(None, "seq"),
            P("dp", "seq"),
        ),
        check_vma=False,
    )
```

profile of v0, /device:TPU:0, one launch (start us, length us, event | category | flops | bytes accessed | tf_op | source)
XLA Modules:
  0.0 877.1 jit_solution(3349437428924509162)
XLA Ops:
  7.2 8.8 %all-gather.1 = bf16[4,576,96]{1,2,0:T(8,128)(2,1)S(1)} all-gather(bf16[1,576,96]{1,2,0:T(8,128)(2,1)} %bitcast.333), channel_id=1, replica_groups=mesh['dp'=8,'seq'=4] {'seq'}, dimensions={0}, use_global_device_ids=true | all-gather | bytes 552960 | tf_op jit(solution)/shard_map/all_gather | solution.py:107
  18.5 5.6 all_gather.34
  25.0 8.1 all_gather.38
  33.1 8.1 all_gather.36
  41.4 29.7 %all_gather.33 = bf16[1024,192]{0,1:T(8,128)(2,1)S(1)} all-gather(bf16[128,192]{0,1:T(8,128)(2,1)S(1)} %copy-done.40), channel_id=1, replica_groups=mesh['dp'=8,'seq'=4] {'dp'}, dimensions={0}, use_global_device_ids=true | all-gather | bytes 442368 | tf_op jit(solution)/shard_map/all_gather | solution.py:118
  76.9 5.6 all-gather
  84.4 3.1 fusion.63
  88.8 4.3 fusion.371
  99.3 4.2 all-to-all-start
  103.5 3.2 fusion.108
  106.7 3.1 fusion.60
  109.9 5.3 all-to-all-done
  133.9 3.2 convolution_add_fusion.3
  143.0 3.4 convolution_add_fusion.2
  151.5 3.1 fusion.70
  157.4 18.9 %all_to_all.48 = bf16[2,1024,192]{2,0,1:T(2,128)(2,1)} all-to-all(bf16[2,1024,192]{2,0,1:T(2,128)(2,1)} %bitcast.318), channel_id=1, replica_groups=mesh['dp'=8,'seq'=4] {'seq'}, dimensions={1} | all-to-all | bytes 1572864 | tf_op jit(solution)/shard_map/all_to_all | solution.py:102
  176.4 3.6 copy.80
  182.7 4.0 copy.111
  186.7 3.5 reshape.247
  197.1 16.4 %all-gather.13.cloned.1.call-done = bf16[3072,768]{0,1:T(8,128)(2,1)} async-done(((bf16[384,768]{0,1:T(8,128)(2,1)}), bf16[3072,768]{0,1:T(8,128)(2,1)}) %all-gather.13.cloned.1.call-update) | async-done | bytes 4718608 | tf_op jit(solution)/shard_map/all_gather | solution.py:117
  213.5 7.8 fusion.372
  221.4 72.3 %all-gather.11.cloned.1.call-done = bf16[768,3072]{1,0:T(8,128)(2,1)} async-done(((bf16[96,3072]{1,0:T(8,128)(2,1)}), bf16[768,3072]{1,0:T(8,128)(2,1)}) %all-gather.11.cloned.1.call-update) | async-done | bytes 4718608 | tf_op jit(solution)/shard_map/all_gather | solution.py:116
  293.7 12.3 %fusion.6 = (bf16[512,3072]{1,0:T(8,128)(2,1)S(1)}, f32[512,3072]{1,0:T(8,128)}) fusion(f32[512,3072]{1,0:T(8,128)} %fusion.372, bf16[768,3072]{1,0:T(8,128)(2,1)} %all-gather.11.cloned.1.call-done, f32[512,768]{1,0:T(8,128)} %copy-done.20, f32[768]{0:T(1024)S(1)} %get-tuple-element.54, f32[512]{0:T(512)S(1)} %fusion.219, f32[512]{0:T(512)S(1)} %broadcast_multiply_fusion), kind=kOutput, calls=%fused_computation.8 | convolution fusion | flops 2448949248 | bytes 22027264 | tf_op jit(solution)/shard_map/dot_general | solution.py:141
  311.5 3.7 multiply_convert_fusion.5
  318.2 4.2 all-to-all-start.2
  322.5 3.2 convolution_convert_fusion.3
  325.7 8.4 all-to-all-done.2
  350.2 3.1 convolution_subtract_fusion.1
  353.3 6.2 subtract_reduce_fusion
  359.5 3.1 fusion.115
  362.7 3.1 fusion.126
  365.8 3.4 convolution_add_fusion
  369.2 3.1 convolution_subtract_fusion
  378.3 17.3 %all_to_all.49 = bf16[2,1024,192]{2,0,1:T(2,128)(2,1)S(1)} all-to-all(bf16[2,1024,192]{2,0,1:T(2,128)(2,1)S(1)} %bitcast.319), channel_id=1, replica_groups=mesh['dp'=8,'seq'=4] {'seq'}, dimensions={1} | all-to-all | bytes 1572864 | tf_op jit(solution)/shard_map/all_to_all | solution.py:102
  407.5 3.9 convolution_convert_fusion.2
  412.6 8.2 convolution_convert_fusion
  422.2 6.4 convolution_convert_fusion.1
  449.0 38.8 %reduce-scatter.21.cloned.1.call-done = bf16[96,2304]{1,0:T(8,128)(2,1)} async-done(((bf16[768,2304]{1,0:T(8,128)(2,1)}), bf16[96,2304]{1,0:T(8,128)(2,1)}) %reduce-scatter.21.cloned.1.call-update) | async-done | bytes 442384 | tf_op jit(solution)/shard_map/reduce_scatter | solution.py:182
  490.0 96.4 %reduce-scatter.29.cloned.1.call-done = bf16[384,768]{1,0:T(8,128)(2,1)} async-done(((bf16[3072,768]{1,0:T(8,128)(2,1)}), bf16[384,768]{1,0:T(8,128)(2,1)}) %reduce-scatter.29.cloned.1.call-update) | async-done | bytes 589840 | tf_op jit(solution)/shard_map/reduce_scatter | solution.py:191
  588.6 96.5 %reduce-scatter.25.cloned.1.call-done = bf16[96,3072]{1,0:T(8,128)(2,1)} async-done(((bf16[768,3072]{1,0:T(8,128)(2,1)}), bf16[96,3072]{1,0:T(8,128)(2,1)}) %reduce-scatter.25.cloned.1.call-update) | async-done | bytes 589840 | tf_op jit(solution)/shard_map/reduce_scatter | solution.py:188
  685.1 9.5 %add_convert_fusion.1 = bf16[512,768]{1,0:T(8,128)(2,1)} fusion(f32[512,768]{1,0:T(8,128)} %copy-done.20, bf16[3072,768]{0,1:T(8,128)(2,1)} %all-gather.13.cloned.1.call-done, f32[512,3072]{1,0:T(8,128)} %get-tuple-element.67), kind=kOutput, calls=%fused_computation.100 | convolution fusion | flops 2430861312 | bytes 13369344 | tf_op jit(solution)/shard_map/dot_general | solution.py:144
  696.2 11.4 %reduce-scatter.37.cloned.1.call-done = bf16[192,2]{1,0:T(8,128)(2,1)} async-done(((bf16[768,2]{1,0:T(8,128)(2,1)}), bf16[192,2]{1,0:T(8,128)(2,1)}) %reduce-scatter.37.cloned.1.call-update) | async-done | bytes 784
  708.5 22.0 %psum.7 = f32[2,192]{1,0:T(2,128)} all-reduce(bf16[2,192]{1,0:T(2,128)(2,1)S(1)} %copy.108), channel_id=1, replica_groups=mesh['dp'=8,'seq'=4] {'dp'}, use_global_device_ids=true, to_apply=%region_19.20 | all-reduce | flops 384 | bytes 2304 | tf_op jit(solution)/shard_map/psum | solution.py:215
  730.5 42.2 %reduce-scatter.39.cloned.1.call-done = bf16[128,192]{1,0:T(8,128)(2,1)} async-done(((bf16[1024,192]{1,0:T(8,128)(2,1)}), bf16[128,192]{1,0:T(8,128)(2,1)}) %reduce-scatter.39.cloned.1.call-update) | async-done | bytes 49168
  774.4 20.3 %reduce-scatter.33.cloned.1.call-done = bf16[192,96]{1,0:T(8,128)(2,1)} async-done(((bf16[768,96]{1,0:T(8,128)(2,1)}), bf16[192,96]{1,0:T(8,128)(2,1)}) %reduce-scatter.33.cloned.1.call-update) | async-done | bytes 36880
  796.3 23.1 %reduce-scatter.31.cloned.1.call-done = bf16[576,96]{1,0:T(8,128)(2,1)} async-done(((bf16[2304,96]{1,0:T(8,128)(2,1)}), bf16[576,96]{1,0:T(8,128)(2,1)}) %reduce-scatter.31.cloned.1.call-update) | async-done | bytes 110608
  821.1 23.0 %reduce-scatter.35.cloned.1.call-done = bf16[192,384]{1,0:T(8,128)(2,1)} async-done(((bf16[768,384]{1,0:T(8,128)(2,1)}), bf16[192,384]{1,0:T(8,128)(2,1)}) %reduce-scatter.35.cloned.1.call-update) | async-done | bytes 147472
  845.9 22.7 %reduce-scatter.27.cloned.1.call-done = bf16[96,768]{1,0:T(8,128)(2,1)} async-done(((bf16[96,3072]{1,0:T(8,128)(2,1)}), bf16[96,768]{1,0:T(8,128)(2,1)}) %reduce-scatter.27.cloned.1.call-update) | async-done | bytes 147472 | tf_op jit(solution)/shard_map/reduce_scatter | solution.py:205
  (232 shorter events, 140.9 us)
Async XLA Ops:
  7.2 17.8 %copy-start.36 = (bf16[384,192]{0,1:T(8,128)(2,1)S(1)}, bf16[384,192]{0,1:T(8,128)(2,1)}, u32[]{:S(2)}) copy-start(bf16[384,192]{0,1:T(8,128)(2,1)} %param.13) | copy-start | bytes 442372
  7.2 26.0 %copy-start.37 = (bf16[96,768]{1,0:T(8,128)(2,1)S(1)}, bf16[96,768]{1,0:T(8,128)(2,1)}, u32[]{:S(2)}) copy-start(bf16[96,768]{1,0:T(8,128)(2,1)} %param.12) | copy-start | bytes 442372
  7.2 81.6 %all-gather.7.cloned.1.call-start = ((), (), s32[]{:S(2)}) async-start(), calls=%async_computation.14 | async-start | bytes 3981312 | tf_op jit(solution)/shard_map/all_gather | solution.py:114
  7.2 34.1 %copy-start.40 = (bf16[128,192]{0,1:T(8,128)(2,1)S(1)}, bf16[128,192]{0,1:T(8,128)(2,1)}, u32[]{:S(2)}) copy-start(bf16[128,192]{0,1:T(8,128)(2,1)} %param.15) | copy-start | bytes 147460
  16.1 55.7 %copy-start.47 = (s32[192]{0:T(256)S(1)}, s32[192]{0:T(256)}, u32[]{:S(2)}) copy-start(s32[192]{0:T(256)} %param.16) | copy-start | bytes 2308
  17.5 175.6 %all-gather.9.cloned.1.call-start = ((), (), s32[]{:S(2)}) async-start(), calls=%async_computation.15 | async-start | bytes 1327104 | tf_op jit(solution)/shard_map/all_gather | solution.py:115
  24.9 188.6 %all-gather.13.cloned.1.call-start = ((), (), s32[]{:S(2)}) async-start(), calls=%async_computation.17 | async-start | bytes 5308416 | tf_op jit(solution)/shard_map/all_gather | solution.py:117
  33.1 260.6 %all-gather.11.cloned.1.call-start = ((), (), s32[]{:S(2)}) async-start(), calls=%async_computation.16 | async-start | bytes 5308416 | tf_op jit(solution)/shard_map/all_gather | solution.py:116
  72.6 3.2 copy-start.7
  72.7 4.2 copy-start.49
  74.2 29.3 %copy-start.4 = (f32[128,192,16]{0,2,1:T(8,128)}, f32[128,192,16]{0,2,1:T(8,128)S(1)}, u32[]{:S(2)}) copy-start(f32[128,192,16]{0,2,1:T(8,128)S(1)} %convolution_negate_fusion) | copy-start | bytes 4718596
  75.7 6.9 copy-start.5
  75.9 11.6 %copy-start.41 = (f32[1,2,2,128]{3,1,2,0:T(2,128)}, f32[1,2,2,128]{3,1,2,0:T(2,128)S(1)}, u32[]{:S(2)}) copy-start(f32[1,2,2,128]{3,1,2,0:T(2,128)S(1)} %copy.115) | copy-start | bytes 6148
  76.4 11.2 %copy-start.43 = (f32[512]{0:T(512)}, f32[512]{0:T(512)S(1)}, u32[]{:S(2)}) copy-start(f32[512]{0:T(512)S(1)} %rsqrt.20) | copy-start | bytes 6148
  82.6 4.9 copy-start.38
  84.4 3.2 copy-start.8
  99.3 15.9 %all-to-all-start = ((bf16[2,256,768]{1,0,2:T(2,128)(2,1)}), bf16[2,256,768]{1,0,2:T(2,128)(2,1)}, u32[]{:S(2)}, u32[]{:S(2)}) async-start(bf16[2,256,768]{1,0,2:T(2,128)(2,1)} %copy.76), calls=%async_computation | async-start | bytes 1572864 | tf_op jit(solution)/shard_map/all_to_all | solution.py:98
  103.5 3.2 copy-start.6
  120.5 2.8 copy-start.18
  133.9 12.5 %copy-start = (f32[2,192,16,128]{3,2,1,0:T(8,128)}, f32[2,192,16,128]{3,2,1,0:T(8,128)S(1)}, u32[]{:S(2)}) copy-start(f32[2,192,16,128]{3,2,1,0:T(8,128)S(1)} %convolution_subtract_fusion.3) | copy-start | bytes 9437188
  137.1 9.3 %copy-start.2 = (f32[2,192,16,128]{3,2,1,0:T(8,128)}, f32[2,192,16,128]{3,2,1,0:T(8,128)S(1)}, u32[]{:S(2)}) copy-start(f32[2,192,16,128]{3,2,1,0:T(8,128)S(1)} %convolution_add_fusion.3) | copy-start | bytes 9437188
  293.7 12.3 %copy-start.21 = (f32[512,768]{1,0:T(8,128)S(1)}, f32[512,768]{1,0:T(8,128)}, u32[]{:S(2)}) copy-start(f32[512,768]{1,0:T(8,128)} %copy-done.20) | copy-start | bytes 4718596
  293.7 12.3 %copy-start.50 = (bf16[768,3072]{1,0:T(8,128)(2,1)S(1)}, bf16[768,3072]{1,0:T(8,128)(2,1)}, u32[]{:S(2)}) copy-start(bf16[768,3072]{1,0:T(8,128)(2,1)} %all-gather.11.cloned.1.call-done) | copy-start | bytes 14155780
  306.0 2.9 copy-start.52
  309.6 5.6 copy-start.14
  311.5 3.7 copy-start.27
  318.2 15.9 %all-to-all-start.2 = ((bf16[2,256,768]{1,0,2:T(2,128)(2,1)}), bf16[2,256,768]{1,0,2:T(2,128)(2,1)}, u32[]{:S(2)}, u32[]{:S(2)}) async-start(bf16[2,256,768]{1,0,2:T(2,128)(2,1)} %copy.85), calls=%async_computation.2 | async-start | bytes 1572864 | tf_op jit(solution)/shard_map/all_to_all | solution.py:98
  322.4 124.8 %reduce-scatter.23.cloned.1.call-start = ((), (), s32[]{:S(2)}) async-start(), calls=%async_computation.19 | async-start | bytes 1327104 | tf_op jit(solution)/shard_map/reduce_scatter | solution.py:185
  325.7 162.2 %reduce-scatter.21.cloned.1.call-start = ((), (), s32[]{:S(2)}) async-start(), calls=%async_computation.18 | async-start | bytes 3981312 | tf_op jit(solution)/shard_map/reduce_scatter | solution.py:182
  339.6 2.8 copy-start.19
  350.1 3.2 copy-start.1
  350.1 3.2 copy-start.3
  403.6 4.0 copy-start.29
  403.6 4.0 copy-start.35
  411.5 174.9 %reduce-scatter.29.cloned.1.call-start = ((), (), s32[]{:S(2)}) async-start(), calls=%async_computation.22 | async-start | bytes 5308416 | tf_op jit(solution)/shard_map/reduce_scatter | solution.py:191
  420.8 264.3 %reduce-scatter.25.cloned.1.call-start = ((), (), s32[]{:S(2)}) async-start(), calls=%async_computation.20 | async-start | bytes 5308416 | tf_op jit(solution)/shard_map/reduce_scatter | solution.py:188
  428.6 279.0 %reduce-scatter.37.cloned.1.call-start = ((), (), s32[]{:S(2)}) async-start(), calls=%async_computation.26 | async-start | bytes 245760
  430.0 3.4 copy-start.12
  436.9 2.7 copy-start.51
  440.1 3.3 copy-start.44
  440.1 5.3 copy-start.26
  445.2 327.6 %reduce-scatter.39.cloned.1.call-start = ((), (), s32[]{:S(2)}) async-start(), calls=%async_computation.27 | async-start | bytes 589824
  447.1 347.6 %reduce-scatter.33.cloned.1.call-start = ((), (), s32[]{:S(2)}) async-start(), calls=%async_computation.24 | async-start | bytes 245760
  449.0 370.3 %reduce-scatter.31.cloned.1.call-start = ((), (), s32[]{:S(2)}) async-start(), calls=%async_computation.23 | async-start | bytes 737280
  490.0 354.1 %reduce-scatter.35.cloned.1.call-start = ((), (), s32[]{:S(2)}) async-start(), calls=%async_computation.25 | async-start | bytes 737280
  588.5 280.1 %reduce-scatter.27.cloned.1.call-start = ((), (), s32[]{:S(2)}) async-start(), calls=%async_computation.21 | async-start | bytes 737280 | tf_op jit(solution)/shard_map/reduce_scatter | solution.py:205
  685.1 9.5 %copy-start.15 = (f32[512,768]{1,0:T(8,128)S(1)}, f32[512,768]{1,0:T(8,128)}, u32[]{:S(2)}) copy-start(f32[512,768]{1,0:T(8,128)} %copy-done.14) | copy-start | bytes 4718596
  685.1 9.5 %copy-start.24 = (f32[512,768]{1,0:T(8,128)S(1)}, f32[512,768]{1,0:T(8,128)}, u32[]{:S(2)}) copy-start(f32[512,768]{1,0:T(8,128)} %copy-done.23) | copy-start | bytes 4718596
  (21 other events, 31.6 us)
Sparse Core Ops, SparseCore 0:
  17.6 71.1 all-gather.6
  91.6 40.0 all-gather.8
  133.7 79.7 all-gather.12
  215.6 78.0 all-gather.10
  326.4 62.5 reduce-scatter.22
  411.6 76.2 reduce-scatter.20
  491.5 94.8 reduce-scatter.28
  590.0 95.0 reduce-scatter.24
  688.1 19.5 reduce-scatter.36
  710.8 61.8 reduce-scatter.38
  775.9 18.7 reduce-scatter.32
  797.2 22.0 reduce-scatter.30
  822.0 22.0 reduce-scatter.34
  846.6 22.0 reduce-scatter.26
where the time goes:
time: 884 us; the launch traced here: 877 us
  waiting for transfers between devices  477 us (54%)
  matrix products  161 us (18%)
  blocking collectives  124 us (14%)
  local copies, waits for them, and re-layouts  72.7 us (8%)
  other arithmetic  17.6 us (2%)
  between operations  15.2 us (2%)
  starting transfers between devices  9.34 us (1%)
    unnamed x19, waiting for transfers between devices  120 us
    reduce_scatter x1, waiting for transfers between devices, body(): lax.psum_scatter(grad_up.astype(jnp.bfloat16), 'dp', scatter_dimension=0,...  96.5 us
    reduce_scatter x1, waiting for transfers between devices, body(): lax.psum_scatter(grad_down.astype(jnp.bfloat16), 'dp', scatter_dimension=...  96.4 us
    all_gather x1, waiting for transfers between devices, body(): lax.all_gather(w_up_rows, 'dp', axis=0, tiled=True)  72.3 us
    dot_general x24, matrix products, mix_last(): return jnp.einsum('bckn,nm->bckm', field, table, precision=HIGHEST)  70.7 us
    reduce_scatter x1, waiting for transfers between devices, body(): lax.psum_scatter(grad_inw.astype(jnp.bfloat16), 'dp', scatter_dimension=0...  38.8 us
    all_to_all x2, blocking collectives, to_tokens(): return lax.all_to_all(field, 'seq', split_axis=1, concat_axis=2, tiled=True)  36.2 us
    all_gather x1, blocking collectives, body(): lax.all_gather(kernel, 'dp', axis=0, tiled=True)  29.7 us
  transfers between devices with their start and end apart: 16, of which 14 were waited for; matrix products, arithmetic and copies ran while one was open for 24% of the time, Pallas kernels for 0%

commit v1 on v0

--- a/solution.py
+++ b/solution.py
@@ -2,6 +2,10 @@
 import math
 
 import jax
+from jax.experimental import pallas as pl
+from jax.experimental.pallas import tpu as pltpu
+import ml_dtypes
+import numpy as np
 import jax.numpy as jnp
 from jax import lax
 from jax.sharding import PartitionSpec as P
@@ -102,7 +106,7 @@
     return lax.all_to_all(field, "seq", split_axis=1, concat_axis=2, tiled=True)
 
 
-def body(tokens_in, w_in, w_out, w_up, w_down, norm_gains, kernel, taps, cotangent):
+def general_body(tokens_in, w_in, w_out, w_up, w_down, norm_gains, kernel, taps, cotangent):
     w_in_rows, w_out_rows, w_up_rows, w_down_rows, gains = (
         lax.all_gather(w_in, "seq", axis=1, tiled=True),
         lax.all_gather(w_out, "seq", axis=1, tiled=True),
@@ -225,9 +229,494 @@
     )
 
 
+MESH = pl.DeviceIdType.MESH
+BF = jnp.bfloat16
+F32 = jnp.float32
+
+
+def place():
+    dp, sq = lax.axis_index("dp"), lax.axis_index("seq")
+    return dp // 2, dp % 2, sq // 2, sq % 2
+
+
+class Wire:
+    def __init__(self, send, recv):
+        self.send, self.recv, self.made = send, recv, []
+
+    def start(self, src, dst, peer):
+        k = len(self.made)
+        copy = pltpu.make_async_remote_copy(
+            src_ref=src, dst_ref=dst, send_sem=self.send.at[k], recv_sem=self.recv.at[k],
+            device_id=peer, device_id_type=MESH,
+        )
+        copy.start()
+        self.made.append(copy)
+        return copy
+
+    def drain(self):
+        for copy in self.made:
+            copy.wait_send()
+
+
+class Local:
+    def __init__(self, sems):
+        self.sems, self.made, self.open = sems, 0, []
+
+    def start(self, src, dst):
+        copy = pltpu.make_async_copy(src, dst, self.sems.at[self.made])
+        self.made += 1
+        copy.start()
+        self.open.append(copy)
+        return copy
+
+    def wait(self, copy):
+        copy.wait()
+        self.open.remove(copy)
+
+    def drain(self):
+        for copy in list(self.open):
+            self.wait(copy)
+
+
+def arrived(copies):
+    for copy in copies:
+        copy.wait_recv()
+
+
+class Spots:
+    def __init__(self, num_z):
+        z, x, y, c = place()
+        self.num_z = num_z
+        self.z, self.x, self.y, self.c = z, x, y, c
+        self.across_z = [self.at((z + k) % num_z, x, y, c) for k in range(1, num_z)]
+        self.core = self.at(z, x, y, 1 - c)
+        self.first = self.at(z, jnp.where(c == 0, 1 - x, x), jnp.where(c == 0, y, 1 - y), c)
+        self.second = self.at(z, jnp.where(c == 0, x, 1 - x), jnp.where(c == 0, 1 - y, y), c)
+        self.x_side = self.at(z, 1 - x, y, c)
+        self.group = [((y + i) % 2, (c + j) % 2) for i, j in ((0, 1), (1, 0), (1, 1))]
+        self.mates = [self.at(z, x, yy, cc) for yy, cc in self.group]
+
+    def at(self, z, x, y, c):
+        return (z * 2 + x, y * 2 + c)
+
+    def meet(self):
+        barrier = pltpu.get_barrier_semaphore()
+        peers = self.across_z + [self.x_side] + self.mates
+        for peer in peers:
+            pl.semaphore_signal(barrier, inc=1, device_id=peer, device_id_type=MESH)
+        pl.semaphore_wait(barrier, len(peers))
+
+
+class Gather:
+    def __init__(self, wire, spots, full):
+        self.wire, self.s, self.full = wire, spots, full
+        self.last = []
+
+    def over_z(self):
+        s = self.s
+        mine = self.full.at[s.y, s.z, s.x, s.c]
+        self.last = [self.wire.start(mine, mine, peer) for peer in s.across_z]
+
+    def over_first(self):
+        arrived(self.last)
+        s = self.s
+        mine = self.full.at[s.y, :, s.x, s.c]
+        self.last = [self.wire.start(mine, mine, s.first)]
+
+    def over_second(self):
+        arrived(self.last)
+        s = self.s
+        self.last = []
+        for i in range(2):
+            mine = self.full.at[jnp.where(s.c == 0, s.y, i), :, jnp.where(s.c == 0, i, s.x), s.c]
+            self.last.append(self.wire.start(mine, mine, s.second))
+
+    def over_core(self):
+        arrived(self.last)
+        s = self.s
+        self.last = []
+        for i in range(2):
+            mine = self.full.at[i, :, :, s.c]
+            self.last.append(self.wire.start(mine, mine, s.core))
+
+    def done(self):
+        arrived(self.last)
+
+
+def norm_parts(values):
+    center = values - jnp.mean(values, axis=-1, keepdims=True)
+    spread = jnp.mean(center * center, axis=-1, keepdims=True)
+    scale = lax.rsqrt(spread + EPSILON)
+    return center * scale, scale
+
+
+def dot(left, right):
+    return jnp.dot(left, right, preferred_element_type=F32)
+
+
+def make_filter(kern, taps):
+    length = kern.shape[0]
+    position = lax.broadcasted_iota(jnp.int32, kern.shape, 0)
+    live = position.astype(F32) < taps
+    masked = jnp.where(live, kern, 0.0)
+    shrunk = masked - SHRINK_SCALE * jnp.tanh(masked / SHRINK_SCALE)
+    before = jnp.where(position == 0, 0.0, pltpu.roll(shrunk, 1, 0))
+    after = jnp.where(position == length - 1, 0.0, pltpu.roll(shrunk, length - 1, 0))
+    return jnp.where(live, (before + shrunk + after) / 3.0, 0.0)
+
+
+def spectrum_product(re_a, im_a, re_b, im_b):
+    return re_a * re_b - im_a * im_b, re_a * im_b + im_a * re_b
+
+
+GELU_K = math.sqrt(2.0 / math.pi)
+
+
+def gelu_both(v):
+    square = v * v
+    t = jnp.tanh(GELU_K * v * (1.0 + 0.044715 * square))
+    half = 0.5 * (1.0 + t)
+    slope = half + 0.5 * v * (1.0 - t * t) * (GELU_K * (1.0 + 3 * 0.044715 * square))
+    return v * half, slope
+
+
+def forward_kernel(
+    num_z,
+    tok, w_in, w_out, w_up, w_down, kern, small, fwd_hbm, inv_hbm,
+    out_o, win_o, wout_o, wup_o, wdown_o, kern_o, small_o, proj_o, normed_o, sig_o, spec_o, filt_o, conv_o,
+    gated_o, resid_o, normed_two_o, act_o, slope_o,
+    win_v, wout_v, wup_v, wdown_v, kern_v, small_v,
+    pre_in, pre_out, pre_up, pre_down, pre_kern,
+    fwd_v, inv_v, proj_v, normed_v, mixed_v, sig_v, spec_v, filt_v, filt_low, turned_v, conv_ch, conv_v,
+    gated_v, resid_v, normed_two_v, act_v, slope_v, out_v,
+    send, recv, local,
+):
+    s = Spots(num_z)
+    z, x, y, c = s.z, s.x, s.y, s.c
+    wire, inner = Wire(send, recv), Local(local)
+    load_fwd = inner.start(fwd_hbm, fwd_v)
+    load_inv = inner.start(inv_hbm, inv_v)
+    s.meet()
+
+    pairs = [(w_in, pre_in, win_v), (kern, pre_kern, kern_v), (w_out, pre_out, wout_v),
+             (w_up, pre_up, wup_v), (w_down, pre_down, wdown_v)]
+    traded = []
+    for src, pre, _ in pairs:
+        half = src.shape[0] // 2
+        traded.append(wire.start(src.at[pl.ds((1 - c) * half, half)], pre.at[c], s.core))
+    me = y * 2 + c
+    small_v[me] = small[...]
+    smalls = [wire.start(small, small_v.at[me], peer) for peer in s.mates]
+    for src, pre, _ in pairs:
+        half = src.shape[0] // 2
+        pre[c] = src[pl.ds(c * half, half)]
+
+    def join(i):
+        traded[i].wait_recv()
+        _, pre, full = pairs[i]
+        both = jnp.concatenate([pre[0], pre[1]], axis=-1)
+        if full is kern_v:
+            full[z, x, c] = both
+        else:
+            full[y, z, x, c] = both
+
+    g_in, g_out, g_up, g_down = (Gather(wire, s, v) for v in (win_v, wout_v, wup_v, wdown_v))
+    join(0)
+    g_in.over_z()
+    join(1)
+    own = kern_v.at[z, x, c]
+    kern_z = [wire.start(own, own, peer) for peer in s.across_z]
+    join(2)
+    join(3)
+    join(4)
+
+    arrived(smalls)
+    gains = jnp.concatenate([small_v[k] for k in range(4)], axis=-1)
+    rows, width = tok.shape
+    group = width // 2
+    normed, _ = norm_parts(tok[...].astype(F32))
+    normed_v[...] = (normed * gains[0:1]).astype(BF)
+
+    g_in.over_first()
+    g_out.over_z()
+    g_up.over_z()
+    arrived(kern_z)
+    own = kern_v.at[:, x, c]
+    kern_x = [wire.start(own, own, s.x_side)]
+    g_in.over_second()
+    arrived(kern_x)
+    own = kern_v.at[:, :, c]
+    kern_c = [wire.start(own, own, s.core)]
+    g_out.over_first()
+
+    arrived(kern_c)
+    taps = jnp.concatenate([small_v[2 * y], small_v[2 * y + 1]], axis=-1)[2:3]
+    length = turned_v.shape[0] // 2
+    tile = 128
+    for j in range(group // tile):
+        cols = slice(j * tile, (j + 1) * tile)
+        filt = make_filter(kern_v[:, :, :, :, cols].reshape(length, tile).astype(F32), taps[:, cols])
+        filt_low[:, cols] = filt.astype(BF)
+    inner.wait(load_fwd)
+    step = 256
+
+    def spectrum(source, target):
+        def one(i, _):
+            at = pl.ds(pl.multiple_of(i * step, step), step)
+            target[at] = dot(fwd_v[at], source[...]).astype(target.dtype)
+            return 0
+        lax.fori_loop(0, 2 * length // step, one, 0)
+
+    spectrum(filt_low, filt_v)
+    g_in.over_core()
+    g_down.over_z()
+    g_up.over_first()
+    g_out.over_second()
+    g_in.done()
+
+    def project(j):
+        weight = win_v[j // 3, :, :, :, :, (j % 3) * group : (j % 3 + 1) * group].reshape(width, group)
+        return dot(normed_v[...], weight)
+
+    for h in range(2):
+        value, gate = project(h), project(2 + h)
+        proj_v[h] = value.astype(BF)
+        proj_v[2 + h] = gate.astype(BF)
+        mixed_v[h] = (value * gate).astype(BF)
+    span = rows // 2
+    chunk = pl.ds(pl.multiple_of((2 * y + c) * span, span), span)
+    to_channels = [
+        wire.start(mixed_v.at[yy, pl.ds(pl.multiple_of(cc * span, span), span)], sig_v.at[chunk], peer)
+        for (yy, cc), peer in zip(s.group, s.mates)
+    ]
+    sig_v[chunk] = mixed_v[y, pl.ds(pl.multiple_of(c * span, span), span)]
+    for h in range(2):
+        proj_v[4 + h] = project(4 + h).astype(BF)
+    g_out.over_core()
+    g_up.over_second()
+    g_down.over_first()
+    inner.wait(load_inv)
+    arrived(to_channels)
+
+    def convolve(i, _):
+        real = pl.ds(pl.multiple_of(i * step, step), step)
+        imag = pl.ds(pl.multiple_of(length + i * step, step), step)
+        re_s, im_s = dot(fwd_v[real], sig_v[...]), dot(fwd_v[imag], sig_v[...])
+        spec_v[real] = re_s.astype(BF)
+        spec_v[imag] = im_s.astype(BF)
+        re, im = spectrum_product(re_s, im_s, filt_v[real].astype(F32), filt_v[imag].astype(F32))
+        turned_v[real] = re.astype(BF)
+        turned_v[imag] = im.astype(BF)
+        return 0
+    lax.fori_loop(0, length // step, convolve, 0)
+
+    def back(i, _):
+        at = pl.ds(pl.multiple_of(i * step, step), step)
+        conv_ch[at] = (dot(inv_v[at], turned_v[...]) * (1.0 / length)).astype(BF)
+        return 0
+    lax.fori_loop(0, length // step, back, 0)
+
+    home = pl.ds(pl.multiple_of(c * span, span), span)
+    to_tokens = [
+        wire.start(conv_ch.at[pl.ds(pl.multiple_of((2 * yy + cc) * span, span), span)], conv_v.at[y, home], peer)
+        for (yy, cc), peer in zip(s.group, s.mates)
+    ]
+    conv_v[y, home] = conv_ch[chunk]
+    g_up.over_core()
+    g_down.over_second()
+    for src, dst in ((win_v, win_o), (kern_v, kern_o), (small_v, small_o), (proj_v, proj_o),
+                     (normed_v, normed_o), (sig_v, sig_o), (spec_v, spec_o), (filt_v, filt_o)):
+        inner.start(src, dst)
+    g_out.done()
+    arrived(to_tokens)
+
+    for h in range(2):
+        gated_v[:, h * group : (h + 1) * group] = (
+            proj_v[4 + h].astype(F32) * conv_v[h].astype(F32)
+        ).astype(BF)
+    for h in range(2):
+        cols = slice(h * group, (h + 1) * group)
+        resid_v[:, cols] = tok[:, cols].astype(F32) + dot(gated_v[...], wout_v[h].reshape(width, group))
+    normed_two, _ = norm_parts(resid_v[...])
+    normed_two_v[...] = (normed_two * gains[1:2]).astype(BF)
+    for src, dst in ((wout_v, wout_o), (conv_v, conv_o), (gated_v, gated_o), (resid_v, resid_o),
+                     (normed_two_v, normed_two_o)):
+        inner.start(src, dst)
+    g_down.over_core()
+    g_up.done()
+
+    hidden = act_v.shape[1]
+    wide = 256
+    per = hidden // 2 // wide
+
+    def feed(j, _):
+        cols = pl.ds(pl.multiple_of((j % per) * wide, wide), wide)
+        weight = wup_v[j // per, :, :, :, :, cols].reshape(width, wide)
+        act, slope = gelu_both(dot(normed_two_v[...], weight))
+        at = pl.ds(pl.multiple_of(j * wide, wide), wide)
+        act_v[:, at] = act.astype(BF)
+        slope_v[:, at] = slope.astype(BF)
+        return 0
+    lax.fori_loop(0, 2 * per, feed, 0)
+    inner.start(wup_v, wup_o)
+    inner.start(act_v, act_o)
+    inner.start(slope_v, slope_o)
+    g_down.done()
+    inner.start(wdown_v, wdown_o)
+    for h in range(2):
+        cols = slice(h * group, (h + 1) * group)
+        out_v[:, cols] = (resid_v[:, cols] + dot(act_v[...], wdown_v[h].reshape(hidden, group))).astype(BF)
+    inner.start(out_v, out_o)
+    wire.drain()
+    inner.drain()
+
+
+def transform_table(length):
+    k = np.arange(length)[:, None]
+    t = np.arange(length)[None, :]
+    angle = np.pi / (2 * length) * (((2 * k + 1) * t) % (4 * length))
+    return np.concatenate([np.cos(angle), np.sin(angle)]).astype(np.float32).astype(ml_dtypes.bfloat16)
+
+
+def forward(num_z, length, tokens, w_in, w_out, w_up, w_down, kernel, small, fwd_table, inv_table):
+    rows, width = tokens.shape
+    group = width // 2
+    hidden = w_down.shape[0] * num_z * 2
+    sds = jax.ShapeDtypeStruct
+
+    def full(block):
+        return (2, num_z, 2, 2, block.shape[0] // 2, block.shape[1] * 2)
+
+    weights = [full(b) for b in (w_in, w_out, w_up, w_down)]
+    kern_full = (num_z, 2, 2, kernel.shape[0] // 2, kernel.shape[1] * 2)
+    small_full = (4,) + small.shape
+    acts = dict(
+        proj=((6, rows, group), BF), normed=((rows, width), BF), sig=((length, group), BF),
+        spec=((2 * length, group), BF), filt=((2 * length, group), BF), conv=((2, rows, group), BF),
+        gated=((rows, width), BF), resid=((rows, width), F32), normed_two=((rows, width), BF),
+        act=((rows, hidden), BF), slope=((rows, hidden), BF),
+    )
+    outs = [sds((rows, width), BF)] + [sds(w, BF) for w in weights]
+    outs += [sds(kern_full, BF), sds(small_full, F32)] + [sds(*acts[k]) for k in acts]
+    vm = lambda k: pltpu.VMEM(*acts[k])
+    scratch = [pltpu.VMEM(w, BF) for w in weights] + [pltpu.VMEM(kern_full, BF), pltpu.VMEM(small_full, F32)]
+    scratch += [pltpu.VMEM((2, b.shape[0] // 2, b.shape[1]), BF) for b in (w_in, w_out, w_up, w_down, kernel)]
+    scratch += [pltpu.VMEM(fwd_table.shape, BF), pltpu.VMEM(inv_table.shape, BF), vm("proj"), vm("normed"),
+                pltpu.VMEM((2, rows, group), BF), vm("sig"), vm("spec"), vm("filt"),
+                pltpu.VMEM((length, group), BF), pltpu.VMEM((2 * length, group), BF), pltpu.VMEM((length, group), BF),
+                vm("conv"), vm("gated"), vm("resid"), vm("normed_two"), vm("act"), vm("slope"),
+                pltpu.VMEM((rows, width), BF)]
+    copies = 80
+    scratch += [pltpu.SemaphoreType.DMA((copies,)), pltpu.SemaphoreType.DMA((copies,)), pltpu.SemaphoreType.DMA((40,))]
+    vmem, hbm = pl.BlockSpec(memory_space=pltpu.VMEM), pl.BlockSpec(memory_space=pl.ANY)
+    return pl.pallas_call(
+        partial(forward_kernel, num_z),
+        out_shape=outs,
+        in_specs=[vmem] * 7 + [hbm] * 2,
+        out_specs=[hbm] * len(outs),
+        scratch_shapes=scratch,
+        compiler_params=pltpu.CompilerParams(collective_id=0, has_side_effects=True, vmem_limit_bytes=60 * 2**20),
+        cost_estimate=pl.CostEstimate(flops=12 * 10**9, bytes_accessed=50 * 10**6, transcendentals=2 * 10**6),
+    )(tokens, w_in, w_out, w_up, w_down, kernel, small, fwd_table, inv_table)
+
+
+def fits(num_dp, num_seq, tokens, w_in, w_out, w_up, w_down, kernel):
+    if num_seq != 4 or num_dp % 2 or kernel.shape[0] * num_dp > 1024:
+        return False
+    blocks = (w_in, w_out, w_up, w_down, kernel)
+    return all(b.shape[0] % 32 == 0 and b.shape[1] * 2 % 128 == 0 for b in blocks) and tokens.shape[0] == 2
+
+
+def unfold(full):
+    flat = full.reshape(2, -1, full.shape[-1])
+    return jnp.concatenate([flat[0], flat[1]], axis=1)
+
+
+def body(num_dp, num_seq, tokens_in, w_in, w_out, w_up, w_down, norm_gains, kernel, taps, cotangent):
+    if not fits(num_dp, num_seq, tokens_in, w_in, w_out, w_up, w_down, kernel):
+        return general_body(tokens_in, w_in, w_out, w_up, w_down, norm_gains, kernel, taps, cotangent)
+    num_seqs, local_len, width = tokens_in.shape
+    total_rows = num_seqs * local_len
+    length = kernel.shape[0] * num_dp
+    table = transform_table(length)
+    small = jnp.concatenate(
+        [norm_gains.astype(F32), taps.astype(F32)[None], jnp.zeros((5, taps.shape[0]), F32)]
+    )
+    tokens = tokens_in.reshape(total_rows, width)
+    (out, win_f, wout_f, wup_f, wdown_f, kern_f, small_f, proj, normed, sig, spec, filt_s, conv, gated, resid,
+     normed_two, act, slope) = forward(
+        num_dp // 2, length, tokens, w_in, w_out, w_up, w_down, kernel, small,
+        jnp.asarray(table), jnp.asarray(np.ascontiguousarray(table.T)))
+    full_in, full_out, full_up, full_down = unfold(win_f), unfold(wout_f), unfold(wup_f), unfold(wdown_f)
+    gains_wide = jnp.concatenate([small_f[k] for k in range(4)], axis=-1)[:2]
+    chan = lax.axis_index("seq") // 2
+    core = lax.axis_index("seq") % 2
+    group = width // 2
+    proj = proj.astype(F32)
+    values, gate_one, gate_two = [jnp.concatenate([proj[2 * k], proj[2 * k + 1]], axis=1) for k in range(3)]
+    conv_tok = jnp.concatenate([conv[0], conv[1]], axis=1).astype(F32)
+    inputs = tokens.astype(F32)
+    _, norm_back_one = jax.vjp(norm_rows, inputs, gains_wide[0])
+    _, norm_back_two = jax.vjp(norm_rows, resid, gains_wide[1])
+    grad_rows = cotangent.reshape(total_rows, width)
+    grad_down = contract_rows(act, grad_rows)
+    grad_active = times_transposed(grad_rows, full_down)
+    grad_pre = (slope.astype(F32) * grad_active).astype(BF)
+    grad_up = contract_rows(normed_two, grad_pre)
+    grad_normed_two = times_transposed(grad_pre, full_up)
+    grad_resid_part, grad_gain_two = norm_back_two(grad_normed_two)
+    grad_resid = grad_rows.astype(jnp.float32) + grad_resid_part
+    resid_low = grad_resid.astype(jnp.bfloat16)
+    grad_outw = contract_rows(gated, resid_low)
+    grad_gated = times_transposed(resid_low, full_out)
+    grad_gate_two = grad_gated * conv_tok
+    grad_conv = (grad_gated * gate_two).astype(jnp.bfloat16).reshape(2, local_len, 2, group)
+    sent = grad_conv.transpose(2, 0, 1, 3).reshape(4, local_len, group)
+    grad_ch = lax.all_to_all(sent, "seq", split_axis=0, concat_axis=0, tiled=True).reshape(length, group)
+    tab = jnp.asarray(table)
+    back = dot(tab, grad_ch)
+    be, bf = back[:length], back[length:]
+    hc, hd = filt_s[:length].astype(F32), filt_s[length:].astype(F32)
+    sa, sb = spec[:length].astype(F32), spec[length:].astype(F32)
+    inv = lambda re, im: contract_rows(tab, jnp.concatenate([re, im]).astype(BF)) / length
+    grad_signal = inv(hc * be + hd * bf, hc * bf - hd * be).astype(BF)
+    grad_filt = inv(sa * be + sb * bf, sa * bf - sb * be)
+    home = lax.all_to_all(grad_signal.reshape(4, local_len, group), "seq", split_axis=0, concat_axis=0, tiled=True)
+    grad_mixed = home.reshape(2, 2, local_len, group).transpose(1, 2, 0, 3).reshape(total_rows, width).astype(F32)
+    kern_cols = kern_f.reshape(length, group).astype(F32)
+    taps_f = jnp.concatenate([small_f[2 * chan], small_f[2 * chan + 1]], axis=-1)[2]
+    _, filter_back = jax.vjp(partial(shape_filter, taps=taps_f.astype(jnp.int32)), kern_cols)
+    grad_kern = filter_back(grad_filt)[0]
+    swap = [(2 * i + j, 2 * i + 1 - j) for i in range(2) for j in range(2)]
+    part = group // 2
+    mine = lax.dynamic_slice_in_dim(grad_kern, core * part, part, 1)
+    other = lax.dynamic_slice_in_dim(grad_kern, (1 - core) * part, part, 1)
+    mine = mine + lax.ppermute(other.astype(BF), "seq", swap).astype(F32)
+    grad_proj = jnp.concatenate([grad_mixed * gate_one, grad_mixed * values, grad_gate_two], axis=1)
+    grad_proj = grad_proj.astype(jnp.bfloat16)
+    grad_inw = contract_rows(normed, grad_proj)
+    grad_normed = times_transposed(grad_proj, full_in)
+    grad_input_part, grad_gain_one = norm_back_one(grad_normed)
+    grad_inputs = (
+        (grad_resid + grad_input_part).astype(jnp.bfloat16).reshape(num_seqs, local_len, width)
+    )
+    grad_gain_pair = jnp.stack([grad_gain_one, grad_gain_two])
+
+    def scatter_dp(v):
+        return lax.psum_scatter(v.astype(BF), "dp", scatter_dimension=0, tiled=True).astype(F32)
+
+    def scatter_seq(v):
+        return lax.psum_scatter(v.astype(BF), "seq", scatter_dimension=1, tiled=True).astype(F32)
+
+    weights = [scatter_seq(scatter_dp(v)) for v in (grad_inw, grad_outw, grad_up, grad_down)]
+    kern_done = scatter_dp(mine)
+    gain_done = lax.psum(scatter_seq(grad_gain_pair), "dp")
+    return (out.reshape(num_seqs, local_len, width), grad_inputs, *weights, gain_done, kern_done)
+
+
 def solution(mesh):
     return jax.shard_map(
-        body,
+        partial(body, mesh.shape["dp"], mesh.shape["seq"]),
         mesh=mesh,
         in_specs=(
             P("dp", "seq", None),

time: 884 us -> 715 us (0.81)
  matrix products: 161 us -> 43.4 us
  Pallas kernels: 0 us -> 113 us
  blocking collectives: 124 us -> 37.1 us
  waiting for transfers between devices: 477 us -> 417 us
  local copies, waits for them, and re-layouts: 72.7 us -> 59.5 us
    dot_general x40 -> x1, matrix products: 123 us -> 4.9 us  [dot(): return jnp.dot(left, right, preferred_element_type=F32)]
    pallas_call x0 -> x1, Pallas kernels: none -> 113 us  [forward(): pl.pallas_call(partial(forward_kernel, num_z), out_shape=outs, in_specs=[...]
    all_gather x4 -> x0, waiting for transfers between devices: 88.8 us -> none  [the longest x1 72.3 us: body(): lax.all_gather(w_up_rows, 'dp', axis=0, tiled=True)]
    all_gather x6 -> x0, blocking collectives: 65.9 us -> none  [the longest x1 29.7 us: body(): lax.all_gather(kernel, 'dp', axis=0, tiled=True)]
    reduce_scatter x5, waiting for transfers between devices: 254 us -> 279 us  [the longest x4 257 us: scatter_dp(): lax.psum_scatter(v.astype(BF), 'dp', scatter_dimension=0, tiled=True)]
    all_to_all x2 -> x1, blocking collectives: 36.2 us -> 15.1 us  [body(): lax.all_to_all(grad_signal.reshape(4, local_len, group), 'seq', split_axi...]
    convert_element_type x9 -> x3, local copies, waits for them, and re-layouts: 22 us -> 4.37 us  [the longest x1 3.09 us: body(): kern_cols = kern_f.reshape(length, group).astype(F32)]
    slice x1 -> x4, local copies, waits for them, and re-layouts: 0.02 us -> 13.1 us  [unfold(): return jnp.concatenate([flat[0], flat[1]], axis=1)]
  transfers between devices with their start and end apart: 16 -> 12, of which waited for: 14 -> 10; matrix products, arithmetic and copies ran while one was open for 24% -> 10% of each run, Pallas kernels for 0% -> 0%
where the time goes in v1:
time: 715 us; the launch traced here: 707 us
  waiting for transfers between devices  417 us (58%)
  Pallas kernels  113 us (16%)
  local copies, waits for them, and re-layouts  59.5 us (8%)
  matrix products  43.4 us (6%)
  blocking collectives  37.1 us (5%)
  other arithmetic  17.7 us (2%)
  between operations  15.2 us (2%)
    reduce_scatter x4, waiting for transfers between devices, scatter_dp(): lax.psum_scatter(v.astype(BF), 'dp', scatter_dimension=0, tiled=True)  257 us
    unnamed x15, waiting for transfers between devices  129 us
    pallas_call x1, Pallas kernels, forward(): pl.pallas_call(partial(forward_kernel, num_z), out_shape=outs, in_specs=[...  113 us
    unnamed x99, local copies, waits for them, and re-layouts  32.5 us
    dot_general x8, matrix products, contract_rows(): lax.dot_general(left, right, (((0,), (0,)), ((), ())), preferred_element_...  25.4 us
    reduce_scatter x1, waiting for transfers between devices, scatter_seq(): lax.psum_scatter(v.astype(BF), 'seq', scatter_dimension=1, tiled=True)  22.7 us
    psum x1, blocking collectives, body(): gain_done = lax.psum(scatter_seq(grad_gain_pair), 'dp')  22 us
    all_to_all x1, blocking collectives, body(): lax.all_to_all(grad_signal.reshape(4, local_len, group), 'seq', split_axi...  15.1 us
  transfers between devices with their start and end apart: 12, of which 10 were waited for; matrix products, arithmetic and copies ran while one was open for 10% of the time, Pallas kernels for 0%

profile of v1, /device:TPU:0, one launch (start us, length us, event | category | flops | bytes accessed | tf_op | source)
XLA Modules:
  0.0 707.2 jit_solution(1336854665936086240)
XLA Ops:
  7.2 1.7 copy.32.w_down
  8.9 1.5 copy.33.kern
  12.6 112.9 %shard_map.170 = (bf16[512,768]{1,0:T(8,128)(2,1)}, bf16[2,4,2,2,48,1152]{5,4,3,2,1,0:T(8,128)(2,1)}, bf16[2,4,2,2,48,384]{5,4,3,2,1,0:T(8,128)(2,1)}, bf16[2,4,...) custom-call(bf16[512,768]{1,0:T(8,128)(2,1)} %bitcast.106, ...), custom_call_target="tpu_custom_call" | custom-call | flops 12000000000 | bytes 50000000 | tf_op jit(solution)/shard_map/pallas_call | solution.py:612
  125.4 5.3 fusion.60
  131.3 5.2 fusion.59
  136.6 6.1 fusion
  142.7 2.9 multiply_reduce_fusion
  147.6 1.4 slice_bitcast_fusion.3
  150.7 2.0 fusion.22
  152.7 2.9 reshape.149
  155.6 2.1 copy.35
  157.8 4.2 all-to-all-start
  162.0 3.2 convolution_convert_fusion.3
  165.3 8.4 %all-to-all-done = bf16[4,256,384]{2,1,0:T(8,128)(2,1)} async-done(((bf16[4,256,384]{2,1,0:T(8,128)(2,1)}), bf16[4,256,384]{2,1,0:T(8,128)(2,1)}, u32[]{:S(2)}, u32[]{:S(2)}) %all-to-all-start) | async-done | bytes 786464 | tf_op jit(solution)/shard_map/all_to_all | solution.py:675
  173.7 4.9 fusion.63
  181.3 2.0 fusion.27
  183.3 2.3 copy.41
  185.7 15.1 %all_to_all.10 = bf16[4,256,384]{2,1,0:T(8,128)(2,1)S(1)} all-to-all(bf16[4,256,384]{2,1,0:T(8,128)(2,1)} %bitcast.110), channel_id=1, replica_groups=mesh['dp'=8,'seq'=4] {'seq'}, dimensions={0} | all-to-all | bytes 1572864 | tf_op jit(solution)/shard_map/all_to_all | solution.py:684
  200.9 1.2 copy.37
  205.0 3.9 convolution_convert_fusion.2
  210.0 6.8 convolution_convert_fusion
  217.9 6.1 convolution_convert_fusion.1
  225.2 1.4 bitcast_convert_fusion
  226.5 3.1 copy.38
  231.5 2.4 fusion.61
  235.5 1.1 fusion.35
  237.1 1.2 fusion.25
  238.5 1.3 add_select_fusion
  241.0 2.1 multiply_reduce_fusion.2
  243.2 1.1 copy-done.5
  244.3 1.4 multiply_reduce_fusion.1
  246.3 1.5 copy.48
  247.9 1.3 add_convert_fusion.1
  250.4 1.7 copy.44
  252.2 63.6 %reduce-scatter.21.cloned.1.call-done = bf16[96,2304]{1,0:T(8,128)(2,1)} async-done(((bf16[768,2304]{1,0:T(8,128)(2,1)}), bf16[96,2304]{1,0:T(8,128)(2,1)}) %reduce-scatter.21.cloned.1.call-update) | async-done | bytes 442384 | tf_op jit(solution)/shard_map/reduce_scatter | solution.py:706
  315.8 2.1 copy.42
  317.9 96.5 %reduce-scatter.29.cloned.1.call-done = bf16[384,768]{1,0:T(8,128)(2,1)} async-done(((bf16[3072,768]{1,0:T(8,128)(2,1)}), bf16[384,768]{1,0:T(8,128)(2,1)}) %reduce-scatter.29.cloned.1.call-update) | async-done | bytes 589840 | tf_op jit(solution)/shard_map/reduce_scatter | solution.py:706
  414.4 2.2 copy.46
  416.6 96.5 %reduce-scatter.25.cloned.1.call-done = bf16[96,3072]{1,0:T(8,128)(2,1)} async-done(((bf16[768,3072]{1,0:T(8,128)(2,1)}), bf16[96,3072]{1,0:T(8,128)(2,1)}) %reduce-scatter.25.cloned.1.call-update) | async-done | bytes 589840 | tf_op jit(solution)/shard_map/reduce_scatter | solution.py:706
  513.1 3.1 add_convert_fusion
  516.2 19.2 %reduce-scatter.37.cloned.1.call-done = bf16[192,2]{1,0:T(8,128)(2,1)} async-done(((bf16[768,2]{1,0:T(8,128)(2,1)}), bf16[192,2]{1,0:T(8,128)(2,1)}) %reduce-scatter.37.cloned.1.call-update) | async-done | bytes 784
  536.4 22.0 %psum.7 = f32[2,192]{1,0:T(2,128)} all-reduce(bf16[2,192]{1,0:T(2,128)(2,1)S(1)} %copy.49), channel_id=1, replica_groups=mesh['dp'=8,'seq'=4] {'dp'}, use_global_device_ids=true, to_apply=%region_19.20 | all-reduce | flops 384 | bytes 2304 | tf_op jit(solution)/shard_map/psum | solution.py:713
  558.4 42.4 %reduce-scatter.39.cloned.1.call-done = bf16[128,192]{1,0:T(8,128)(2,1)} async-done(((bf16[1024,192]{1,0:T(8,128)(2,1)}), bf16[128,192]{1,0:T(8,128)(2,1)}) %reduce-scatter.39.cloned.1.call-update) | async-done | bytes 49168
  602.4 20.3 %reduce-scatter.33.cloned.1.call-done = bf16[192,96]{1,0:T(8,128)(2,1)} async-done(((bf16[768,96]{1,0:T(8,128)(2,1)}), bf16[192,96]{1,0:T(8,128)(2,1)}) %reduce-scatter.33.cloned.1.call-update) | async-done | bytes 36880
  624.2 23.8 %reduce-scatter.31.cloned.1.call-done = bf16[576,96]{1,0:T(8,128)(2,1)} async-done(((bf16[2304,96]{1,0:T(8,128)(2,1)}), bf16[576,96]{1,0:T(8,128)(2,1)}) %reduce-scatter.31.cloned.1.call-update) | async-done | bytes 110608
  649.8 23.0 %reduce-scatter.35.cloned.1.call-done = bf16[192,384]{1,0:T(8,128)(2,1)} async-done(((bf16[768,384]{1,0:T(8,128)(2,1)}), bf16[192,384]{1,0:T(8,128)(2,1)}) %reduce-scatter.35.cloned.1.call-update) | async-done | bytes 147472
  674.7 22.7 %reduce-scatter.27.cloned.1.call-done = bf16[96,768]{1,0:T(8,128)(2,1)} async-done(((bf16[96,3072]{1,0:T(8,128)(2,1)}), bf16[96,768]{1,0:T(8,128)(2,1)}) %reduce-scatter.27.cloned.1.call-update) | async-done | bytes 147472 | tf_op jit(solution)/shard_map/reduce_scatter | solution.py:709
  697.4 1.6 convert_element_type.154
  (150 shorter events, 31.2 us)
Async XLA Ops:
  125.4 5.4 copy-start
  131.3 5.2 copy-start.28
  131.3 5.3 copy-start.11
  136.6 6.1 copy-start.15
  136.6 6.1 copy-start.16
  142.7 2.9 copy-start.39
  145.6 1.7 copy-start.14
  147.6 1.5 copy-start.17
  149.1 1.4 copy-start.12
  150.7 2.0 copy-start.25
  157.8 15.9 %all-to-all-start = ((bf16[4,256,384]{2,1,0:T(8,128)(2,1)}), bf16[4,256,384]{2,1,0:T(8,128)(2,1)}, u32[]{:S(2)}, u32[]{:S(2)}) async-start(bf16[4,256,384]{2,1,0:T(8,128)(2,1)} %bitcast.109), calls=%async_computation | async-start | bytes 1572864 | tf_op jit(solution)/shard_map/all_to_all | solution.py:675
  162.0 88.4 %reduce-scatter.23.cloned.1.call-start = ((), (), s32[]{:S(2)}) async-start(), calls=%async_computation.13 | async-start | bytes 1327104 | tf_op jit(solution)/shard_map/reduce_scatter | solution.py:706
  165.2 150.6 %reduce-scatter.21.cloned.1.call-start = ((), (), s32[]{:S(2)}) async-start(), calls=%async_computation.12 | async-start | bytes 3981312 | tf_op jit(solution)/shard_map/reduce_scatter | solution.py:706
  173.7 4.9 copy-start.2
  173.7 4.9 copy-start.27
  178.6 1.8 copy-start.9
  178.6 2.7 copy-start.34
  202.1 1.1 copy-start.7
  202.1 1.4 copy-start.8
  203.5 1.5 copy-start.36
  203.5 1.5 copy-start.38
  208.9 1.1 copy-start.13
  208.9 205.5 %reduce-scatter.29.cloned.1.call-start = ((), (), s32[]{:S(2)}) async-start(), calls=%async_computation.16 | async-start | bytes 5308416 | tf_op jit(solution)/shard_map/reduce_scatter | solution.py:706
  216.8 296.3 %reduce-scatter.25.cloned.1.call-start = ((), (), s32[]{:S(2)}) async-start(), calls=%async_computation.14 | async-start | bytes 5308416 | tf_op jit(solution)/shard_map/reduce_scatter | solution.py:706
  224.1 311.4 %reduce-scatter.37.cloned.1.call-start = ((), (), s32[]{:S(2)}) async-start(), calls=%async_computation.20 | async-start | bytes 245760
  226.5 3.1 copy-start.1
  231.5 2.7 copy-start.3
  231.5 3.6 copy-start.10
  231.5 4.1 copy-start.26
  235.5 1.6 copy-start.35
  237.1 1.4 copy-start.4
  238.5 2.4 copy-start.19
  238.5 2.4 copy-start.21
  238.5 2.4 copy-start.37
  239.8 1.2 copy-start.6
  239.9 8.0 %collective-permute-start = (bf16[1024,192]{0,1:T(8,128)(2,1)S(1)}, bf16[1024,192]{0,1:T(8,128)(2,1)}, u32[]{:S(2)}, u32[]{:S(2)}) collective-permute-start(bf16[1024,192]{0,1:T(8,128)(2,1)S(1)} %dynamic-slice_convert_fusion), channel_id=1, source_target_pairs={{0,1},{1,0},{2,3},{3,2},{4,5},{5,4},{6,7},{7,6},{8,9},{9,8},{10,11... | collective-permute-start | bytes 1179656 | tf_op jit(solution)/shard_map/ppermute | solution.py:694
  241.0 2.2 copy-start.32
  243.2 1.1 copy-start.5
  243.2 2.6 copy-start.31
  243.2 2.5 copy-start.29
  247.9 352.9 %reduce-scatter.39.cloned.1.call-start = ((), (), s32[]{:S(2)}) async-start(), calls=%async_computation.21 | async-start | bytes 589824
  250.3 372.4 %reduce-scatter.33.cloned.1.call-start = ((), (), s32[]{:S(2)}) async-start(), calls=%async_computation.18 | async-start | bytes 245760
  252.1 395.9 %reduce-scatter.31.cloned.1.call-start = ((), (), s32[]{:S(2)}) async-start(), calls=%async_computation.17 | async-start | bytes 737280
  317.9 195.3 %copy-start.33 = (f32[512]{0:T(512)S(1)}, f32[512]{0:T(512)}, u32[]{:S(2)}) copy-start(f32[512]{0:T(512)} %get-tuple-element.69) | copy-start | bytes 6148
  317.9 195.3 %copy-start.30 = (f32[512]{0:T(512)S(1)}, f32[512]{0:T(512)}, u32[]{:S(2)}) copy-start(f32[512]{0:T(512)} %copy-done.29) | copy-start | bytes 6148
  317.9 354.9 %reduce-scatter.35.cloned.1.call-start = ((), (), s32[]{:S(2)}) async-start(), calls=%async_computation.19 | async-start | bytes 737280
  416.6 280.8 %reduce-scatter.27.cloned.1.call-start = ((), (), s32[]{:S(2)}) async-start(), calls=%async_computation.15 | async-start | bytes 737280 | tf_op jit(solution)/shard_map/reduce_scatter | solution.py:709
  516.2 182.8 %copy-start.22 = (bf16[512,768]{1,0:T(8,128)(2,1)S(1)}, bf16[512,768]{1,0:T(8,128)(2,1)}, u32[]{:S(2)}) copy-start(bf16[512,768]{1,0:T(8,128)(2,1)} %get-tuple-element.25) | copy-start | bytes 2359300
  (5 other events, 5.4 us)
Sparse Core Ops, SparseCore 0:
  166.2 67.9 reduce-scatter.22
  237.8 77.9 reduce-scatter.20
  319.4 94.9 reduce-scatter.28
  417.9 95.1 reduce-scatter.24
  516.0 19.4 reduce-scatter.36
  538.7 62.0 reduce-scatter.38
  603.9 18.7 reduce-scatter.32
  625.9 22.0 reduce-scatter.30
  650.7 22.0 reduce-scatter.34
  675.3 22.0 reduce-scatter.26

commit v2 on v1

--- a/solution.py
+++ b/solution.py
@@ -271,7 +271,7 @@
 
     def wait(self, copy):
         copy.wait()
-        self.open.remove(copy)
+        self.open = [other for other in self.open if other is not copy]
 
     def drain(self):
         for copy in list(self.open):
@@ -354,6 +354,14 @@
     return jnp.dot(left, right, preferred_element_type=F32)
 
 
+def dot_rows(left, right):
+    return lax.dot_general(left, right, (((0,), (0,)), ((), ())), preferred_element_type=F32)
+
+
+def dot_cols(left, right):
+    return lax.dot_general(left, right, (((1,), (1,)), ((), ())), preferred_element_type=F32)
+
+
 def make_filter(kern, taps):
     length = kern.shape[0]
     position = lax.broadcasted_iota(jnp.int32, kern.shape, 0)
@@ -382,20 +390,19 @@
 
 def forward_kernel(
     num_z,
-    tok, w_in, w_out, w_up, w_down, kern, small, fwd_hbm, inv_hbm,
-    out_o, win_o, wout_o, wup_o, wdown_o, kern_o, small_o, proj_o, normed_o, sig_o, spec_o, filt_o, conv_o,
-    gated_o, resid_o, normed_two_o, act_o, slope_o,
+    tok, cot, w_in, w_out, w_up, w_down, kern, small, twist, table_hbm,
+    out_o, win_o, wout_o, wup_o, gdown_o, kern_o, small_o, proj_o, normed_o, sig_o, spec_o, filt_o, conv_o,
+    gated_o, resid_o, normed_two_o, gpre_o,
     win_v, wout_v, wup_v, wdown_v, kern_v, small_v,
     pre_in, pre_out, pre_up, pre_down, pre_kern,
-    fwd_v, inv_v, proj_v, normed_v, mixed_v, sig_v, spec_v, filt_v, filt_low, turned_v, conv_ch, conv_v,
-    gated_v, resid_v, normed_two_v, act_v, slope_v, out_v,
+    table_v, proj_v, normed_v, mixed_v, sig_v, spec_v, filt_v, filt_low, turned_v, conv_ch, conv_v,
+    gated_v, resid_v, normed_two_v, act_v, slope_v, gdown_v, out_v,
     send, recv, local,
 ):
     s = Spots(num_z)
     z, x, y, c = s.z, s.x, s.y, s.c
     wire, inner = Wire(send, recv), Local(local)
-    load_fwd = inner.start(fwd_hbm, fwd_v)
-    load_inv = inner.start(inv_hbm, inv_v)
+    load_table = inner.start(table_hbm, table_v)
     s.meet()
 
     pairs = [(w_in, pre_in, win_v), (kern, pre_kern, kern_v), (w_out, pre_out, wout_v),
@@ -457,17 +464,18 @@
         cols = slice(j * tile, (j + 1) * tile)
         filt = make_filter(kern_v[:, :, :, :, cols].reshape(length, tile).astype(F32), taps[:, cols])
         filt_low[:, cols] = filt.astype(BF)
-    inner.wait(load_fwd)
+    inner.wait(load_table)
     step = 256
 
-    def spectrum(source, target):
-        def one(i, _):
-            at = pl.ds(pl.multiple_of(i * step, step), step)
-            target[at] = dot(fwd_v[at], source[...]).astype(target.dtype)
-            return 0
-        lax.fori_loop(0, 2 * length // step, one, 0)
-
-    spectrum(filt_low, filt_v)
+    def spectrum(i, _):
+        real = pl.ds(pl.multiple_of(i * step, step), step)
+        imag = pl.ds(pl.multiple_of(length + i * step, step), step)
+        re, im = dot(table_v[real], filt_low[...]), dot(table_v[imag], filt_low[...])
+        cosine, sine = twist[real, 0:1], twist[real, 1:2]
+        filt_v[real] = (re * cosine + im * sine).astype(BF)
+        filt_v[imag] = (im * cosine - re * sine).astype(BF)
+        return 0
+    lax.fori_loop(0, length // step, spectrum, 0)
     g_in.over_core()
     g_down.over_z()
     g_up.over_first()
@@ -495,13 +503,12 @@
     g_out.over_core()
     g_up.over_second()
     g_down.over_first()
-    inner.wait(load_inv)
     arrived(to_channels)
 
     def convolve(i, _):
         real = pl.ds(pl.multiple_of(i * step, step), step)
         imag = pl.ds(pl.multiple_of(length + i * step, step), step)
-        re_s, im_s = dot(fwd_v[real], sig_v[...]), dot(fwd_v[imag], sig_v[...])
+        re_s, im_s = dot(table_v[real], sig_v[...]), dot(table_v[imag], sig_v[...])
         spec_v[real] = re_s.astype(BF)
         spec_v[imag] = im_s.astype(BF)
         re, im = spectrum_product(re_s, im_s, filt_v[real].astype(F32), filt_v[imag].astype(F32))
@@ -512,7 +519,9 @@
 
     def back(i, _):
         at = pl.ds(pl.multiple_of(i * step, step), step)
-        conv_ch[at] = (dot(inv_v[at], turned_v[...]) * (1.0 / length)).astype(BF)
+        imag = pl.ds(pl.multiple_of(length + i * step, step), step)
+        both = dot(table_v[at], turned_v[0:length]) + dot(table_v[imag], turned_v[length:])
+        conv_ch[at] = (both * (1.0 / length)).astype(BF)
         return 0
     lax.fori_loop(0, length // step, back, 0)
 
@@ -559,26 +568,48 @@
         return 0
     lax.fori_loop(0, 2 * per, feed, 0)
     inner.start(wup_v, wup_o)
-    inner.start(act_v, act_o)
-    inner.start(slope_v, slope_o)
+
+    deep = hidden // (2 * num_z)
+
+    def down_grad(i, _):
+        grad = dot_rows(act_v[:, pl.ds(pl.multiple_of(i * deep, deep), deep)], cot[...]).astype(BF)
+        for h in range(2):
+            gdown_v[h, i // 2, i % 2] = grad[:, h * group : (h + 1) * group].reshape(2, deep // 2, group)
+        return 0
+    lax.fori_loop(0, 2 * num_z, down_grad, 0)
+    inner.start(gdown_v, gdown_o)
     g_down.done()
-    inner.start(wdown_v, wdown_o)
     for h in range(2):
         cols = slice(h * group, (h + 1) * group)
         out_v[:, cols] = (resid_v[:, cols] + dot(act_v[...], wdown_v[h].reshape(hidden, group))).astype(BF)
     inner.start(out_v, out_o)
+
+    def pre_grad(i, _):
+        at = pl.ds(pl.multiple_of(i * deep, deep), deep)
+        grad = sum(
+            dot_cols(cot[:, h * group : (h + 1) * group], wdown_v[h, i // 2, i % 2].reshape(deep, group))
+            for h in range(2)
+        )
+        slope_v[:, at] = (slope_v[:, at].astype(F32) * grad).astype(BF)
+        return 0
+    lax.fori_loop(0, 2 * num_z, pre_grad, 0)
+    inner.start(slope_v, gpre_o)
     wire.drain()
     inner.drain()
 
 
 def transform_table(length):
-    k = np.arange(length)[:, None]
-    t = np.arange(length)[None, :]
-    angle = np.pi / (2 * length) * (((2 * k + 1) * t) % (4 * length))
+    k = 2 * np.arange(length)[:, None] + 1
+    angle = np.pi / (4 * length) * ((k * k.T) % (8 * length))
     return np.concatenate([np.cos(angle), np.sin(angle)]).astype(np.float32).astype(ml_dtypes.bfloat16)
 
 
-def forward(num_z, length, tokens, w_in, w_out, w_up, w_down, kernel, small, fwd_table, inv_table):
+def twist_table(length):
+    angle = np.pi / (4 * length) * (2 * np.arange(length) + 1)
+    return np.stack([np.cos(angle), np.sin(angle)], axis=1).astype(np.float32)
+
+
+def forward(num_z, length, tokens, cot, w_in, w_out, w_up, w_down, kernel, small, twist, table):
     rows, width = tokens.shape
     group = width // 2
     hidden = w_down.shape[0] * num_z * 2
@@ -594,30 +625,420 @@
         proj=((6, rows, group), BF), normed=((rows, width), BF), sig=((length, group), BF),
         spec=((2 * length, group), BF), filt=((2 * length, group), BF), conv=((2, rows, group), BF),
         gated=((rows, width), BF), resid=((rows, width), F32), normed_two=((rows, width), BF),
-        act=((rows, hidden), BF), slope=((rows, hidden), BF),
+        grad_pre=((rows, hidden), BF),
     )
     outs = [sds((rows, width), BF)] + [sds(w, BF) for w in weights]
     outs += [sds(kern_full, BF), sds(small_full, F32)] + [sds(*acts[k]) for k in acts]
     vm = lambda k: pltpu.VMEM(*acts[k])
     scratch = [pltpu.VMEM(w, BF) for w in weights] + [pltpu.VMEM(kern_full, BF), pltpu.VMEM(small_full, F32)]
     scratch += [pltpu.VMEM((2, b.shape[0] // 2, b.shape[1]), BF) for b in (w_in, w_out, w_up, w_down, kernel)]
-    scratch += [pltpu.VMEM(fwd_table.shape, BF), pltpu.VMEM(inv_table.shape, BF), vm("proj"), vm("normed"),
+    scratch += [pltpu.VMEM(table.shape, BF), vm("proj"), vm("normed"),
                 pltpu.VMEM((2, rows, group), BF), vm("sig"), vm("spec"), vm("filt"),
                 pltpu.VMEM((length, group), BF), pltpu.VMEM((2 * length, group), BF), pltpu.VMEM((length, group), BF),
-                vm("conv"), vm("gated"), vm("resid"), vm("normed_two"), vm("act"), vm("slope"),
-                pltpu.VMEM((rows, width), BF)]
+                vm("conv"), vm("gated"), vm("resid"), vm("normed_two"), vm("grad_pre"), vm("grad_pre"),
+                pltpu.VMEM(weights[3], BF), pltpu.VMEM((rows, width), BF)]
     copies = 80
     scratch += [pltpu.SemaphoreType.DMA((copies,)), pltpu.SemaphoreType.DMA((copies,)), pltpu.SemaphoreType.DMA((40,))]
     vmem, hbm = pl.BlockSpec(memory_space=pltpu.VMEM), pl.BlockSpec(memory_space=pl.ANY)
     return pl.pallas_call(
         partial(forward_kernel, num_z),
         out_shape=outs,
-        in_specs=[vmem] * 7 + [hbm] * 2,
+        in_specs=[vmem] * 9 + [hbm],
         out_specs=[hbm] * len(outs),
         scratch_shapes=scratch,
         compiler_params=pltpu.CompilerParams(collective_id=0, has_side_effects=True, vmem_limit_bytes=60 * 2**20),
-        cost_estimate=pl.CostEstimate(flops=12 * 10**9, bytes_accessed=50 * 10**6, transcendentals=2 * 10**6),
-    )(tokens, w_in, w_out, w_up, w_down, kernel, small, fwd_table, inv_table)
+        cost_estimate=pl.CostEstimate(flops=17 * 10**9, bytes_accessed=50 * 10**6, transcendentals=2 * 10**6),
+    )(tokens, cot, w_in, w_out, w_up, w_down, kernel, small, twist, table)
+
+
+class Scatter:
+    def __init__(self, wire, spots, total, from_core, from_second, from_first, from_z, ends, away=None):
+        self.wire, self.s, self.total = wire, spots, total
+        self.from_core, self.from_second, self.from_first = from_core, from_second, from_first
+        self.from_z, self.ends, self.away = from_z, ends, away
+        self.last = []
+
+    def mine(self, yy, zz, xx):
+        if self.away is None:
+            return self.total.at[yy, zz, xx, self.s.c]
+        return self.total.at[yy, zz, xx]
+
+    def send_core(self):
+        s = self.s
+        source = self.total if self.away is None else self.away
+        self.last = [
+            self.wire.start(source.at[i, :, :, 1 - s.c], self.from_core.at[i], s.core) for i in range(2)
+        ]
+
+    def add(self, into, term):
+        into[...] = (into[...].astype(F32) + term.astype(F32)).astype(BF)
+
+    def add_core(self):
+        arrived(self.last)
+        num_z = self.s.num_z
+
+        def one(i, _):
+            yy, zz, xx = i // (2 * num_z), (i // 2) % num_z, i % 2
+            self.add(self.mine(yy, zz, xx), self.from_core[yy, zz, xx])
+            return 0
+        lax.fori_loop(0, 4 * num_z, one, 0)
+
+    def send_second(self):
+        s = self.s
+        self.last = []
+        for i in range(2):
+            yy, xx = jnp.where(s.c == 0, 1 - s.y, i), jnp.where(s.c == 0, i, 1 - s.x)
+            self.last.append(self.wire.start(self.mine(yy, slice(None), xx), self.from_second.at[i], s.second))
+
+    def add_second(self):
+        arrived(self.last)
+        s = self.s
+
+        def one(k, _):
+            i, zz = k // s.num_z, k % s.num_z
+            yy, xx = jnp.where(s.c == 0, s.y, i), jnp.where(s.c == 0, i, s.x)
+            self.add(self.mine(yy, zz, xx), self.from_second[i, zz])
+            return 0
+        lax.fori_loop(0, 2 * s.num_z, one, 0)
+
+    def send_first(self):
+        s = self.s
+        yy, xx = jnp.where(s.c == 0, s.y, 1 - s.y), jnp.where(s.c == 0, 1 - s.x, s.x)
+        self.last = [self.wire.start(self.mine(yy, slice(None), xx), self.from_first, s.first)]
+
+    def add_first(self):
+        arrived(self.last)
+        s = self.s
+
+        def one(zz, _):
+            self.add(self.mine(s.y, zz, s.x), self.from_first[zz])
+            return 0
+        lax.fori_loop(0, s.num_z, one, 0)
+
+    def send_z(self):
+        s = self.s
+        self.last = [
+            self.wire.start(self.mine(s.y, (s.z + k) % s.num_z, s.x), self.from_z.at[k - 1], peer)
+            for k, peer in zip(range(1, s.num_z), s.across_z)
+        ]
+
+    def add_z(self):
+        arrived(self.last)
+        s = self.s
+        total = self.mine(s.y, s.z, s.x)[...].astype(F32)
+        for k in range(s.num_z - 1):
+            total = total + self.from_z[k].astype(F32)
+        part = total.shape[-1] // 2
+        for core in range(2):
+            self.ends[core] = total[:, core * part : (core + 1) * part]
+        self.last = [self.wire.start(self.ends.at[1 - s.c], self.ends.at[2], s.core)]
+
+    def finish(self, out):
+        arrived(self.last)
+        half = self.ends.shape[1]
+        c = self.s.c
+        out[pl.ds(pl.multiple_of(c * half, 16), half)] = self.ends[c]
+        out[pl.ds(pl.multiple_of((1 - c) * half, 16), half)] = self.ends[2]
+
+
+class ScatterTaps(Scatter):
+    def send_core(self):
+        s = self.s
+        self.last = [self.wire.start(self.total.at[:, :, 1 - s.c], self.from_core, s.core)]
+
+    def add_core(self):
+        arrived(self.last)
+
+        def one(i, _):
+            zz, xx = i // 2, i % 2
+            self.add(self.total.at[zz, xx, self.s.c], self.from_core[zz, xx])
+            return 0
+        lax.fori_loop(0, 2 * self.s.num_z, one, 0)
+
+    def send_first(self):
+        s = self.s
+        self.last = [self.wire.start(self.total.at[:, 1 - s.x, s.c], self.from_first, s.x_side)]
+
+    def mine(self, yy, zz, xx):
+        return self.total.at[zz, xx, self.s.c]
+
+
+def norm_back(normal, scale, grad, gain):
+    p = grad * gain
+    flat = jnp.mean(p, axis=-1, keepdims=True)
+    along = jnp.mean(p * normal, axis=-1, keepdims=True)
+    return (p - flat - normal * along) * scale, jnp.sum(grad * normal, axis=0, keepdims=True)
+
+
+def backward_kernel(
+    num_z, length,
+    tok, cot, twist, small_v, table_h, win_h, wout_h, wup_h, gdown_h, kern_h, proj_h, normed_h, sig_h, spec_h,
+    filt_h, conv_h, gated_h, resid_h, normed_two_h, gpre_h,
+    grad_in_o, gin_o, gout_o, gup_o, gdn_o, gains_o, gkern_o,
+    table_v, win_v, wout_v, wup_v, kern_v, proj_v, spec_v, filt_v, conv_v,
+    gated_v, resid_v, normed_two_v, gpre_v,
+    gup_v, gdn_v, gkern_v,
+    core_in, core_out, core_up, core_dn, core_kern,
+    two_in, two_out, two_up, two_dn,
+    one_in, one_out, one_up, one_dn, one_kern,
+    z_in, z_out, z_up, z_dn, z_kern,
+    ends_in, ends_out, ends_up, ends_dn, ends_kern,
+    low_v, gconv_v, gch_v, gmix_v, gain_v, gain_got,
+    send, recv, local,
+):
+    s = Spots(num_z)
+    z, x, y, c = s.z, s.x, s.y, s.c
+    wire, inner = Wire(send, recv), Local(local)
+    rows, width = tok.shape
+    group = width // 2
+    hidden = gpre_v.shape[1]
+    own_dn = [inner.start(gdown_h.at[i, :, :, c], gdn_v.at[i]) for i in range(2)]
+    loads = {}
+    for name, src, dst in (
+        ("normed_two", normed_two_h, normed_two_v), ("gpre", gpre_h, gpre_v), ("wup", wup_h, wup_v),
+        ("resid", resid_h, resid_v), ("wout", wout_h, wout_v), ("proj", proj_h, proj_v), ("conv", conv_h, conv_v),
+        ("gated", gated_h, gated_v), ("table", table_h, table_v), ("spec", spec_h, spec_v), ("filt", filt_h, filt_v),
+        ("kern", kern_h, kern_v), ("win", win_h, win_v),
+    ):
+        loads[name] = inner.start(src, dst)
+
+    def need(*names):
+        for name in names:
+            inner.wait(loads[name])
+
+    s.meet()
+    gin_v, gout_v = wup_v.at[:, :, :, :, :, 0 : 3 * group], wup_v.at[:, :, :, :, :, 3 * group : 4 * group]
+    down = Scatter(wire, s, gdn_v, core_dn, two_dn, one_dn, z_dn, ends_dn, away=gdown_h)
+    up = Scatter(wire, s, gup_v, core_up, two_up, one_up, z_up, ends_up)
+    out = Scatter(wire, s, gout_v, core_out, two_out, one_out, z_out, ends_out)
+    into = Scatter(wire, s, gin_v, core_in, two_in, one_in, z_in, ends_in)
+    taps_grad = ScatterTaps(wire, s, gkern_v, core_kern, None, one_kern, z_kern, ends_kern)
+    down.send_core()
+
+    gains = jnp.concatenate([small_v[k] for k in range(4)], axis=-1)
+
+    need("normed_two", "gpre")
+    wide = 256
+    per = hidden // 2 // wide
+
+    def up_grad(j, _):
+        at = pl.ds(pl.multiple_of(j * wide, wide), wide)
+        grad = dot_rows(normed_two_v[...], gpre_v[:, at]).astype(BF)
+        cols = pl.ds(pl.multiple_of((j % per) * wide, wide), wide)
+        gup_v[j // per, :, :, :, :, cols] = grad.reshape(num_z, 2, 2, width // (4 * num_z), wide)
+        return 0
+    lax.fori_loop(0, 2 * per, up_grad, 0)
+    normed_v = normed_two_v
+    loads["normed"] = inner.start(normed_h, normed_v)
+    up.send_core()
+    for copy in own_dn:
+        inner.wait(copy)
+    down.add_core()
+    down.send_second()
+
+    need("wup", "resid")
+    half = hidden // 2
+    grad = sum(
+        dot_cols(gpre_v[:, h * half : (h + 1) * half], wup_v[h].reshape(width, half)) for h in range(2)
+    )
+    normal, scale = norm_parts(resid_v[...])
+    part, gain_two = norm_back(normal, scale, grad, gains[1:2])
+    resid_v[...] = cot[...].astype(F32) + part
+    low_v[...] = resid_v[...].astype(BF)
+
+    need("wout", "proj", "conv")
+    span = rows // 2
+    for h in range(2):
+        grad = sum(
+            dot_cols(
+                low_v[:, k * group : (k + 1) * group],
+                wout_v[k].reshape(width, group)[h * group : (h + 1) * group],
+            )
+            for k in range(2)
+        )
+        gconv_v[h] = (grad * proj_v[4 + h].astype(F32)).astype(BF)
+        gpre_v[:, (4 + h) * group : (5 + h) * group] = (grad * conv_v[h].astype(F32)).astype(BF)
+    chunk = pl.ds(pl.multiple_of((2 * y + c) * span, span), span)
+    to_channels = [
+        wire.start(gconv_v.at[yy, pl.ds(pl.multiple_of(cc * span, span), span)], gch_v.at[chunk], peer)
+        for (yy, cc), peer in zip(s.group, s.mates)
+    ]
+    gch_v[chunk] = gconv_v[y, pl.ds(pl.multiple_of(c * span, span), span)]
+    up.add_core()
+    up.send_second()
+
+    need("gated")
+    for h in range(2):
+        grad = dot_rows(gated_v[...], low_v[:, h * group : (h + 1) * group]).astype(BF)
+        gout_v[h] = grad.reshape(num_z, 2, 2, width // (4 * num_z), group)
+    out.send_core()
+    down.add_second()
+    down.send_first()
+
+    need("table", "spec", "filt")
+    arrived(to_channels)
+    step = 256
+
+    def turn(i, _):
+        real = pl.ds(pl.multiple_of(i * step, step), step)
+        imag = pl.ds(pl.multiple_of(length + i * step, step), step)
+        re, im = dot(table_v[real], gch_v[...]), dot(table_v[imag], gch_v[...])
+        re_f, im_f = filt_v[real].astype(F32), filt_v[imag].astype(F32)
+        filt_v[real] = (re_f * re + im_f * im).astype(BF)
+        filt_v[imag] = (re_f * im - im_f * re).astype(BF)
+        re_s, im_s = spec_v[real].astype(F32), spec_v[imag].astype(F32)
+        re_k, im_k = re_s * re + im_s * im, re_s * im - im_s * re
+        cosine, sine = twist[real, 0:1], twist[real, 1:2]
+        spec_v[real] = (re_k * cosine - im_k * sine).astype(BF)
+        spec_v[imag] = (im_k * cosine + re_k * sine).astype(BF)
+        return 0
+    lax.fori_loop(0, length // step, turn, 0)
+
+    def back(i, _):
+        at = pl.ds(pl.multiple_of(i * step, step), step)
+        imag = pl.ds(pl.multiple_of(length + i * step, step), step)
+        both = dot(table_v[at], filt_v[0:length]) + dot(table_v[imag], filt_v[length:])
+        gch_v[at] = (both * (1.0 / length)).astype(BF)
+        return 0
+    lax.fori_loop(0, length // step, back, 0)
+    home = pl.ds(pl.multiple_of(c * span, span), span)
+    to_tokens = [
+        wire.start(gch_v.at[pl.ds(pl.multiple_of((2 * yy + cc) * span, span), span)], gmix_v.at[y, home], peer)
+        for (yy, cc), peer in zip(s.group, s.mates)
+    ]
+    gmix_v[y, home] = gch_v[chunk]
+    out.add_core()
+    out.send_second()
+
+    need("kern")
+    taps = jnp.concatenate([small_v[2 * y], small_v[2 * y + 1]], axis=-1)[2:3]
+    tile = 128
+    for j in range(group // tile):
+        cols = slice(j * tile, (j + 1) * tile)
+        both = dot(table_v[0:length], spec_v[0:length, cols]) + dot(table_v[length:], spec_v[length:, cols])
+        grad = kernel_back(kern_v[:, :, :, :, cols].reshape(length, tile).astype(F32), taps[:, cols],
+                           both * (1.0 / length))
+        gkern_v[:, :, :, :, cols] = grad.astype(BF).reshape(num_z, 2, 2, length // (4 * num_z), tile)
+    taps_grad.send_core()
+    down.add_first()
+    down.send_z()
+    up.add_second()
+    up.send_first()
+
+    need("normed", "win")
+    arrived(to_tokens)
+    for h in range(2):
+        grad = gmix_v[h].astype(F32)
+        gpre_v[:, h * group : (h + 1) * group] = (grad * proj_v[2 + h].astype(F32)).astype(BF)
+        gpre_v[:, (2 + h) * group : (3 + h) * group] = (grad * proj_v[h].astype(F32)).astype(BF)
+    for j in range(6):
+        grad = dot_rows(normed_v[...], gpre_v[:, j * group : (j + 1) * group]).astype(BF)
+        gin_v[j // 3, :, :, :, :, (j % 3) * group : (j % 3 + 1) * group] = grad.reshape(
+            num_z, 2, 2, width // (4 * num_z), group)
+    into.send_core()
+    out.add_second()
+    out.send_first()
+    taps_grad.add_core()
+    taps_grad.send_first()
+    into.add_core()
+    into.send_second()
+
+    wide_in = 3 * group
+    grad = sum(
+        dot_cols(gpre_v[:, h * wide_in : (h + 1) * wide_in], win_v[h].reshape(width, wide_in)) for h in range(2)
+    )
+    normal, scale = norm_parts(tok[...].astype(F32))
+    part, gain_one = norm_back(normal, scale, grad, gains[0:1])
+    low_v[...] = (resid_v[...] + part).astype(BF)
+    inner.start(low_v, grad_in_o)
+
+    gain_v[0] = jnp.concatenate([gain_one, gain_two, jnp.zeros((6, width), F32)], axis=0)
+    got = [wire.start(gain_v.at[0], gain_got.at[k], peer) for k, peer in enumerate(s.mates)]
+    up.add_first()
+    up.send_z()
+    arrived(got)
+    gain_v[1] = gain_v[0] + gain_got[0] + gain_got[1] + gain_got[2]
+    got = [wire.start(gain_v.at[1], gain_got.at[3], s.x_side)]
+    out.add_first()
+    out.send_z()
+    taps_grad.add_first()
+    taps_grad.send_z()
+    arrived(got)
+    gain_v[2] = gain_v[1] + gain_got[3]
+    got = [wire.start(gain_v.at[2], gain_got.at[3 + k], peer) for k, peer in zip(range(1, num_z), s.across_z)]
+    into.add_second()
+    into.send_first()
+    down.add_z()
+    up.add_z()
+    out.add_z()
+    taps_grad.add_z()
+    arrived(got)
+    total = gain_v[2]
+    for k in range(1, num_z):
+        total = total + gain_got[3 + k]
+    part = width // 4
+    mine = total[:, 0:part]
+    for k in range(1, 4):
+        mine = jnp.where(2 * y + c == k, total[:, k * part : (k + 1) * part], mine)
+    gains_o[...] = mine
+    into.add_first()
+    into.send_z()
+    down.finish(gdn_o)
+    up.finish(gup_o)
+    out.finish(gout_o)
+    taps_grad.finish(gkern_o)
+    into.add_z()
+    into.finish(gin_o)
+    wire.drain()
+    inner.drain()
+
+
+def kernel_back(kern, taps, grad):
+    length = kern.shape[0]
+    position = lax.broadcasted_iota(jnp.int32, kern.shape, 0)
+    live = position.astype(F32) < taps
+    slope = jnp.tanh(jnp.where(live, kern, 0.0) / SHRINK_SCALE)
+    pooled = jnp.where(live, grad, 0.0)
+    before = jnp.where(position == 0, 0.0, pltpu.roll(pooled, 1, 0))
+    after = jnp.where(position == length - 1, 0.0, pltpu.roll(pooled, length - 1, 0))
+    return jnp.where(live, (before + pooled + after) / 3.0 * slope * slope, 0.0)
+
+
+def backward(num_z, length, tokens, cot, twist, small_f, table, full):
+    rows, width = tokens.shape
+    group = width // 2
+    sds = jax.ShapeDtypeStruct
+    win, wout, wup, gdown, kern, proj, normed, sig, spec, filt, conv, gated, resid, normed_two, gpre = full
+    weights = (win, wout, wup, gdown)
+    vmem, hbm = pl.BlockSpec(memory_space=pltpu.VMEM), pl.BlockSpec(memory_space=pl.ANY)
+
+    def vm(shape, dtype=BF):
+        return pltpu.VMEM(tuple(shape), dtype)
+
+    like = lambda a: vm(a.shape, a.dtype)
+    blocks = [(2 * w.shape[-2], w.shape[-1] // 2) for w in (win, wout, wup, gdown, kern)]
+    outs = [sds((rows, width), BF)] + [sds(b, F32) for b in blocks[:4]]
+    outs += [sds((8, width // 4), F32), sds(blocks[4], F32)]
+    scratch = [like(a) for a in (table, win, wout, wup, kern, proj, spec, filt, conv, gated, resid,
+                                 normed_two, gpre)]
+    scratch += [like(wup), vm(gdown.shape[:3] + gdown.shape[4:]), like(kern)]
+    scratch += [vm(w.shape[:3] + w.shape[4:]) for w in weights] + [vm(kern.shape[:2] + kern.shape[3:])]
+    scratch += [vm((2, num_z) + w.shape[4:]) for w in weights]
+    scratch += [vm((num_z,) + w.shape[-2:]) for w in weights + (kern,)]
+    scratch += [vm((num_z - 1,) + w.shape[-2:]) for w in weights + (kern,)]
+    scratch += [vm((3, w.shape[-2], w.shape[-1] // 2), F32) for w in weights + (kern,)]
+    scratch += [vm((rows, width)), vm((2, rows, group)), vm((length, group)),
+                vm((2, rows, group)), vm((3, 8, width), F32), vm((3 + num_z, 8, width), F32)]
+    scratch += [pltpu.SemaphoreType.DMA((80,)), pltpu.SemaphoreType.DMA((80,)), pltpu.SemaphoreType.DMA((40,))]
+    return pl.pallas_call(
+        partial(backward_kernel, num_z, length),
+        out_shape=outs,
+        in_specs=[vmem] * 4 + [hbm] * 16,
+        out_specs=[hbm] + [vmem] * 6,
+        scratch_shapes=scratch,
+        compiler_params=pltpu.CompilerParams(collective_id=1, has_side_effects=True, vmem_limit_bytes=63 * 2**20),
+        cost_estimate=pl.CostEstimate(flops=17 * 10**9, bytes_accessed=50 * 10**6, transcendentals=2 * 10**6),
+    )(tokens, cot, twist, small_f, table, *full)
 
 
 def fits(num_dp, num_seq, tokens, w_in, w_out, w_up, w_down, kernel):
@@ -627,91 +1048,22 @@
     return all(b.shape[0] % 32 == 0 and b.shape[1] * 2 % 128 == 0 for b in blocks) and tokens.shape[0] == 2
 
 
-def unfold(full):
-    flat = full.reshape(2, -1, full.shape[-1])
-    return jnp.concatenate([flat[0], flat[1]], axis=1)
-
-
 def body(num_dp, num_seq, tokens_in, w_in, w_out, w_up, w_down, norm_gains, kernel, taps, cotangent):
     if not fits(num_dp, num_seq, tokens_in, w_in, w_out, w_up, w_down, kernel):
         return general_body(tokens_in, w_in, w_out, w_up, w_down, norm_gains, kernel, taps, cotangent)
-    num_seqs, local_len, width = tokens_in.shape
-    total_rows = num_seqs * local_len
+    width = tokens_in.shape[-1]
     length = kernel.shape[0] * num_dp
-    table = transform_table(length)
+    num_z = num_dp // 2
+    table, twist = jnp.asarray(transform_table(length)), jnp.asarray(twist_table(length))
     small = jnp.concatenate(
         [norm_gains.astype(F32), taps.astype(F32)[None], jnp.zeros((5, taps.shape[0]), F32)]
     )
-    tokens = tokens_in.reshape(total_rows, width)
-    (out, win_f, wout_f, wup_f, wdown_f, kern_f, small_f, proj, normed, sig, spec, filt_s, conv, gated, resid,
-     normed_two, act, slope) = forward(
-        num_dp // 2, length, tokens, w_in, w_out, w_up, w_down, kernel, small,
-        jnp.asarray(table), jnp.asarray(np.ascontiguousarray(table.T)))
-    full_in, full_out, full_up, full_down = unfold(win_f), unfold(wout_f), unfold(wup_f), unfold(wdown_f)
-    gains_wide = jnp.concatenate([small_f[k] for k in range(4)], axis=-1)[:2]
-    chan = lax.axis_index("seq") // 2
-    core = lax.axis_index("seq") % 2
-    group = width // 2
-    proj = proj.astype(F32)
-    values, gate_one, gate_two = [jnp.concatenate([proj[2 * k], proj[2 * k + 1]], axis=1) for k in range(3)]
-    conv_tok = jnp.concatenate([conv[0], conv[1]], axis=1).astype(F32)
-    inputs = tokens.astype(F32)
-    _, norm_back_one = jax.vjp(norm_rows, inputs, gains_wide[0])
-    _, norm_back_two = jax.vjp(norm_rows, resid, gains_wide[1])
-    grad_rows = cotangent.reshape(total_rows, width)
-    grad_down = contract_rows(act, grad_rows)
-    grad_active = times_transposed(grad_rows, full_down)
-    grad_pre = (slope.astype(F32) * grad_active).astype(BF)
-    grad_up = contract_rows(normed_two, grad_pre)
-    grad_normed_two = times_transposed(grad_pre, full_up)
-    grad_resid_part, grad_gain_two = norm_back_two(grad_normed_two)
-    grad_resid = grad_rows.astype(jnp.float32) + grad_resid_part
-    resid_low = grad_resid.astype(jnp.bfloat16)
-    grad_outw = contract_rows(gated, resid_low)
-    grad_gated = times_transposed(resid_low, full_out)
-    grad_gate_two = grad_gated * conv_tok
-    grad_conv = (grad_gated * gate_two).astype(jnp.bfloat16).reshape(2, local_len, 2, group)
-    sent = grad_conv.transpose(2, 0, 1, 3).reshape(4, local_len, group)
-    grad_ch = lax.all_to_all(sent, "seq", split_axis=0, concat_axis=0, tiled=True).reshape(length, group)
-    tab = jnp.asarray(table)
-    back = dot(tab, grad_ch)
-    be, bf = back[:length], back[length:]
-    hc, hd = filt_s[:length].astype(F32), filt_s[length:].astype(F32)
-    sa, sb = spec[:length].astype(F32), spec[length:].astype(F32)
-    inv = lambda re, im: contract_rows(tab, jnp.concatenate([re, im]).astype(BF)) / length
-    grad_signal = inv(hc * be + hd * bf, hc * bf - hd * be).astype(BF)
-    grad_filt = inv(sa * be + sb * bf, sa * bf - sb * be)
-    home = lax.all_to_all(grad_signal.reshape(4, local_len, group), "seq", split_axis=0, concat_axis=0, tiled=True)
-    grad_mixed = home.reshape(2, 2, local_len, group).transpose(1, 2, 0, 3).reshape(total_rows, width).astype(F32)
-    kern_cols = kern_f.reshape(length, group).astype(F32)
-    taps_f = jnp.concatenate([small_f[2 * chan], small_f[2 * chan + 1]], axis=-1)[2]
-    _, filter_back = jax.vjp(partial(shape_filter, taps=taps_f.astype(jnp.int32)), kern_cols)
-    grad_kern = filter_back(grad_filt)[0]
-    swap = [(2 * i + j, 2 * i + 1 - j) for i in range(2) for j in range(2)]
-    part = group // 2
-    mine = lax.dynamic_slice_in_dim(grad_kern, core * part, part, 1)
-    other = lax.dynamic_slice_in_dim(grad_kern, (1 - core) * part, part, 1)
-    mine = mine + lax.ppermute(other.astype(BF), "seq", swap).astype(F32)
-    grad_proj = jnp.concatenate([grad_mixed * gate_one, grad_mixed * values, grad_gate_two], axis=1)
-    grad_proj = grad_proj.astype(jnp.bfloat16)
-    grad_inw = contract_rows(normed, grad_proj)
-    grad_normed = times_transposed(grad_proj, full_in)
-    grad_input_part, grad_gain_one = norm_back_one(grad_normed)
-    grad_inputs = (
-        (grad_resid + grad_input_part).astype(jnp.bfloat16).reshape(num_seqs, local_len, width)
-    )
-    grad_gain_pair = jnp.stack([grad_gain_one, grad_gain_two])
-
-    def scatter_dp(v):
-        return lax.psum_scatter(v.astype(BF), "dp", scatter_dimension=0, tiled=True).astype(F32)
-
-    def scatter_seq(v):
-        return lax.psum_scatter(v.astype(BF), "seq", scatter_dimension=1, tiled=True).astype(F32)
-
-    weights = [scatter_seq(scatter_dp(v)) for v in (grad_inw, grad_outw, grad_up, grad_down)]
-    kern_done = scatter_dp(mine)
-    gain_done = lax.psum(scatter_seq(grad_gain_pair), "dp")
-    return (out.reshape(num_seqs, local_len, width), grad_inputs, *weights, gain_done, kern_done)
+    tokens, cot = tokens_in.reshape(-1, width), cotangent.reshape(-1, width)
+    out, win, wout, wup, gdown, kern, small_f, *saved = forward(
+        num_z, length, tokens, cot, w_in, w_out, w_up, w_down, kernel, small, twist, table)
+    grad_in, gin, gout, gup, gdn, gains, gkern = backward(
+        num_z, length, tokens, cot, twist, small_f, table, [win, wout, wup, gdown, kern, *saved])
+    return (out.reshape(tokens_in.shape), grad_in.reshape(tokens_in.shape), gin, gout, gup, gdn, gains[:2], gkern)
 
 
 def solution(mesh):

time: 715 us -> 256 us (0.36); the launches traced: 707 us -> 255 us
  waiting for transfers between devices: 417 us -> 0 us
  Pallas kernels: 113 us -> 240 us
  local copies, waits for them, and re-layouts: 59.5 us -> 13.2 us
  matrix products: 43.4 us -> 0 us
  blocking collectives: 37.1 us -> 0 us
  other arithmetic: 17.7 us -> 2.03 us
  between operations: 15.2 us -> 0.7 us
    reduce_scatter x5 -> x0, waiting for transfers between devices: 279 us -> none  [the longest x4 257 us: scatter_dp(): lax.psum_scatter(v.astype(BF), 'dp', scatter_dimension=0, tiled=True)]
    unnamed x15 -> x0, waiting for transfers between devices: 129 us -> none
    pallas_call x0 -> x1, Pallas kernels: none -> 117 us  [backward(): pl.pallas_call(partial(backward_kernel, num_z, length), out_shape=outs, i...]
    dot_general x13 -> x0, matrix products: 43.4 us -> none  [the longest x8 25.4 us: contract_rows(): lax.dot_general(left, right, (((0,), (0,)), ((), ())), preferred_element_...]
    psum x1 -> x0, blocking collectives: 22 us -> none  [body(): gain_done = lax.psum(scatter_seq(grad_gain_pair), 'dp')]
    unnamed x99 -> x17, local copies, waits for them, and re-layouts: 32.5 us -> 11.8 us
    all_to_all x1 -> x0, blocking collectives: 15.1 us -> none  [body(): lax.all_to_all(grad_signal.reshape(4, local_len, group), 'seq', split_axi...]
    slice x4 -> x1, local copies, waits for them, and re-layouts: 13.1 us -> 1.34 us  [body(): gains[:2]]
  transfers between devices with their start and end apart: 12 -> 0, of which waited for: 10 -> 0; matrix products, arithmetic and copies ran while one was open for 10% -> 0% of each run, Pallas kernels for 0% -> 0%
where the time goes in v2:
time: 256 us; the launch traced here: 255 us
  Pallas kernels  240 us (94%)
  local copies, waits for them, and re-layouts  13.2 us (5%)
    pallas_call x1, Pallas kernels, forward(): pl.pallas_call(partial(forward_kernel, num_z), out_shape=outs, in_specs=[...  123 us
    pallas_call x1, Pallas kernels, backward(): pl.pallas_call(partial(backward_kernel, num_z, length), out_shape=outs, i...  117 us
    unnamed x17, local copies, waits for them, and re-layouts  11.8 us

profile of v2, /device:TPU:0, one launch (start us, length us, event | category | flops | bytes accessed | tf_op | source)
XLA Modules:
  0.0 255.5 jit_solution(2562269869910490754)
XLA Ops:
  0.6 0.1 pad.2.clone
  0.7 0.7 convert_element_type.7
  1.4 0.7 convert_element_type.6
  2.1 0.7 maximum_maximum_fusion.small
  2.7 1.5 copy.20.kern
  4.3 1.7 copy.19.w_down
  6.0 122.7 %shard_map.170 = (bf16[512,768]{1,0:T(8,128)(2,1)}, bf16[2,4,2,2,48,1152]{5,4,3,2,1,0:T(8,128)(2,1)}, bf16[2,4,2,2,48,384]{5,4,3,2,1,0:T(8,128)(2,1)}, bf16[2,4,...) custom-call(bf16[512,768]{1,0:T(8,128)(2,1)} %bitcast.8, ...), custom_call_target="tpu_custom_call" | custom-call | flops 16999999488 | bytes 50000000 | tf_op jit(solution)/shard_map/pallas_call | solution.py:643
  128.7 0.0 copy-start
  128.7 116.8 %shard_map.171 = (bf16[512,768]{1,0:T(8,128)(2,1)}, f32[96,576]{1,0:T(8,128)}, f32[96,192]{1,0:T(8,128)}, f32[96,768]{1,0:T(8,128)}, f32[384,192]{1,0:T(8,128)}, /*index=5*/f32[8,192]{1,0:T(8,128)}, f32[128,192]{1,0:T(8,128)}) custom-call(bf16[512,768]{1,0:T(8,128)(2,1)} %bitcast.9, bf16[512,768]{1,0:T(8,128)(2,1)} %bitcast.11, ...), custom_call_target="tpu_custom_call" | custom-call | flops 16999999488 | bytes 50000000 | tf_op jit(solution)/shard_map/pallas_call | solution.py:1033
  245.6 0.0 copy-start.2
  245.6 0.0 copy-start.3
  245.6 0.0 copy-start.1
  245.6 1.3 slice.3
  247.0 1.6 copy.22
  248.6 1.9 copy.21
  250.5 0.0 copy-done
  250.5 0.9 copy.28
  251.3 2.1 copy.29
  253.4 0.0 copy-done.2
  253.4 0.7 copy.30
  254.1 0.0 copy-done.3
  254.1 0.6 copy.31
  254.7 0.0 copy-done.1
  254.8 0.7 copy.32
  (1 shorter events, 0.0 us)
Async XLA Ops:
  128.7 121.7 %copy-start = (bf16[512,768]{1,0:T(8,128)(2,1)S(1)}, bf16[512,768]{1,0:T(8,128)(2,1)}, u32[]{:S(2)}) copy-start(bf16[512,768]{1,0:T(8,128)(2,1)} %get-tuple-element.32) | copy-start | bytes 2359300
  245.6 7.8 %copy-start.2 = (f32[96,576]{1,0:T(8,128)S(1)}, f32[96,576]{1,0:T(8,128)}, u32[]{:S(2)}) copy-start(f32[96,576]{1,0:T(8,128)} %get-tuple-element.74) | copy-start | bytes 663556
  245.6 8.5 %copy-start.3 = (f32[96,192]{1,0:T(8,128)S(1)}, f32[96,192]{1,0:T(8,128)}, u32[]{:S(2)}) copy-start(f32[96,192]{1,0:T(8,128)} %get-tuple-element.75) | copy-start | bytes 221188
  245.6 9.1 %copy-start.1 = (f32[96,768]{1,0:T(8,128)S(1)}, f32[96,768]{1,0:T(8,128)}, u32[]{:S(2)}) copy-start(f32[96,768]{1,0:T(8,128)} %get-tuple-element.76) | copy-start | bytes 884740

commit v3 on v0

--- a/solution.py
+++ b/solution.py
@@ -2,6 +2,10 @@
 import math
 
 import jax
+from jax.experimental import pallas as pl
+from jax.experimental.pallas import tpu as pltpu
+import ml_dtypes
+import numpy as np
 import jax.numpy as jnp
 from jax import lax
 from jax.sharding import PartitionSpec as P
@@ -102,7 +106,7 @@
     return lax.all_to_all(field, "seq", split_axis=1, concat_axis=2, tiled=True)
 
 
-def body(tokens_in, w_in, w_out, w_up, w_down, norm_gains, kernel, taps, cotangent):
+def general_body(tokens_in, w_in, w_out, w_up, w_down, norm_gains, kernel, taps, cotangent):
     w_in_rows, w_out_rows, w_up_rows, w_down_rows, gains = (
         lax.all_gather(w_in, "seq", axis=1, tiled=True),
         lax.all_gather(w_out, "seq", axis=1, tiled=True),
@@ -225,9 +229,923 @@
     )
 
 
+MESH = pl.DeviceIdType.MESH
+BF = jnp.bfloat16
+F32 = jnp.float32
+
+
+class Remote:
+    def __init__(self, wire, slot, src, dst, peer):
+        self.wire, self.slot, self.src, self.dst, self.peer = wire, slot, src, dst, peer
+
+    def named(self):
+        return pltpu.make_async_remote_copy(
+            src_ref=self.src(), dst_ref=self.dst(), send_sem=self.wire.send.at[self.slot],
+            recv_sem=self.wire.recv.at[self.slot], device_id=self.peer, device_id_type=MESH,
+        )
+
+    def wait_recv(self):
+        self.named().wait_recv()
+
+
+class Wire:
+    def __init__(self, send, recv, spots):
+        self.send, self.recv, self.s, self.made = send, recv, spots, []
+
+    def start(self, src, dst, peer, core=None):
+        src, dst = (end if callable(end) else partial(lambda ref: ref, end) for end in (src, dst))
+        copy = Remote(self, len(self.made), src, dst, peer)
+        copy.named().start()
+        self.made.append((core, copy))
+        return copy
+
+    def drain(self):
+        for which in (None, 0, 1):
+            @self.s.on(which)
+            def _():
+                for core, copy in self.made:
+                    if core == which:
+                        copy.named().wait_send()
+
+
+class Local:
+    def __init__(self, sems):
+        self.sems, self.made, self.open = sems, 0, []
+
+    def start(self, src, dst):
+        copy = pltpu.make_async_copy(src, dst, self.sems.at[self.made])
+        self.made += 1
+        copy.start()
+        self.open.append(copy)
+        return copy
+
+    def wait(self, copy):
+        copy.wait()
+        self.open = [other for other in self.open if other is not copy]
+
+    def drain(self):
+        for copy in list(self.open):
+            self.wait(copy)
+
+
+def arrived(copies):
+    for copy in copies:
+        copy.wait_recv()
+
+
+class Spots:
+    def __init__(self, num_z):
+        dp, sq = lax.axis_index("dp"), lax.axis_index("seq")
+        z, x, y, c = dp // 2, dp % 2, sq // 2, sq % 2
+        self.num_z = num_z
+        self.z, self.x, self.y, self.c = z, x, y, c
+        self.own = dict(x=x, y=y, z=z)
+        self.size = dict(x=2, y=2, z=num_z)
+        self.core = self.at(z, x, y, 1 - c)
+        self.others = dict(x=[1 - x], y=[1 - y], z=[(z + k) % num_z for k in range(1, num_z)])
+        self.along = dict(
+            x=[self.at(z, 1 - x, y, c)], y=[self.at(z, x, 1 - y, c)],
+            z=[self.at(other, x, y, c) for other in self.others["z"]],
+        )
+        self.group = [((y + i) % 2, (c + j) % 2) for i, j in ((1, 0), (1, 1), (0, 1))]
+        self.mates = [self.at(z, x, yy, cc) for yy, cc in self.group]
+
+    def at(self, z, x, y, c):
+        return (z * 2 + x, y * 2 + c)
+
+    def on(self, core):
+        return (lambda body: body()) if core is None else pl.when(self.c == core)
+
+    def meet(self):
+        barrier = pltpu.get_barrier_semaphore()
+        peers = self.along["z"] + self.along["x"] + self.mates
+        for peer in peers:
+            pl.semaphore_signal(barrier, inc=1, device_id=peer, device_id_type=MESH)
+        pl.semaphore_wait(barrier, len(peers))
+
+
+def both_cores(orders):
+    return [(None, orders[0])] if len(orders) == 1 else list(enumerate(orders))
+
+
+def block_index(s, axes, wide, core, at=None):
+    place = {**s.own, **(at or {})}
+    index = tuple(slice(None) if axis in wide else place[axis] for axis in axes)
+    return index if core is None else index + (core,)
+
+
+class Gather:
+    def __init__(self, wire, spots, full, axes, *orders, part=None):
+        self.wire, self.s, self.full, self.axes, self.part = wire, spots, full, axes, part
+        self.orders, self.last = both_cores(orders), {}
+
+    def view(self, have):
+        index = block_index(self.s, self.axes, have, self.s.c)
+        return self.full.at[index if self.part is None else index + (self.part,)]
+
+    def settle(self):
+        for core, copies in self.last.items():
+            self.s.on(core)(partial(arrived, copies))
+        self.last = {}
+
+    def step(self, n):
+        s = self.s
+        if n == len(self.orders[0][1]):
+            self.settle()
+            view = partial(self.view, self.axes)
+            self.last[None] = [self.wire.start(view, view, s.core)]
+            return
+        before, self.last = self.last, {}
+        for core, order in self.orders:
+            @s.on(core)
+            def _():
+                arrived(before.get(core, []))
+                view = partial(self.view, order[:n])
+                self.last[core] = [self.wire.start(view, view, peer, core) for peer in s.along[order[n]]]
+
+    def done(self):
+        self.settle()
+
+
+class Scatter:
+    def __init__(self, wire, spots, total, axes, orders, from_core, got, result, away=None):
+        self.wire, self.s, self.total, self.axes = wire, spots, total, axes
+        self.orders = [(core, order[::-1]) for core, order in both_cores(orders)]
+        self.from_core, self.got, self.result, self.away = from_core, got, result, away
+        self.last = {}
+
+    def mine(self, wide, at=None):
+        return self.total.at[block_index(self.s, self.axes, wide, None if self.away is not None else self.s.c, at)]
+
+    def send_core(self):
+        s = self.s
+        source = self.total if self.away is None else self.away
+        rest = (slice(None),) * (len(self.axes) - 1) + (1 - s.c,)
+        self.last = [
+            self.wire.start(source.at[(i,) + rest], self.from_core.at[i], s.core)
+            for i in range(self.from_core.shape[0])
+        ]
+
+    def add_core(self):
+        arrived(self.last)
+        self.last = {}
+        s = self.s
+        count = math.prod(s.size[axis] for axis in self.axes)
+
+        def one(i, _):
+            at, left = {}, i
+            for axis in reversed(self.axes):
+                at[axis], left = left % s.size[axis], left // s.size[axis]
+            into = self.mine("", at)
+            term = self.from_core[tuple(at[axis] for axis in self.axes)]
+            into[...] = (into[...].astype(F32) + term.astype(F32)).astype(BF)
+            return 0
+        lax.fori_loop(0, count, one, 0)
+
+    def stages(self, order, n):
+        s = self.s
+        begin = 0
+        for k in range(n + 1):
+            wide = sorted(order[k + 1 :])
+            count = math.prod(s.size[axis] for axis in wide)
+            if k < n:
+                begin += count * (s.size[order[k]] - 1)
+        return order[n], wide, count, begin
+
+    def slots(self, start, count):
+        return self.got.at[start] if count is None else self.got.at[start : start + count]
+
+    def send(self, n):
+        s = self.s
+        for core, order in self.orders:
+            axis, wide, count, begin = self.stages(order, n)
+
+            @s.on(core)
+            def _():
+                self.last[core] = []
+                for j, (other, peer) in enumerate(zip(s.others[axis], s.along[axis])):
+                    outer = s.size[wide[0]] if len(wide) == 2 else 1
+                    inner = count // outer
+                    for i in range(outer):
+                        at = {axis: other}
+                        if len(wide) == 2:
+                            at[wide[0]] = i
+                        start = begin + j * count + i * inner
+                        src = partial(self.mine, wide[-1:], at)
+                        dst = partial(self.slots, start, inner if wide else None)
+                        self.last[core].append(self.wire.start(src, dst, peer, core))
+
+    def add(self, n):
+        s = self.s
+        for core, order in self.orders:
+            axis, wide, count, begin = self.stages(order, n)
+            peers = len(s.others[axis])
+
+            @s.on(core)
+            def _():
+                arrived(self.last[core])
+                if n == len(order) - 1:
+                    total = self.mine("")[...].astype(F32)
+                    for j in range(peers):
+                        total = total + self.got[begin + j].astype(F32)
+                    self.result[...] = total
+                    return
+
+                def one(i, _):
+                    at, left = {}, i
+                    for a in reversed(wide):
+                        at[a], left = left % s.size[a], left // s.size[a]
+                    into = self.mine("", at)
+                    total = into[...].astype(F32)
+                    for j in range(peers):
+                        total = total + self.got[begin + j * count + i].astype(F32)
+                    into[...] = total.astype(BF)
+                    return 0
+                lax.fori_loop(0, count, one, 0)
+
+    def trade(self, ends):
+        part = ends.shape[-1]
+        for core in range(2):
+            ends[core] = self.result[:, core * part : (core + 1) * part]
+        self.last = [self.wire.start(ends.at[1 - self.s.c], ends.at[2], self.s.core)]
+        self.ends = ends
+
+    def finish(self, out, turned=False):
+        arrived(self.last)
+        c, own, other = self.s.c, self.ends[self.s.c], self.ends[2]
+        both = jnp.concatenate([jnp.where(c == 0, own, other), jnp.where(c == 0, other, own)], axis=0)
+        out[...] = both.T if turned else both
+
+
+def norm_parts(values):
+    center = values - jnp.mean(values, axis=-1, keepdims=True)
+    spread = jnp.mean(center * center, axis=-1, keepdims=True)
+    scale = lax.rsqrt(spread + EPSILON)
+    return center * scale, scale
+
+
+def norm_back(normal, scale, grad, gain):
+    p = grad * gain
+    flat = jnp.mean(p, axis=-1, keepdims=True)
+    along = jnp.mean(p * normal, axis=-1, keepdims=True)
+    return (p - flat - normal * along) * scale, jnp.sum(grad * normal, axis=0, keepdims=True)
+
+
+def dot(left, right):
+    return jnp.dot(left, right, preferred_element_type=F32)
+
+
+def dot_rows(left, right):
+    return lax.dot_general(left, right, (((0,), (0,)), ((), ())), preferred_element_type=F32)
+
+
+def dot_cols(left, right):
+    return lax.dot_general(left, right, (((1,), (1,)), ((), ())), preferred_element_type=F32)
+
+
+def live_taps(kern, taps):
+    position = lax.broadcasted_iota(jnp.int32, kern.shape, 0)
+    return position, position.astype(F32) < taps
+
+
+def pool(values, position):
+    length = values.shape[0]
+    before = jnp.where(position == 0, 0.0, pltpu.roll(values, 1, 0))
+    after = jnp.where(position == length - 1, 0.0, pltpu.roll(values, length - 1, 0))
+    return (before + values + after) / 3.0
+
+
+def make_filter(kern, taps):
+    position, live = live_taps(kern, taps)
+    masked = jnp.where(live, kern, 0.0)
+    shrunk = masked - SHRINK_SCALE * jnp.tanh(masked / SHRINK_SCALE)
+    return jnp.where(live, pool(shrunk, position), 0.0)
+
+
+def kernel_back(kern, taps, grad):
+    position, live = live_taps(kern, taps)
+    slope = jnp.tanh(jnp.where(live, kern, 0.0) / SHRINK_SCALE)
+    return jnp.where(live, pool(jnp.where(live, grad, 0.0), position) * slope * slope, 0.0)
+
+
+GELU_K = math.sqrt(2.0 / math.pi)
+
+
+def gelu_both(v):
+    square = v * v
+    t = jnp.tanh(GELU_K * v * (1.0 + 0.044715 * square))
+    half = 0.5 * (1.0 + t)
+    slope = half + 0.5 * v * (1.0 - t * t) * (GELU_K * (1.0 + 3 * 0.044715 * square))
+    return v * half, slope
+
+
+def spans(start, size, step=16):
+    return pl.ds(pl.multiple_of(start, step), size)
+
+
+def transform_table(length):
+    k = 2 * np.arange(length)[:, None] + 1
+    angle = np.pi / (4 * length) * ((k * k.T) % (8 * length))
+    return np.concatenate([np.cos(angle), np.sin(angle)]).astype(np.float32).astype(ml_dtypes.bfloat16)
+
+
+def twist_table(length):
+    angle = np.pi / (4 * length) * (2 * np.arange(length) + 1)
+    return np.stack([np.cos(angle), np.sin(angle)], axis=1).astype(np.float32)
+
+
+ORDER_OUT = ("zxy", "zyx")
+ORDER_UP = ("zxy", "zyx")
+ORDER_DOWN = ("zyx", "yzx")
+STEP = 256
+
+
+def forward_kernel(
+    num_z, length,
+    tok, cot, w_in, w_out, w_up, w_down_t, kern_t, gains_in, taps_in, twist, table_hbm,
+    out_o, win_o, wout_o, wup_o, gdown_o, kern_o, small_o, proj_o, normed_o, spec_o, filt_o, conv_o,
+    gated_o, resid_o, normed_two_o, gpre_o,
+    win_v, wout_v, wup_v, wdown_v, kern_v, small_v,
+    pre_in, pre_out, pre_up, pre_down, pre_kern, w_down, kern,
+    table_v, proj_v, normed_own, normed_v, sig_v, spec_v, filt_v, filt_low, turned_v, conv_v, gated_ch,
+    gated_v, resid_v, normed_two_v, act_v, slope_v, gdown_v, out_v,
+    send, recv, local,
+):
+    s = Spots(num_z)
+    z, x, y, c = s.z, s.x, s.y, s.c
+    wire, inner = Wire(send, recv, s), Local(local)
+    load_table = inner.start(table_hbm, table_v)
+    rows, width = tok.shape
+    group, span = width // 2, rows // 2
+    hidden = act_v.shape[1]
+    me = 2 * y + c
+    w_down[...] = w_down_t[...].T
+    kern[...] = kern_t[...].T
+    small_v[me, 0:2] = gains_in[...].astype(F32)
+    small_v[me, 2:3] = taps_in[...].astype(F32)
+    s.meet()
+
+    half = w_in.shape[0] // 2
+    trade_in = [
+        wire.start(w_in.at[spans(cc * half, half)], pre_in.at[me], peer) for (yy, cc), peer in zip(s.group, s.mates)
+    ]
+    smalls = [wire.start(small_v.at[me], small_v.at[me], peer) for peer in s.mates]
+    pairs = [(kern, pre_kern), (w_out, pre_out), (w_up, pre_up), (w_down, pre_down)]
+    traded = []
+    for src, pre in pairs:
+        half = src.shape[0] // 2
+        traded.append(wire.start(src.at[spans((1 - c) * half, half)], pre.at[c], s.core))
+    half = w_in.shape[0] // 2
+    pre_in[me] = w_in[spans(c * half, half)]
+    for src, pre in pairs:
+        half = src.shape[0] // 2
+        pre[c] = src[spans(c * half, half)]
+
+    g_in = [Gather(wire, s, win_v, "zx", "zx", part=k) for k in range(3)]
+    g_kern = Gather(wire, s, kern_v, "zx", "zx")
+    g_out = Gather(wire, s, wout_v, "yzx", *ORDER_OUT)
+    g_up = Gather(wire, s, wup_v, "yzx", *ORDER_UP)
+    g_down = Gather(wire, s, wdown_v, "yzx", *ORDER_DOWN)
+
+    def join(i, full):
+        traded[i].wait_recv()
+        pre = pairs[i][1]
+        full[block_index(s, "zx" if i == 0 else "yzx", "", c)] = jnp.concatenate([pre[0], pre[1]], axis=-1)
+
+    arrived(trade_in)
+    whole = jnp.concatenate([pre_in[k] for k in range(4)], axis=-1)
+    for k in range(3):
+        left, right = (whole[:, (2 * k + h) * group : (2 * k + h + 1) * group] for h in range(2))
+        win_v[z, x, c, k] = jnp.where(y == 0, left, right)
+        g_in[k].step(0)
+
+    arrived(smalls)
+    gains = jnp.concatenate([small_v[k] for k in range(4)], axis=-1)
+    normed, _ = norm_parts(tok[...].astype(F32))
+    normed_own[...] = (normed * gains[0:1]).astype(BF)
+    chunk = spans(me * span, span)
+    to_group = [
+        wire.start(normed_own.at[spans(cc * span, span)], normed_v.at[chunk], peer)
+        for (yy, cc), peer in zip(s.group, s.mates)
+    ]
+    normed_v[chunk] = normed_own[spans(c * span, span)]
+    join(0, kern_v)
+    g_kern.step(0)
+    join(1, wout_v)
+    join(2, wup_v)
+    join(3, wdown_v)
+
+    g_in[0].step(1)
+    g_in[1].step(1)
+    g_out.step(0)
+    g_in[2].step(1)
+    g_up.step(0)
+    g_kern.step(1)
+    g_in[0].step(2)
+    g_in[1].step(2)
+    g_down.step(0)
+    g_in[2].step(2)
+    g_kern.step(2)
+    g_out.step(1)
+
+    g_kern.done()
+    taps = jnp.concatenate([small_v[2 * y], small_v[2 * y + 1]], axis=-1)[2:3]
+    tile = 128
+    for j in range(group // tile):
+        cols = slice(j * tile, (j + 1) * tile)
+        filt = make_filter(kern_v[:, :, :, :, cols].reshape(length, tile).astype(F32), taps[:, cols])
+        filt_low[:, cols] = filt.astype(BF)
+    inner.wait(load_table)
+
+    def spectrum(i, _):
+        real, imag = spans(i * STEP, STEP, STEP), spans(length + i * STEP, STEP, STEP)
+        re, im = dot(table_v[real], filt_low[...]), dot(table_v[imag], filt_low[...])
+        cosine, sine = twist[real, 0:1], twist[real, 1:2]
+        filt_v[real] = (re * cosine + im * sine).astype(BF)
+        filt_v[imag] = (im * cosine - re * sine).astype(BF)
+        return 0
+    lax.fori_loop(0, length // STEP, spectrum, 0)
+
+    g_up.step(1)
+    g_out.step(2)
+    arrived(to_group)
+    g_in[0].done()
+    g_in[1].done()
+
+    def project(k, at):
+        return dot(normed_v[at], win_v[:, :, :, k].reshape(width, group))
+
+    tall = length // 2
+    for i in range(2):
+        at = slice(i * tall, (i + 1) * tall)
+        value, gate = project(0, at), project(1, at)
+        proj_v[0, at] = value.astype(BF)
+        proj_v[1, at] = gate.astype(BF)
+        sig_v[at] = (value * gate).astype(BF)
+    g_up.step(2)
+    g_down.step(1)
+    g_in[2].done()
+    for i in range(2):
+        at = slice(i * tall, (i + 1) * tall)
+        proj_v[2, at] = project(2, at).astype(BF)
+
+    def convolve(i, _):
+        real, imag = spans(i * STEP, STEP, STEP), spans(length + i * STEP, STEP, STEP)
+        re_s, im_s = dot(table_v[real], sig_v[...]), dot(table_v[imag], sig_v[...])
+        spec_v[real] = re_s.astype(BF)
+        spec_v[imag] = im_s.astype(BF)
+        re_f, im_f = filt_v[real].astype(F32), filt_v[imag].astype(F32)
+        turned_v[real] = (re_s * re_f - im_s * im_f).astype(BF)
+        turned_v[imag] = (re_s * im_f + im_s * re_f).astype(BF)
+        return 0
+    lax.fori_loop(0, length // STEP, convolve, 0)
+
+    def back(i, _):
+        at, imag = spans(i * STEP, STEP, STEP), spans(length + i * STEP, STEP, STEP)
+        both = dot(table_v[at], turned_v[0:length]) + dot(table_v[imag], turned_v[length:])
+        conv = (both * (1.0 / length)).astype(BF)
+        conv_v[at] = conv
+        gated_ch[at] = (proj_v[2, at].astype(F32) * conv.astype(F32)).astype(BF)
+        return 0
+    lax.fori_loop(0, length // STEP, back, 0)
+
+    home = spans(c * span, span)
+    to_tokens = [
+        wire.start(gated_ch.at[spans((2 * yy + cc) * span, span)], gated_v.at[y, home], peer)
+        for (yy, cc), peer in zip(s.group, s.mates)
+    ]
+    gated_v[y, home] = gated_ch[chunk]
+    g_out.step(3)
+    g_down.step(2)
+    g_up.step(3)
+    for src, dst in ((win_v, win_o), (kern_v, kern_o), (small_v, small_o), (proj_v, proj_o),
+                     (normed_v, normed_o), (spec_v, spec_o), (filt_v, filt_o), (conv_v, conv_o)):
+        inner.start(src, dst)
+    g_out.done()
+    arrived(to_tokens)
+
+    for k in range(2):
+        cols = slice(k * group, (k + 1) * group)
+        mixed = sum(
+            dot(gated_v[h], wout_v[k, h * num_z // 2 : (h + 1) * num_z // 2].reshape(group, group)) for h in range(2)
+        )
+        resid_v[:, cols] = tok[:, cols].astype(F32) + mixed
+    normed_two, _ = norm_parts(resid_v[...])
+    normed_two_v[...] = (normed_two * gains[1:2]).astype(BF)
+    for src, dst in ((wout_v, wout_o), (gated_v, gated_o), (resid_v, resid_o), (normed_two_v, normed_two_o)):
+        inner.start(src, dst)
+    g_up.done()
+
+    wide = 256
+    per = hidden // 2 // wide
+
+    def feed(j, _):
+        weight = wup_v[j // per, :, :, :, :, spans((j % per) * wide, wide, wide)].reshape(width, wide)
+        act, slope = gelu_both(dot(normed_two_v[...], weight))
+        at = spans(j * wide, wide, wide)
+        act_v[:, at] = act.astype(BF)
+        slope_v[:, at] = slope.astype(BF)
+        return 0
+    lax.fori_loop(0, 2 * per, feed, 0)
+    inner.start(wup_v, wup_o)
+    g_down.step(3)
+
+    deep = hidden // (2 * num_z)
+
+    def down_grad(i, _):
+        grad = dot_rows(act_v[:, spans(i * deep, deep, deep)], cot[...]).astype(BF)
+        for h in range(2):
+            gdown_v[h, i // 2, i % 2] = grad[:, h * group : (h + 1) * group].reshape(2, deep // 2, group)
+        return 0
+    lax.fori_loop(0, 2 * num_z, down_grad, 0)
+    inner.start(gdown_v, gdown_o)
+    g_down.done()
+
+    def pre_grad(i, _):
+        at = spans(i * deep, deep, deep)
+        grad = sum(
+            dot_cols(cot[:, h * group : (h + 1) * group], wdown_v[h, i // 2, i % 2].reshape(deep, group))
+            for h in range(2)
+        )
+        slope_v[:, at] = (slope_v[:, at].astype(F32) * grad).astype(BF)
+        return 0
+    lax.fori_loop(0, 2 * num_z, pre_grad, 0)
+    inner.start(slope_v, gpre_o)
+    for h in range(2):
+        cols = slice(h * group, (h + 1) * group)
+        out_v[:, cols] = (resid_v[:, cols] + dot(act_v[...], wdown_v[h].reshape(hidden, group))).astype(BF)
+    inner.start(out_v, out_o)
+    wire.drain()
+    inner.drain()
+
+
+def vm(shape, dtype=BF):
+    return pltpu.VMEM(tuple(shape), dtype)
+
+
+VMEM_SPEC, HBM_SPEC = pl.BlockSpec(memory_space=pltpu.VMEM), pl.BlockSpec(memory_space=pl.ANY)
+
+
+def forward(num_z, length, tokens, cot, w_in, w_out, w_up, w_down_t, kernel_t, gains, taps, twist, table):
+    rows, width = tokens.shape
+    group = width // 2
+    part = w_down_t.shape[1]
+    hidden = part * num_z * 2
+    sds = jax.ShapeDtypeStruct
+    axes = (2, num_z, 2, 2)
+    win = axes[1:] + (3, w_in.shape[0] // 2, group)
+    wout, wup, wdown = axes + (w_out.shape[0] // 2, group), axes + (w_up.shape[0] // 2, hidden // 2), axes + (part // 2, group)
+    kern = axes[1:] + (kernel_t.shape[1] // 2, group)
+    small = (4, 8, width // 4)
+    acts = dict(
+        proj=((3, length, group), BF), normed=((length, width), BF), spec=((2 * length, group), BF),
+        filt=((2 * length, group), BF), conv=((length, group), BF), gated=((2, rows, group), BF),
+        resid=((rows, width), F32), normed_two=((rows, width), BF), gpre=((rows, hidden), BF),
+    )
+    outs = [sds((rows, width), BF)] + [sds(w, BF) for w in (win, wout, wup, wdown, kern)] + [sds(small, F32)]
+    outs += [sds(*acts[k]) for k in acts]
+    act = lambda k: vm(*acts[k])
+    scratch = [vm(w) for w in (win, wout, wup, wdown, kern)] + [vm(small, F32)]
+    scratch += [vm((4, w_in.shape[0] // 2, w_in.shape[1])), vm((2, w_out.shape[0] // 2, w_out.shape[1])),
+                vm((2, w_up.shape[0] // 2, w_up.shape[1])), vm((2, part // 2, w_down_t.shape[0])),
+                vm((2, kernel_t.shape[1] // 2, kernel_t.shape[0])), vm(w_down_t.shape[::-1]), vm(kernel_t.shape[::-1])]
+    scratch += [vm(table.shape), act("proj"), vm((rows, width)), act("normed"), vm((length, group)), act("spec"),
+                act("filt"), vm((length, group)), vm((2 * length, group)), act("conv"), vm((length, group)),
+                act("gated"), act("resid"), act("normed_two"), act("gpre"), act("gpre"), vm(wdown), vm((rows, width))]
+    scratch += [pltpu.SemaphoreType.DMA((160,)), pltpu.SemaphoreType.DMA((160,)), pltpu.SemaphoreType.DMA((40,))]
+    return pl.pallas_call(
+        partial(forward_kernel, num_z, length),
+        out_shape=outs,
+        in_specs=[VMEM_SPEC] * 10 + [HBM_SPEC],
+        out_specs=[HBM_SPEC] * len(outs),
+        scratch_shapes=scratch,
+        compiler_params=pltpu.CompilerParams(collective_id=0, has_side_effects=True, vmem_limit_bytes=61 * 2**20),
+        cost_estimate=pl.CostEstimate(flops=17 * 10**9, bytes_accessed=50 * 10**6, transcendentals=2 * 10**6),
+    )(tokens, cot, w_in, w_out, w_up, w_down_t, kernel_t, gains, taps, twist, table)
+
+
+def backward_kernel(
+    num_z, length,
+    tok, cot, twist, small_v, table_h, win_h, wout_h, wup_h, gdown_h, kern_h, proj_h, normed_h, spec_h,
+    filt_h, conv_h, gated_h, resid_h, normed_two_h, gpre_h,
+    grad_in_o, gin_o, gout_o, gup_o, gdn_o, gains_o, gkern_o,
+    table_v, win_v, wout_v, wup_v, kern_v, proj_v, normed_v, spec_v, filt_v, conv_v,
+    gated_v, resid_v, normed_two_v, gpre_v,
+    gup_v, gdn_v, gkern_v,
+    core_in, core_out, core_up, core_dn, core_kern,
+    got_in, got_out, got_up, got_dn, got_kern,
+    sum_in, sum_out, sum_up, sum_dn, sum_kern,
+    ends_out, ends_up, ends_dn, ends_kern, swap_core, swap_y,
+    low_v, ggate_v, gch_v, gnorm_got, gain_v, gain_got,
+    send, recv, local,
+):
+    s = Spots(num_z)
+    z, x, y, c = s.z, s.x, s.y, s.c
+    wire, inner = Wire(send, recv, s), Local(local)
+    rows, width = tok.shape
+    group, span = width // 2, rows // 2
+    hidden = gpre_v.shape[1]
+    me = 2 * y + c
+    own_dn = [inner.start(gdown_h.at[i, :, :, c], gdn_v.at[i]) for i in range(2)]
+    loads = {}
+    for name, src, dst in (
+        ("gpre", gpre_h, gpre_v), ("wup", wup_h, wup_v), ("normed_two", normed_two_h, normed_two_v),
+        ("resid", resid_h, resid_v), ("wout", wout_h, wout_v), ("proj", proj_h, proj_v), ("conv", conv_h, conv_v),
+        ("gated", gated_h, gated_v), ("table", table_h, table_v), ("spec", spec_h, spec_v), ("filt", filt_h, filt_v),
+        ("kern", kern_h, kern_v), ("normed", normed_h, normed_v), ("win", win_h, win_v),
+    ):
+        loads[name] = inner.start(src, dst)
+
+    def need(*names):
+        for name in names:
+            inner.wait(loads[name])
+
+    s.meet()
+    block = width // (4 * num_z)
+    gout_v = wup_v.at[:, :, :, :, :, 0:group]
+    gin_v = win_v
+    down = Scatter(wire, s, gdn_v, "yzx", ORDER_DOWN, core_dn, got_dn, sum_dn, away=gdown_h)
+    up = Scatter(wire, s, gup_v, "yzx", ORDER_UP, core_up, got_up, sum_up)
+    out = Scatter(wire, s, gout_v, "yzx", ORDER_OUT, core_out, got_out, sum_out)
+    into = Scatter(wire, s, gin_v, "zx", ("zx",), core_in, got_in, sum_in)
+    taps_grad = Scatter(wire, s, gkern_v, "zx", ("zx",), core_kern, got_kern, sum_kern)
+    down.send_core()
+    gains = jnp.concatenate([small_v[k] for k in range(4)], axis=-1)
+
+    need("gpre", "wup", "resid")
+    half = hidden // 2
+    grad = sum(
+        dot_cols(gpre_v[:, h * half : (h + 1) * half], wup_v[h].reshape(width, half)) for h in range(2)
+    )
+    normal, scale = norm_parts(resid_v[...])
+    part, gain_two = norm_back(normal, scale, grad, gains[1:2])
+    resid_v[...] = cot[...].astype(F32) + part
+    low_v[...] = resid_v[...].astype(BF)
+
+    for copy in own_dn:
+        inner.wait(copy)
+    down.add_core()
+    down.send(0)
+
+    need("wout")
+    for h in range(2):
+        grad = sum(
+            dot_cols(
+                low_v[:, k * group : (k + 1) * group],
+                wout_v[k, h * num_z // 2 : (h + 1) * num_z // 2].reshape(group, group),
+            )
+            for k in range(2)
+        )
+        ggate_v[h] = grad.astype(BF)
+    chunk, home = spans(me * span, span), spans(c * span, span)
+    to_channels = [
+        wire.start(ggate_v.at[yy, spans(cc * span, span)], gch_v.at[chunk], peer)
+        for (yy, cc), peer in zip(s.group, s.mates)
+    ]
+    gch_v[chunk] = ggate_v[y, home]
+
+    need("normed_two")
+    wide = 256
+    per = hidden // 2 // wide
+
+    def up_grad(j, _):
+        grad = dot_rows(normed_two_v[...], gpre_v[:, spans(j * wide, wide, wide)]).astype(BF)
+        cols = spans((j % per) * wide, wide, wide)
+        gup_v[j // per, :, :, :, :, cols] = grad.reshape(num_z, 2, 2, block, wide)
+        return 0
+    lax.fori_loop(0, 2 * per, up_grad, 0)
+    up.send_core()
+    down.add(0)
+    down.send(1)
+
+    need("gated")
+    for h in range(2):
+        for k in range(2):
+            grad = dot_rows(gated_v[h], low_v[:, k * group : (k + 1) * group]).astype(BF)
+            gout_v[k, h * num_z // 2 : (h + 1) * num_z // 2] = grad.reshape(num_z // 2, 2, 2, block, group)
+    out.send_core()
+    up.add_core()
+    up.send(0)
+
+    need("proj", "conv", "table", "spec", "filt")
+    arrived(to_channels)
+
+    def gate(i, _):
+        at = spans(i * STEP, STEP, STEP)
+        grad = gch_v[at].astype(F32)
+        gch_v[at] = (grad * proj_v[2, at].astype(F32)).astype(BF)
+        proj_v[2, at] = (grad * conv_v[at].astype(F32)).astype(BF)
+        return 0
+    lax.fori_loop(0, length // STEP, gate, 0)
+
+    def turn(i, _):
+        real, imag = spans(i * STEP, STEP, STEP), spans(length + i * STEP, STEP, STEP)
+        re, im = dot(table_v[real], gch_v[...]), dot(table_v[imag], gch_v[...])
+        re_f, im_f = filt_v[real].astype(F32), filt_v[imag].astype(F32)
+        filt_v[real] = (re_f * re + im_f * im).astype(BF)
+        filt_v[imag] = (re_f * im - im_f * re).astype(BF)
+        re_s, im_s = spec_v[real].astype(F32), spec_v[imag].astype(F32)
+        re_k, im_k = re_s * re + im_s * im, re_s * im - im_s * re
+        cosine, sine = twist[real, 0:1], twist[real, 1:2]
+        spec_v[real] = (re_k * cosine - im_k * sine).astype(BF)
+        spec_v[imag] = (im_k * cosine + re_k * sine).astype(BF)
+        return 0
+    lax.fori_loop(0, length // STEP, turn, 0)
+    down.add(1)
+    down.send(2)
+    out.add_core()
+    out.send(0)
+
+    def back(i, _):
+        at, imag = spans(i * STEP, STEP, STEP), spans(length + i * STEP, STEP, STEP)
+        both = dot(table_v[at], filt_v[0:length]) + dot(table_v[imag], filt_v[length:])
+        grad = (both * (1.0 / length)).astype(BF).astype(F32)
+        value, first = proj_v[0, at].astype(F32), proj_v[1, at].astype(F32)
+        proj_v[0, at] = (grad * first).astype(BF)
+        proj_v[1, at] = (grad * value).astype(BF)
+        return 0
+    lax.fori_loop(0, length // STEP, back, 0)
+
+    need("normed", "win")
+
+    def normed_grad(j):
+        grad = sum(
+            dot_cols(proj_v[k, spans(j * span, span)], win_v[:, :, :, k].reshape(width, group)) for k in range(3)
+        )
+        return grad.astype(BF)
+
+    to_owner = []
+    for i, ((yy, cc), peer) in enumerate(zip(s.group, s.mates)):
+        place = gpre_v.at[0:span, i * width : (i + 1) * width]
+        place[...] = normed_grad(2 * yy + cc)
+        to_owner.append(wire.start(place, gnorm_got.at[i], peer))
+    mine = gpre_v.at[0:span, 3 * width : 4 * width]
+    mine[...] = normed_grad(me)
+
+    up.add(0)
+    up.send(1)
+    for k in range(3):
+        grad = dot_rows(normed_v[...], proj_v[k]).astype(BF)
+        gin_v[:, :, :, k] = grad.reshape(num_z, 2, 2, block, group)
+    into.send_core()
+    out.add(0)
+    out.send(1)
+    into.add_core()
+    into.send(0)
+
+    need("kern")
+    taps = jnp.concatenate([small_v[2 * y], small_v[2 * y + 1]], axis=-1)[2:3]
+    tile = 128
+    for j in range(group // tile):
+        cols = slice(j * tile, (j + 1) * tile)
+        both = dot(table_v[0:length], spec_v[0:length, cols]) + dot(table_v[length:], spec_v[length:, cols])
+        grad = kernel_back(kern_v[:, :, :, :, cols].reshape(length, tile).astype(F32), taps[:, cols],
+                           both * (1.0 / length))
+        gkern_v[:, :, :, :, cols] = grad.astype(BF).reshape(num_z, 2, 2, length // (4 * num_z), tile)
+    taps_grad.send_core()
+    up.add(1)
+    up.send(2)
+    into.add(0)
+    into.send(1)
+    taps_grad.add_core()
+    taps_grad.send(0)
+    out.add(1)
+    out.send(2)
+    down.add(2)
+    down.trade(ends_dn)
+
+    arrived(to_owner)
+    across, diagonal, beside = (gnorm_got[i].astype(F32) for i in range(3))
+    here = mine[...].astype(F32) + across
+    there = beside + diagonal
+    first_rows, second_rows = jnp.where(c == 0, here, there), jnp.where(c == 0, there, here)
+    grad = jnp.concatenate([first_rows, second_rows], axis=0)
+    normal, scale = norm_parts(tok[...].astype(F32))
+    part, gain_one = norm_back(normal, scale, grad, gains[0:1])
+    low_v[...] = (resid_v[...] + part).astype(BF)
+    inner.start(low_v, grad_in_o)
+
+    gain_v[0] = jnp.concatenate([gain_one, gain_two, jnp.zeros((6, width), F32)], axis=0)
+    got = [wire.start(gain_v.at[0], gain_got.at[k], peer) for k, peer in enumerate(s.mates)]
+    taps_grad.add(0)
+    taps_grad.send(1)
+    arrived(got)
+    gain_v[1] = gain_v[0] + gain_got[0] + gain_got[1] + gain_got[2]
+    got = [wire.start(gain_v.at[1], gain_got.at[3], s.along["x"][0])]
+    up.add(2)
+    up.trade(ends_up)
+    out.add(2)
+    out.trade(ends_out)
+    arrived(got)
+    gain_v[2] = gain_v[1] + gain_got[3]
+    got = [wire.start(gain_v.at[2], gain_got.at[3 + k], peer) for k, peer in zip(range(1, num_z), s.along["z"])]
+
+    into.add(1)
+    first, second, third = sum_in[y], sum_in[y + 1], sum_in[(y + 2) % 3]
+    swap_core[0, 0], swap_core[0, 1] = first.astype(BF), second.astype(BF)
+    swap_y[0] = third.astype(BF)
+    swaps = [wire.start(swap_y.at[0], swap_y.at[1], s.mates[0]), wire.start(swap_y.at[0], swap_y.at[2], s.mates[1]),
+             wire.start(swap_core.at[0], swap_core.at[1], s.core)]
+    taps_grad.add(1)
+    taps_grad.trade(ends_kern)
+    down.finish(gdn_o, turned=True)
+    up.finish(gup_o)
+    out.finish(gout_o)
+    arrived(got)
+    total = gain_v[2]
+    for k in range(1, num_z):
+        total = total + gain_got[3 + k]
+    part = width // 4
+    mine = total[:, 0:part]
+    for k in range(1, 4):
+        mine = jnp.where(me == k, total[:, k * part : (k + 1) * part], mine)
+    gains_o[...] = mine[0:2]
+    taps_grad.finish(gkern_o, turned=True)
+    arrived(swaps)
+    cut = group // 2
+    for row, near, far in ((c, swap_core.at[0], swap_y.at[1]), (1 - c, swap_core.at[1], swap_y.at[2])):
+        far = far[...].astype(F32)
+        left = jnp.concatenate([near[0].astype(F32), far[:, 0:cut]], axis=-1)
+        right = jnp.concatenate([far[:, cut:], near[1].astype(F32)], axis=-1)
+        gin_o[spans(row * block, block)] = jnp.where(c == 0, left, right)
+    wire.drain()
+    inner.drain()
+
+
+def backward(num_z, length, tokens, cot, twist, small_f, table, full):
+    rows, width = tokens.shape
+    group = width // 2
+    sds = jax.ShapeDtypeStruct
+    win, wout, wup, gdown, kern, proj, normed, spec, filt, conv, gated, resid, normed_two, gpre = full
+    like = lambda a: vm(a.shape, a.dtype)
+    weights = (win, wout, wup, gdown, kern)
+    blocks = [a.shape[-2:] for a in weights]
+    blocks[0] = win.shape[-3:]
+    counts = [7, 15, 15, 15, 7]
+    outs = [sds((rows, width), BF), sds((2 * win.shape[-2], width * 3 // 4), F32)]
+    outs += [sds((2 * w.shape[-2], w.shape[-1] // 2), F32) for w in (wout, wup)]
+    outs += [sds((gdown.shape[-1] // 2, 2 * gdown.shape[-2]), F32), sds((2, width // 4), F32)]
+    outs += [sds((kern.shape[-1] // 2, 2 * kern.shape[-2]), F32)]
+    scratch = [like(a) for a in (table, win, wout, wup, kern, proj, normed, spec, filt, conv, gated, resid,
+                                 normed_two, gpre)]
+    scratch += [like(wup), vm(gdown.shape[:3] + gdown.shape[4:]), like(kern)]
+    scratch += [vm(win.shape[:2] + win.shape[3:])] + [vm(w.shape[:3] + w.shape[4:]) for w in (wout, wup, gdown)]
+    scratch += [vm(kern.shape[:2] + kern.shape[3:])]
+    scratch += [vm((n,) + b) for n, b in zip(counts, blocks)] + [vm(b, F32) for b in blocks]
+    scratch += [vm((3, b[0], b[1] // 2), F32) for b in blocks[1:]]
+    scratch += [vm((2, 2) + blocks[0][1:]), vm((3,) + blocks[0][1:])]
+    scratch += [vm((rows, width)), vm((2, rows, group)), vm((length, group)), vm((3, rows // 2, width)),
+                vm((3, 8, width), F32), vm((3 + num_z, 8, width), F32)]
+    scratch += [pltpu.SemaphoreType.DMA((160,)), pltpu.SemaphoreType.DMA((160,)), pltpu.SemaphoreType.DMA((40,))]
+    return pl.pallas_call(
+        partial(backward_kernel, num_z, length),
+        out_shape=outs,
+        in_specs=[VMEM_SPEC] * 4 + [HBM_SPEC] * 15,
+        out_specs=[HBM_SPEC] + [VMEM_SPEC] * 6,
+        scratch_shapes=scratch,
+        compiler_params=pltpu.CompilerParams(collective_id=1, has_side_effects=True, vmem_limit_bytes=63 * 2**20),
+        cost_estimate=pl.CostEstimate(flops=17 * 10**9, bytes_accessed=50 * 10**6, transcendentals=2 * 10**6),
+    )(tokens, cot, twist, small_f, table, *full)
+
+
+def publish(*arrays):
+    def copy_all(*refs):
+        for src, dst in zip(refs[: len(arrays)], refs[len(arrays) :]):
+            dst[...] = src[...]
+
+    return pl.pallas_call(
+        copy_all,
+        out_shape=[jax.ShapeDtypeStruct(a.shape, a.dtype) for a in arrays],
+        in_specs=[VMEM_SPEC] * len(arrays),
+        out_specs=[VMEM_SPEC] * len(arrays),
+    )(*arrays)
+
+
+def fits(num_dp, num_seq, tokens, w_in, w_out, w_up, w_down, kernel):
+    if num_seq != 4 or num_dp % 4 or kernel.shape[0] * num_dp > 1024 or kernel.shape[0] * num_dp % 512:
+        return False
+    blocks = (w_in, w_out, w_up, w_down, kernel)
+    return all(b.shape[0] % 32 == 0 and b.shape[1] * 2 % 128 == 0 for b in blocks) and tokens.shape[0] == 2
+
+
+def body(num_dp, num_seq, tokens_in, w_in, w_out, w_up, w_down, norm_gains, kernel, taps, cotangent):
+    if not fits(num_dp, num_seq, tokens_in, w_in, w_out, w_up, w_down, kernel):
+        return general_body(tokens_in, w_in, w_out, w_up, w_down, norm_gains, kernel, taps, cotangent)
+    width = tokens_in.shape[-1]
+    length = kernel.shape[0] * num_dp
+    num_z = num_dp // 2
+    table, twist = jnp.asarray(transform_table(length)), jnp.asarray(twist_table(length))
+    tokens, cot = tokens_in.reshape(-1, width), cotangent.reshape(-1, width)
+    out, win, wout, wup, gdown, kern, small, *saved = forward(
+        num_z, length, tokens, cot, w_in, w_out, w_up, w_down.T, kernel.T, norm_gains, taps[None], twist, table)
+    results = backward(num_z, length, tokens, cot, twist, small, table, [win, wout, wup, gdown, kern, *saved])
+    out, grad_in, gin, gout, gup, gdn, gains, gkern = publish(out, *results)
+    return (out.reshape(tokens_in.shape), grad_in.reshape(tokens_in.shape), gin, gout, gup, gdn.T, gains, gkern.T)
+
+
 def solution(mesh):
     return jax.shard_map(
-        body,
+        partial(body, mesh.shape["dp"], mesh.shape["seq"]),
         mesh=mesh,
         in_specs=(
             P("dp", "seq", None),

time: 884 us -> 237 us (0.27)
  waiting for transfers between devices: 477 us -> 0 us
  Pallas kernels: 0 us -> 234 us
  matrix products: 161 us -> 0 us
  blocking collectives: 124 us -> 0 us
  local copies, waits for them, and re-layouts: 72.7 us -> 0 us
  other arithmetic: 17.6 us -> 0 us
  between operations: 15.2 us -> 0.7 us
  starting transfers between devices: 9.34 us -> 0 us
    reduce_scatter x5 -> x0, waiting for transfers between devices: 254 us -> none  [the longest x1 96.5 us: body(): lax.psum_scatter(grad_up.astype(jnp.bfloat16), 'dp', scatter_dimension=0,...]
    pallas_call x0 -> x3, Pallas kernels: none -> 234 us  [the longest x1 118 us: backward(): pl.pallas_call(partial(backward_kernel, num_z, length), out_shape=outs, i...]
    dot_general x48 -> x0, matrix products: 161 us -> none  [the longest x24 70.7 us: mix_last(): return jnp.einsum('bckn,nm->bckm', field, table, precision=HIGHEST)]
    unnamed x19 -> x0, waiting for transfers between devices: 120 us -> none
    all_gather x4 -> x0, waiting for transfers between devices: 88.8 us -> none  [the longest x1 72.3 us: body(): lax.all_gather(w_up_rows, 'dp', axis=0, tiled=True)]
    all_gather x6 -> x0, blocking collectives: 65.9 us -> none  [the longest x1 29.7 us: body(): lax.all_gather(kernel, 'dp', axis=0, tiled=True)]
    all_to_all x2 -> x0, blocking collectives: 36.2 us -> none  [to_tokens(): return lax.all_to_all(field, 'seq', split_axis=1, concat_axis=2, tiled=True)]
    unnamed x122 -> x0, local copies, waits for them, and re-layouts: 28.4 us -> none
  transfers between devices with their start and end apart: 16 -> 0, of which waited for: 14 -> 0; matrix products, arithmetic and copies ran while one was open for 24% -> 0% of each run, Pallas kernels for 0% -> 0%
where the time goes in v3:
time: 237 us; the launch traced here: 235 us
  Pallas kernels  234 us (99%)
    pallas_call x1, Pallas kernels, backward(): pl.pallas_call(partial(backward_kernel, num_z, length), out_shape=outs, i...  118 us
    pallas_call x1, Pallas kernels, forward(): pl.pallas_call(partial(forward_kernel, num_z, length), out_shape=outs, in...  113 us

profile of v3, /device:TPU:0, one launch (start us, length us, event | category | flops | bytes accessed | tf_op | source)
XLA Modules:
  0.0 235.0 jit_solution(6573023221550595725)
XLA Ops:
  0.6 113.0 %shard_map.170 = (bf16[512,768]{1,0:T(8,128)(2,1)}, bf16[4,2,2,3,48,384]{5,4,3,2,1,0:T(8,128)(2,1)}, bf16[2,4,2,2,48,384]{5,4,3,2,1,0:T(8,128)(2,1)}, bf16[2,4,2...) custom-call(bf16[512,768]{1,0:T(8,128)(2,1)} %bitcast.9, ...), custom_call_target="tpu_custom_call" | custom-call | flops 16999999488 | bytes 50000000 | tf_op jit(solution)/shard_map/pallas_call | solution.py:816
  113.6 118.1 %shard_map.171 = (bf16[512,768]{1,0:T(8,128)(2,1)}, f32[96,576]{1,0:T(8,128)}, f32[96,192]{1,0:T(8,128)}, f32[96,768]{1,0:T(8,128)}, f32[192,384]{1,0:T(8,128)}, /*index=5*/f32[2,192]{1,0:T(2,128)}, f32[192,128]{1,0:T(8,128)}) custom-call(bf16[512,768]{1,0:T(8,128)(2,1)} %bitcast.10, bf16[512,768]{1,0:T(8,128)(2,1)} %bitcast.12, ...), custom_call_target="tpu_custom_call" | custom-call | flops 16999999488 | bytes 50000000 | tf_op jit(solution)/shard_map/pallas_call | solution.py:1100
  231.8 3.2 %shard_map.172 = (bf16[512,768]{1,0:T(8,128)(2,1)}, bf16[512,768]{1,0:T(8,128)(2,1)}, f32[96,576]{1,0:T(8,128)}, f32[96,192]{1,0:T(8,128)}, f32[96,768]{1,0:T(8,...) custom-call(bf16[512,768]{1,0:T(8,128)(2,1)} %get-tuple-element.39.refs_0_, ...), custom_call_target="tpu_custom_call" | custom-call | tf_op jit(solution)/shard_map/pallas_call | solution.py:1116

commit v4 on v3

--- a/solution.py
+++ b/solution.py
@@ -335,13 +335,12 @@
 
 
 class Gather:
-    def __init__(self, wire, spots, full, axes, *orders, part=None):
+    def __init__(self, wire, spots, full, axes, *orders, part=()):
         self.wire, self.s, self.full, self.axes, self.part = wire, spots, full, axes, part
         self.orders, self.last = both_cores(orders), {}
 
     def view(self, have):
-        index = block_index(self.s, self.axes, have, self.s.c)
-        return self.full.at[index if self.part is None else index + (self.part,)]
+        return self.full.at[block_index(self.s, self.axes, have, self.s.c) + self.part]
 
     def settle(self):
         for core, copies in self.last.items():
@@ -367,22 +366,39 @@
         self.settle()
 
 
+class Rounds:
+    LAG = 2
+
+    def __init__(self, gathers):
+        self.gathers, self.now = gathers, 0
+
+    def run(self, count=1):
+        for _ in range(count):
+            for step in reversed(range(4)):
+                k = self.now - step * self.LAG
+                if 0 <= k < len(self.gathers) and step <= len(self.gathers[k].orders[0][1]):
+                    self.gathers[k].step(step)
+            self.now += 1
+
+
 class Scatter:
-    def __init__(self, wire, spots, total, axes, orders, from_core, got, result, away=None):
-        self.wire, self.s, self.total, self.axes = wire, spots, total, axes
+    def __init__(self, wire, spots, total, axes, orders, from_core, got, result, away=None, part=()):
+        self.wire, self.s, self.total, self.axes, self.part = wire, spots, total, axes, part
         self.orders = [(core, order[::-1]) for core, order in both_cores(orders)]
         self.from_core, self.got, self.result, self.away = from_core, got, result, away
         self.last = {}
 
     def mine(self, wide, at=None):
-        return self.total.at[block_index(self.s, self.axes, wide, None if self.away is not None else self.s.c, at)]
+        core = None if self.away is not None else self.s.c
+        return self.total.at[block_index(self.s, self.axes, wide, core, at) + self.part]
 
     def send_core(self):
         s = self.s
         source = self.total if self.away is None else self.away
-        rest = (slice(None),) * (len(self.axes) - 1) + (1 - s.c,)
+        whole = (slice(None),) * (len(self.axes) - 1)
         self.last = [
-            self.wire.start(source.at[(i,) + rest], self.from_core.at[i], s.core)
+            self.wire.start(source.at[(i,) + whole + (1 - s.c,) + self.part],
+                            self.from_core.at[(i,) + whole + self.part], s.core)
             for i in range(self.from_core.shape[0])
         ]
 
@@ -397,7 +413,7 @@
             for axis in reversed(self.axes):
                 at[axis], left = left % s.size[axis], left // s.size[axis]
             into = self.mine("", at)
-            term = self.from_core[tuple(at[axis] for axis in self.axes)]
+            term = self.from_core[tuple(at[axis] for axis in self.axes) + self.part]
             into[...] = (into[...].astype(F32) + term.astype(F32)).astype(BF)
             return 0
         lax.fori_loop(0, count, one, 0)
@@ -413,7 +429,7 @@
         return order[n], wide, count, begin
 
     def slots(self, start, count):
-        return self.got.at[start] if count is None else self.got.at[start : start + count]
+        return self.got.at[(start if count is None else slice(start, start + count),) + self.part]
 
     def send(self, n):
         s = self.s
@@ -447,8 +463,8 @@
                 if n == len(order) - 1:
                     total = self.mine("")[...].astype(F32)
                     for j in range(peers):
-                        total = total + self.got[begin + j].astype(F32)
-                    self.result[...] = total
+                        total = total + self.got[(begin + j,) + self.part].astype(F32)
+                    self.result[self.part or ...] = total
                     return
 
                 def one(i, _):
@@ -458,23 +474,39 @@
                     into = self.mine("", at)
                     total = into[...].astype(F32)
                     for j in range(peers):
-                        total = total + self.got[begin + j * count + i].astype(F32)
+                        total = total + self.got[(begin + j * count + i,) + self.part].astype(F32)
                     into[...] = total.astype(BF)
                     return 0
                 lax.fori_loop(0, count, one, 0)
 
-    def trade(self, ends):
-        part = ends.shape[-1]
+
+    def go(self, n):
+        if n == 0:
+            self.add_core()
+        else:
+            self.add(n - 1)
+        if n < len(self.orders[0][1]):
+            self.send(n)
+
+
+class Trade:
+    def __init__(self, wire, spots, result, ends):
+        self.s, self.ends = spots, ends
+        width = ends.shape[-1]
         for core in range(2):
-            ends[core] = self.result[:, core * part : (core + 1) * part]
-        self.last = [self.wire.start(ends.at[1 - self.s.c], ends.at[2], self.s.core)]
-        self.ends = ends
+            ends[core] = result[:, core * width : (core + 1) * width]
+        self.copy = wire.start(ends.at[1 - spots.c], ends.at[2], spots.core)
 
     def finish(self, out, turned=False):
-        arrived(self.last)
+        self.copy.wait_recv()
         c, own, other = self.s.c, self.ends[self.s.c], self.ends[2]
         both = jnp.concatenate([jnp.where(c == 0, own, other), jnp.where(c == 0, other, own)], axis=0)
         out[...] = both.T if turned else both
+
+
+def row_parts(rows):
+    size = rows // PARTS
+    return [(slice(i * size, (i + 1) * size),) for i in range(PARTS)]
 
 
 def norm_parts(values):
@@ -556,7 +588,8 @@
 
 ORDER_OUT = ("zxy", "zyx")
 ORDER_UP = ("zxy", "zyx")
-ORDER_DOWN = ("zyx", "yzx")
+ORDER_DOWN = ("zxy", "yzx")
+PARTS = 3
 STEP = 256
 
 
@@ -601,11 +634,13 @@
         half = src.shape[0] // 2
         pre[c] = src[spans(c * half, half)]
 
-    g_in = [Gather(wire, s, win_v, "zx", "zx", part=k) for k in range(3)]
+    g_in = [Gather(wire, s, win_v, "zx", "zx", part=(k,)) for k in range(3)]
     g_kern = Gather(wire, s, kern_v, "zx", "zx")
     g_out = Gather(wire, s, wout_v, "yzx", *ORDER_OUT)
-    g_up = Gather(wire, s, wup_v, "yzx", *ORDER_UP)
-    g_down = Gather(wire, s, wdown_v, "yzx", *ORDER_DOWN)
+    g_up = [Gather(wire, s, wup_v, "yzx", *ORDER_UP, part=part) for part in row_parts(wup_v.shape[-2])]
+    g_down = [Gather(wire, s, wdown_v, "yzx", *ORDER_DOWN, part=part) for part in row_parts(wdown_v.shape[-2])]
+
+    rounds = Rounds([*g_in, g_kern, g_out, *g_up, *g_down])
 
     def join(i, full):
         traded[i].wait_recv()
@@ -617,7 +652,8 @@
     for k in range(3):
         left, right = (whole[:, (2 * k + h) * group : (2 * k + h + 1) * group] for h in range(2))
         win_v[z, x, c, k] = jnp.where(y == 0, left, right)
-        g_in[k].step(0)
+        if k < 2:
+            rounds.run()
 
     arrived(smalls)
     gains = jnp.concatenate([small_v[k] for k in range(4)], axis=-1)
@@ -630,23 +666,32 @@
     ]
     normed_v[chunk] = normed_own[spans(c * span, span)]
     join(0, kern_v)
-    g_kern.step(0)
     join(1, wout_v)
     join(2, wup_v)
     join(3, wdown_v)
-
-    g_in[0].step(1)
-    g_in[1].step(1)
-    g_out.step(0)
-    g_in[2].step(1)
-    g_up.step(0)
-    g_kern.step(1)
-    g_in[0].step(2)
-    g_in[1].step(2)
-    g_down.step(0)
-    g_in[2].step(2)
-    g_kern.step(2)
-    g_out.step(1)
+    rounds.run(5)
+
+
+    arrived(to_group)
+    g_in[0].done()
+    g_in[1].done()
+
+    def project(k, at):
+        return dot(normed_v[at], win_v[:, :, :, k].reshape(width, group))
+
+    tall = length // 2
+    for i in range(2):
+        at = slice(i * tall, (i + 1) * tall)
+        value, gate = project(0, at), project(1, at)
+        proj_v[0, at] = value.astype(BF)
+        proj_v[1, at] = gate.astype(BF)
+        sig_v[at] = (value * gate).astype(BF)
+    g_in[2].done()
+    rounds.run()
+    for i in range(2):
+        at = slice(i * tall, (i + 1) * tall)
+        proj_v[2, at] = project(2, at).astype(BF)
+    rounds.run()
 
     g_kern.done()
     taps = jnp.concatenate([small_v[2 * y], small_v[2 * y + 1]], axis=-1)[2:3]
@@ -666,28 +711,8 @@
         return 0
     lax.fori_loop(0, length // STEP, spectrum, 0)
 
-    g_up.step(1)
-    g_out.step(2)
-    arrived(to_group)
-    g_in[0].done()
-    g_in[1].done()
-
-    def project(k, at):
-        return dot(normed_v[at], win_v[:, :, :, k].reshape(width, group))
-
-    tall = length // 2
-    for i in range(2):
-        at = slice(i * tall, (i + 1) * tall)
-        value, gate = project(0, at), project(1, at)
-        proj_v[0, at] = value.astype(BF)
-        proj_v[1, at] = gate.astype(BF)
-        sig_v[at] = (value * gate).astype(BF)
-    g_up.step(2)
-    g_down.step(1)
-    g_in[2].done()
-    for i in range(2):
-        at = slice(i * tall, (i + 1) * tall)
-        proj_v[2, at] = project(2, at).astype(BF)
+
+    rounds.run()
 
     def convolve(i, _):
         real, imag = spans(i * STEP, STEP, STEP), spans(length + i * STEP, STEP, STEP)
@@ -700,6 +725,8 @@
         return 0
     lax.fori_loop(0, length // STEP, convolve, 0)
 
+    rounds.run()
+
     def back(i, _):
         at, imag = spans(i * STEP, STEP, STEP), spans(length + i * STEP, STEP, STEP)
         both = dot(table_v[at], turned_v[0:length]) + dot(table_v[imag], turned_v[length:])
@@ -715,13 +742,12 @@
         for (yy, cc), peer in zip(s.group, s.mates)
     ]
     gated_v[y, home] = gated_ch[chunk]
-    g_out.step(3)
-    g_down.step(2)
-    g_up.step(3)
     for src, dst in ((win_v, win_o), (kern_v, kern_o), (small_v, small_o), (proj_v, proj_o),
                      (normed_v, normed_o), (spec_v, spec_o), (filt_v, filt_o), (conv_v, conv_o)):
         inner.start(src, dst)
+    rounds.run()
     g_out.done()
+    rounds.run()
     arrived(to_tokens)
 
     for k in range(2):
@@ -734,7 +760,9 @@
     normed_two_v[...] = (normed_two * gains[1:2]).astype(BF)
     for src, dst in ((wout_v, wout_o), (gated_v, gated_o), (resid_v, resid_o), (normed_two_v, normed_two_o)):
         inner.start(src, dst)
-    g_up.done()
+    rounds.run(2)
+    for g in g_up:
+        g.done()
 
     wide = 256
     per = hidden // 2 // wide
@@ -746,9 +774,12 @@
         act_v[:, at] = act.astype(BF)
         slope_v[:, at] = slope.astype(BF)
         return 0
-    lax.fori_loop(0, 2 * per, feed, 0)
+    lax.fori_loop(0, per, feed, 0)
+    rounds.run()
+    lax.fori_loop(per, 2 * per, feed, 0)
     inner.start(wup_v, wup_o)
-    g_down.step(3)
+
+    rounds.run()
 
     deep = hidden // (2 * num_z)
 
@@ -759,7 +790,9 @@
         return 0
     lax.fori_loop(0, 2 * num_z, down_grad, 0)
     inner.start(gdown_v, gdown_o)
-    g_down.done()
+    rounds.run()
+    for g in g_down:
+        g.done()
 
     def pre_grad(i, _):
         at = spans(i * deep, deep, deep)
@@ -864,12 +897,15 @@
     block = width // (4 * num_z)
     gout_v = wup_v.at[:, :, :, :, :, 0:group]
     gin_v = win_v
-    down = Scatter(wire, s, gdn_v, "yzx", ORDER_DOWN, core_dn, got_dn, sum_dn, away=gdown_h)
-    up = Scatter(wire, s, gup_v, "yzx", ORDER_UP, core_up, got_up, sum_up)
+    down = [Scatter(wire, s, gdn_v, "yzx", ORDER_DOWN, core_dn, got_dn, sum_dn, away=gdown_h, part=part)
+            for part in row_parts(gdn_v.shape[-2])]
+    up = [Scatter(wire, s, gup_v, "yzx", ORDER_UP, core_up, got_up, sum_up, part=part)
+          for part in row_parts(gup_v.shape[-2])]
     out = Scatter(wire, s, gout_v, "yzx", ORDER_OUT, core_out, got_out, sum_out)
-    into = Scatter(wire, s, gin_v, "zx", ("zx",), core_in, got_in, sum_in)
+    into = [Scatter(wire, s, gin_v, "zx", ("zx",), core_in, got_in, sum_in, part=(k,)) for k in range(3)]
     taps_grad = Scatter(wire, s, gkern_v, "zx", ("zx",), core_kern, got_kern, sum_kern)
-    down.send_core()
+    for k in range(3):
+        down[k].send_core()
     gains = jnp.concatenate([small_v[k] for k in range(4)], axis=-1)
 
     need("gpre", "wup", "resid")
@@ -884,8 +920,8 @@
 
     for copy in own_dn:
         inner.wait(copy)
-    down.add_core()
-    down.send(0)
+    down[0].go(0)
+    down[1].go(0)
 
     need("wout")
     for h in range(2):
@@ -904,6 +940,8 @@
     ]
     gch_v[chunk] = ggate_v[y, home]
 
+    down[2].go(0)
+
     need("normed_two")
     wide = 256
     per = hidden // 2 // wide
@@ -914,9 +952,11 @@
         gup_v[j // per, :, :, :, :, cols] = grad.reshape(num_z, 2, 2, block, wide)
         return 0
     lax.fori_loop(0, 2 * per, up_grad, 0)
-    up.send_core()
-    down.add(0)
-    down.send(1)
+    for k in range(3):
+        up[k].send_core()
+    down[0].go(1)
+    down[1].go(1)
+    up[0].go(0)
 
     need("gated")
     for h in range(2):
@@ -924,8 +964,9 @@
             grad = dot_rows(gated_v[h], low_v[:, k * group : (k + 1) * group]).astype(BF)
             gout_v[k, h * num_z // 2 : (h + 1) * num_z // 2] = grad.reshape(num_z // 2, 2, 2, block, group)
     out.send_core()
-    up.add_core()
-    up.send(0)
+    down[2].go(1)
+    down[0].go(2)
+    up[1].go(0)
 
     need("proj", "conv", "table", "spec", "filt")
     arrived(to_channels)
@@ -951,10 +992,10 @@
         spec_v[imag] = (im_k * cosine + re_k * sine).astype(BF)
         return 0
     lax.fori_loop(0, length // STEP, turn, 0)
-    down.add(1)
-    down.send(2)
-    out.add_core()
-    out.send(0)
+    down[1].go(2)
+    up[2].go(0)
+    up[0].go(1)
+    out.go(0)
 
     def back(i, _):
         at, imag = spans(i * STEP, STEP, STEP), spans(length + i * STEP, STEP, STEP)
@@ -982,16 +1023,17 @@
     mine = gpre_v.at[0:span, 3 * width : 4 * width]
     mine[...] = normed_grad(me)
 
-    up.add(0)
-    up.send(1)
+    down[2].go(2)
+    up[1].go(1)
     for k in range(3):
         grad = dot_rows(normed_v[...], proj_v[k]).astype(BF)
         gin_v[:, :, :, k] = grad.reshape(num_z, 2, 2, block, group)
-    into.send_core()
-    out.add(0)
-    out.send(1)
-    into.add_core()
-    into.send(0)
+        into[k].send_core()
+    up[0].go(2)
+    for k in range(3):
+        into[k].go(0)
+    up[2].go(1)
+    out.go(1)
 
     need("kern")
     taps = jnp.concatenate([small_v[2 * y], small_v[2 * y + 1]], axis=-1)[2:3]
@@ -1003,16 +1045,16 @@
                            both * (1.0 / length))
         gkern_v[:, :, :, :, cols] = grad.astype(BF).reshape(num_z, 2, 2, length // (4 * num_z), tile)
     taps_grad.send_core()
-    up.add(1)
-    up.send(2)
-    into.add(0)
-    into.send(1)
-    taps_grad.add_core()
-    taps_grad.send(0)
-    out.add(1)
-    out.send(2)
-    down.add(2)
-    down.trade(ends_dn)
+    up[1].go(2)
+    for k in range(3):
+        into[k].go(1)
+    taps_grad.go(0)
+    up[2].go(2)
+    out.go(2)
+    for k in range(3):
+        down[k].go(3)
+    trade_dn = Trade(wire, s, sum_dn, ends_dn)
+    taps_grad.go(1)
 
     arrived(to_owner)
     across, diagonal, beside = (gnorm_got[i].astype(F32) for i in range(3))
@@ -1027,30 +1069,30 @@
 
     gain_v[0] = jnp.concatenate([gain_one, gain_two, jnp.zeros((6, width), F32)], axis=0)
     got = [wire.start(gain_v.at[0], gain_got.at[k], peer) for k, peer in enumerate(s.mates)]
-    taps_grad.add(0)
-    taps_grad.send(1)
     arrived(got)
     gain_v[1] = gain_v[0] + gain_got[0] + gain_got[1] + gain_got[2]
     got = [wire.start(gain_v.at[1], gain_got.at[3], s.along["x"][0])]
-    up.add(2)
-    up.trade(ends_up)
-    out.add(2)
-    out.trade(ends_out)
+    for k in range(3):
+        up[k].go(3)
+    trade_up = Trade(wire, s, sum_up, ends_up)
+    out.go(3)
+    trade_out = Trade(wire, s, sum_out, ends_out)
     arrived(got)
     gain_v[2] = gain_v[1] + gain_got[3]
     got = [wire.start(gain_v.at[2], gain_got.at[3 + k], peer) for k, peer in zip(range(1, num_z), s.along["z"])]
 
-    into.add(1)
+    for k in range(3):
+        into[k].go(2)
     first, second, third = sum_in[y], sum_in[y + 1], sum_in[(y + 2) % 3]
     swap_core[0, 0], swap_core[0, 1] = first.astype(BF), second.astype(BF)
     swap_y[0] = third.astype(BF)
     swaps = [wire.start(swap_y.at[0], swap_y.at[1], s.mates[0]), wire.start(swap_y.at[0], swap_y.at[2], s.mates[1]),
              wire.start(swap_core.at[0], swap_core.at[1], s.core)]
-    taps_grad.add(1)
-    taps_grad.trade(ends_kern)
-    down.finish(gdn_o, turned=True)
-    up.finish(gup_o)
-    out.finish(gout_o)
+    taps_grad.go(2)
+    trade_kern = Trade(wire, s, sum_kern, ends_kern)
+    trade_dn.finish(gdn_o, turned=True)
+    trade_up.finish(gup_o)
+    trade_out.finish(gout_o)
     arrived(got)
     total = gain_v[2]
     for k in range(1, num_z):
@@ -1060,7 +1102,7 @@
     for k in range(1, 4):
         mine = jnp.where(me == k, total[:, k * part : (k + 1) * part], mine)
     gains_o[...] = mine[0:2]
-    taps_grad.finish(gkern_o, turned=True)
+    trade_kern.finish(gkern_o, turned=True)
     arrived(swaps)
     cut = group // 2
     for row, near, far in ((c, swap_core.at[0], swap_y.at[1]), (1 - c, swap_core.at[1], swap_y.at[2])):

time: 237 us -> 204 us (0.86)
  Pallas kernels: 234 us -> 203 us
    pallas_call x1, Pallas kernels: 118 us -> 102 us  [backward(): pl.pallas_call(partial(backward_kernel, num_z, length), out_shape=outs, i...]
    pallas_call x1, Pallas kernels: 113 us -> 97.5 us  [forward(): pl.pallas_call(partial(forward_kernel, num_z, length), out_shape=outs, in...]
where the time goes in v4:
time: 204 us; the launch traced here: 203 us
  Pallas kernels  203 us (100%)
    pallas_call x1, Pallas kernels, backward(): pl.pallas_call(partial(backward_kernel, num_z, length), out_shape=outs, i...  102 us
    pallas_call x1, Pallas kernels, forward(): pl.pallas_call(partial(forward_kernel, num_z, length), out_shape=outs, in...  97.5 us

profile of v4, /device:TPU:0, one launch (start us, length us, event | category | flops | bytes accessed | tf_op | source)
XLA Modules:
  0.0 203.3 jit_solution(16117901996406015280)
XLA Ops:
  0.6 97.5 %shard_map.170 = (bf16[512,768]{1,0:T(8,128)(2,1)}, bf16[4,2,2,3,48,384]{5,4,3,2,1,0:T(8,128)(2,1)}, bf16[2,4,2,2,48,384]{5,4,3,2,1,0:T(8,128)(2,1)}, bf16[2,4,2...) custom-call(bf16[512,768]{1,0:T(8,128)(2,1)} %bitcast.9, ...), custom_call_target="tpu_custom_call" | custom-call | flops 16999999488 | bytes 50000000 | tf_op jit(solution)/shard_map/pallas_call | solution.py:849
  98.2 101.9 %shard_map.171 = (bf16[512,768]{1,0:T(8,128)(2,1)}, f32[96,576]{1,0:T(8,128)}, f32[96,192]{1,0:T(8,128)}, f32[96,768]{1,0:T(8,128)}, f32[192,384]{1,0:T(8,128)}, /*index=5*/f32[2,192]{1,0:T(2,128)}, f32[192,128]{1,0:T(8,128)}) custom-call(bf16[512,768]{1,0:T(8,128)(2,1)} %bitcast.10, bf16[512,768]{1,0:T(8,128)(2,1)} %bitcast.12, ...), custom_call_target="tpu_custom_call" | custom-call | flops 16999999488 | bytes 50000000 | tf_op jit(solution)/shard_map/pallas_call | solution.py:1142
  200.1 3.2 %shard_map.172 = (bf16[512,768]{1,0:T(8,128)(2,1)}, bf16[512,768]{1,0:T(8,128)(2,1)}, f32[96,576]{1,0:T(8,128)}, f32[96,192]{1,0:T(8,128)}, f32[96,768]{1,0:T(8,...) custom-call(bf16[512,768]{1,0:T(8,128)(2,1)} %get-tuple-element.39.refs_0_, ...), custom_call_target="tpu_custom_call" | custom-call | tf_op jit(solution)/shard_map/pallas_call | solution.py:1158

commit v5 on v4

--- a/solution.py
+++ b/solution.py
@@ -237,6 +237,7 @@
 class Remote:
     def __init__(self, wire, slot, src, dst, peer):
         self.wire, self.slot, self.src, self.dst, self.peer = wire, slot, src, dst, peer
+        self.sent = False
 
     def named(self):
         return pltpu.make_async_remote_copy(
@@ -252,20 +253,24 @@
     def __init__(self, send, recv, spots):
         self.send, self.recv, self.s, self.made = send, recv, spots, []
 
-    def start(self, src, dst, peer, core=None):
+    def start(self, src, dst, peer, core=None, buffer=None):
         src, dst = (end if callable(end) else partial(lambda ref: ref, end) for end in (src, dst))
         copy = Remote(self, len(self.made), src, dst, peer)
+        copy.buffer = buffer
         copy.named().start()
         self.made.append((core, copy))
         return copy
 
-    def drain(self):
+    def drain(self, src=None):
+        made = [(core, copy) for core, copy in self.made if not copy.sent and src in (None, copy.buffer)]
         for which in (None, 0, 1):
             @self.s.on(which)
             def _():
-                for core, copy in self.made:
+                for core, copy in made:
                     if core == which:
                         copy.named().wait_send()
+        for _, copy in made:
+            copy.sent = True
 
 
 class Local:
@@ -335,7 +340,8 @@
 
 
 class Gather:
-    def __init__(self, wire, spots, full, axes, *orders, part=()):
+    def __init__(self, wire, spots, full, axes, *orders, part=(), buffer=None):
+        self.buffer = buffer
         self.wire, self.s, self.full, self.axes, self.part = wire, spots, full, axes, part
         self.orders, self.last = both_cores(orders), {}
 
@@ -352,7 +358,7 @@
         if n == len(self.orders[0][1]):
             self.settle()
             view = partial(self.view, self.axes)
-            self.last[None] = [self.wire.start(view, view, s.core)]
+            self.last[None] = [self.wire.start(view, view, s.core, buffer=self.buffer)]
             return
         before, self.last = self.last, {}
         for core, order in self.orders:
@@ -360,7 +366,9 @@
             def _():
                 arrived(before.get(core, []))
                 view = partial(self.view, order[:n])
-                self.last[core] = [self.wire.start(view, view, peer, core) for peer in s.along[order[n]]]
+                self.last[core] = [
+                    self.wire.start(view, view, peer, core, self.buffer) for peer in s.along[order[n]]
+                ]
 
     def done(self):
         self.settle()
@@ -382,22 +390,20 @@
 
 
 class Scatter:
-    def __init__(self, wire, spots, total, axes, orders, from_core, got, result, away=None, part=()):
+    def __init__(self, wire, spots, total, axes, orders, from_core, got, result, part=()):
         self.wire, self.s, self.total, self.axes, self.part = wire, spots, total, axes, part
         self.orders = [(core, order[::-1]) for core, order in both_cores(orders)]
-        self.from_core, self.got, self.result, self.away = from_core, got, result, away
+        self.from_core, self.got, self.result = from_core, got, result
         self.last = {}
 
     def mine(self, wide, at=None):
-        core = None if self.away is not None else self.s.c
-        return self.total.at[block_index(self.s, self.axes, wide, core, at) + self.part]
+        return self.total.at[block_index(self.s, self.axes, wide, self.s.c, at) + self.part]
 
     def send_core(self):
         s = self.s
-        source = self.total if self.away is None else self.away
         whole = (slice(None),) * (len(self.axes) - 1)
         self.last = [
-            self.wire.start(source.at[(i,) + whole + (1 - s.c,) + self.part],
+            self.wire.start(self.total.at[(i,) + whole + (1 - s.c,) + self.part],
                             self.from_core.at[(i,) + whole + self.part], s.core)
             for i in range(self.from_core.shape[0])
         ]
@@ -490,18 +496,26 @@
 
 
 class Trade:
-    def __init__(self, wire, spots, result, ends):
-        self.s, self.ends = spots, ends
-        width = ends.shape[-1]
+    def __init__(self, wire, spots, halves, ends):
+        self.s, self.ends, self.pieces = spots, ends, len(halves[0])
         for core in range(2):
-            ends[core] = result[:, core * width : (core + 1) * width]
+            for i, piece in enumerate(halves[core]):
+                ends[core, i] = piece
         self.copy = wire.start(ends.at[1 - spots.c], ends.at[2], spots.core)
 
     def finish(self, out, turned=False):
         self.copy.wait_recv()
-        c, own, other = self.s.c, self.ends[self.s.c], self.ends[2]
+        c = self.s.c
+        own, other = (
+            jnp.concatenate([self.ends[k, i] for i in range(self.pieces)], axis=-1) for k in (c, 2)
+        )
         both = jnp.concatenate([jnp.where(c == 0, own, other), jnp.where(c == 0, other, own)], axis=0)
         out[...] = both.T if turned else both
+
+
+def column_halves(total):
+    part = total.shape[-1] // 2
+    return [[total[:, core * part : (core + 1) * part]] for core in range(2)]
 
 
 def row_parts(rows):
@@ -593,15 +607,19 @@
 STEP = 256
 
 
-def forward_kernel(
+def layer_kernel(
     num_z, length,
     tok, cot, w_in, w_out, w_up, w_down_t, kern_t, gains_in, taps_in, twist, table_hbm,
-    out_o, win_o, wout_o, wup_o, gdown_o, kern_o, small_o, proj_o, normed_o, spec_o, filt_o, conv_o,
-    gated_o, resid_o, normed_two_o, gpre_o,
-    win_v, wout_v, wup_v, wdown_v, kern_v, small_v,
+    out_o, grad_in_o, gin_o, gout_o, gup_o, gdn_o, gains_o, gkern_o,
+    win_v, wout_v, wup_v, wdown_v, gdn_v, kern_v, small_v,
     pre_in, pre_out, pre_up, pre_down, pre_kern, w_down, kern,
-    table_v, proj_v, normed_own, normed_v, sig_v, spec_v, filt_v, filt_low, turned_v, conv_v, gated_ch,
-    gated_v, resid_v, normed_two_v, act_v, slope_v, gdown_v, out_v,
+    table_v, proj_v, normed_own, normed_v, sig_v, spec_v, filt_v, turned_v, conv_v, gated_ch,
+    gated_v, resid_v, normed_two_v, act_v, slope_v,
+    core_in, core_out, core_dn, core_kern,
+    got_in, got_out, got_up, got_dn, got_kern,
+    sum_in, sum_out, sum_up, sum_dn, sum_kern,
+    ends_out, ends_up, ends_dn, ends_kern, swap_core, swap_y,
+    gain_v, gain_got,
     send, recv, local,
 ):
     s = Spots(num_z)
@@ -611,7 +629,9 @@
     rows, width = tok.shape
     group, span = width // 2, rows // 2
     hidden = act_v.shape[1]
+    block = width // (4 * num_z)
     me = 2 * y + c
+    chunk, home = spans(me * span, span), spans(c * span, span)
     w_down[...] = w_down_t[...].T
     kern[...] = kern_t[...].T
     small_v[me, 0:2] = gains_in[...].astype(F32)
@@ -634,18 +654,18 @@
         half = src.shape[0] // 2
         pre[c] = src[spans(c * half, half)]
 
-    g_in = [Gather(wire, s, win_v, "zx", "zx", part=(k,)) for k in range(3)]
-    g_kern = Gather(wire, s, kern_v, "zx", "zx")
+    g_in = [Gather(wire, s, win_v, "zx", "zx", part=(k,), buffer="in") for k in range(3)]
+    g_kern = Gather(wire, s, kern_v, "zx", "zx", buffer="kern")
     g_out = Gather(wire, s, wout_v, "yzx", *ORDER_OUT)
-    g_up = [Gather(wire, s, wup_v, "yzx", *ORDER_UP, part=part) for part in row_parts(wup_v.shape[-2])]
-    g_down = [Gather(wire, s, wdown_v, "yzx", *ORDER_DOWN, part=part) for part in row_parts(wdown_v.shape[-2])]
-
+    parts = row_parts(wup_v.shape[-2])
+    g_up = [Gather(wire, s, wup_v, "yzx", *ORDER_UP, part=part, buffer="up") for part in parts]
+    g_down = [Gather(wire, s, wdown_v, "yzx", *ORDER_DOWN, part=part, buffer="down") for part in parts]
     rounds = Rounds([*g_in, g_kern, g_out, *g_up, *g_down])
 
-    def join(i, full):
+    def join(i):
         traded[i].wait_recv()
         pre = pairs[i][1]
-        full[block_index(s, "zx" if i == 0 else "yzx", "", c)] = jnp.concatenate([pre[0], pre[1]], axis=-1)
+        return jnp.concatenate([pre[0], pre[1]], axis=-1)
 
     arrived(trade_in)
     whole = jnp.concatenate([pre_in[k] for k in range(4)], axis=-1)
@@ -657,20 +677,27 @@
 
     arrived(smalls)
     gains = jnp.concatenate([small_v[k] for k in range(4)], axis=-1)
-    normed, _ = norm_parts(tok[...].astype(F32))
-    normed_own[...] = (normed * gains[0:1]).astype(BF)
-    chunk = spans(me * span, span)
+    tile = 128
+
+    def norm_one(i, _):
+        at = spans(i * tile, tile)
+        normed, _ = norm_parts(tok[at].astype(F32))
+        normed_own[at] = (normed * gains[0:1]).astype(BF)
+        return 0
+    lax.fori_loop(0, rows // tile, norm_one, 0)
     to_group = [
-        wire.start(normed_own.at[spans(cc * span, span)], normed_v.at[chunk], peer)
+        wire.start(normed_own.at[spans(cc * span, span)], normed_v.at[chunk], peer, buffer="normed")
         for (yy, cc), peer in zip(s.group, s.mates)
     ]
-    normed_v[chunk] = normed_own[spans(c * span, span)]
-    join(0, kern_v)
-    join(1, wout_v)
-    join(2, wup_v)
-    join(3, wdown_v)
+    normed_v[chunk] = normed_own[home]
+    kern_v[z, x, c] = join(0)
+    wout_v[y, z, x, c] = join(1)
+    both = join(2)
+    pieces = both.shape[-1] // group
+    for q in range(pieces):
+        wup_v[y, z, x, c, q * block : (q + 1) * block] = both[:, q * group : (q + 1) * group]
+    wdown_v[y, z, x, c] = join(3)
     rounds.run(5)
-
 
     arrived(to_group)
     g_in[0].done()
@@ -679,39 +706,44 @@
     def project(k, at):
         return dot(normed_v[at], win_v[:, :, :, k].reshape(width, group))
 
-    tall = length // 2
-    for i in range(2):
-        at = slice(i * tall, (i + 1) * tall)
+    def mix(i, _):
+        at = spans(i * STEP, STEP, STEP)
         value, gate = project(0, at), project(1, at)
         proj_v[0, at] = value.astype(BF)
         proj_v[1, at] = gate.astype(BF)
         sig_v[at] = (value * gate).astype(BF)
+        return 0
+    lax.fori_loop(0, length // STEP, mix, 0)
+    rounds.run()
     g_in[2].done()
+
+    def second_gate(i, _):
+        at = spans(i * STEP, STEP, STEP)
+        proj_v[2, at] = project(2, at).astype(BF)
+        return 0
+    lax.fori_loop(0, length // STEP, second_gate, 0)
     rounds.run()
-    for i in range(2):
-        at = slice(i * tall, (i + 1) * tall)
-        proj_v[2, at] = project(2, at).astype(BF)
-    rounds.run()
 
     g_kern.done()
-    taps = jnp.concatenate([small_v[2 * y], small_v[2 * y + 1]], axis=-1)[2:3]
-    tile = 128
-    for j in range(group // tile):
-        cols = slice(j * tile, (j + 1) * tile)
-        filt = make_filter(kern_v[:, :, :, :, cols].reshape(length, tile).astype(F32), taps[:, cols])
-        filt_low[:, cols] = filt.astype(BF)
+    taps_v = gain_v.at[2, 0:1]
+    taps_v[:, 0:group] = jnp.concatenate([small_v[2 * y], small_v[2 * y + 1]], axis=-1)[2:3]
+
+    def shape_taps(j, _):
+        cols = spans(j * tile, tile, tile)
+        filt = make_filter(kern_v[:, :, :, :, cols].reshape(length, tile).astype(F32), taps_v[:, cols])
+        gated_ch[:, cols] = filt.astype(BF)
+        return 0
+    lax.fori_loop(0, group // tile, shape_taps, 0)
     inner.wait(load_table)
 
     def spectrum(i, _):
         real, imag = spans(i * STEP, STEP, STEP), spans(length + i * STEP, STEP, STEP)
-        re, im = dot(table_v[real], filt_low[...]), dot(table_v[imag], filt_low[...])
+        re, im = dot(table_v[real], gated_ch[...]), dot(table_v[imag], gated_ch[...])
         cosine, sine = twist[real, 0:1], twist[real, 1:2]
         filt_v[real] = (re * cosine + im * sine).astype(BF)
         filt_v[imag] = (im * cosine - re * sine).astype(BF)
         return 0
     lax.fori_loop(0, length // STEP, spectrum, 0)
-
-
     rounds.run()
 
     def convolve(i, _):
@@ -724,7 +756,6 @@
         turned_v[imag] = (re_s * im_f + im_s * re_f).astype(BF)
         return 0
     lax.fori_loop(0, length // STEP, convolve, 0)
-
     rounds.run()
 
     def back(i, _):
@@ -736,15 +767,11 @@
         return 0
     lax.fori_loop(0, length // STEP, back, 0)
 
-    home = spans(c * span, span)
     to_tokens = [
-        wire.start(gated_ch.at[spans((2 * yy + cc) * span, span)], gated_v.at[y, home], peer)
+        wire.start(gated_ch.at[spans((2 * yy + cc) * span, span)], gated_v.at[y, home], peer, buffer="gated")
         for (yy, cc), peer in zip(s.group, s.mates)
     ]
     gated_v[y, home] = gated_ch[chunk]
-    for src, dst in ((win_v, win_o), (kern_v, kern_o), (small_v, small_o), (proj_v, proj_o),
-                     (normed_v, normed_o), (spec_v, spec_o), (filt_v, filt_o), (conv_v, conv_o)):
-        inner.start(src, dst)
     rounds.run()
     g_out.done()
     rounds.run()
@@ -756,46 +783,52 @@
             dot(gated_v[h], wout_v[k, h * num_z // 2 : (h + 1) * num_z // 2].reshape(group, group)) for h in range(2)
         )
         resid_v[:, cols] = tok[:, cols].astype(F32) + mixed
-    normed_two, _ = norm_parts(resid_v[...])
-    normed_two_v[...] = (normed_two * gains[1:2]).astype(BF)
-    for src, dst in ((wout_v, wout_o), (gated_v, gated_o), (resid_v, resid_o), (normed_two_v, normed_two_o)):
-        inner.start(src, dst)
+
+    def norm_two(i, _):
+        at = spans(i * tile, tile)
+        normed, _ = norm_parts(resid_v[at])
+        normed_two_v[at] = (normed * gains[1:2]).astype(BF)
+        return 0
+    lax.fori_loop(0, rows // tile, norm_two, 0)
     rounds.run(2)
     for g in g_up:
         g.done()
 
-    wide = 256
-    per = hidden // 2 // wide
+    def piece(ref, j):
+        return ref.at[j // pieces, :, :, :, spans((j % pieces) * block, block)]
 
     def feed(j, _):
-        weight = wup_v[j // per, :, :, :, :, spans((j % per) * wide, wide, wide)].reshape(width, wide)
-        act, slope = gelu_both(dot(normed_two_v[...], weight))
-        at = spans(j * wide, wide, wide)
-        act_v[:, at] = act.astype(BF)
-        slope_v[:, at] = slope.astype(BF)
-        return 0
-    lax.fori_loop(0, per, feed, 0)
+        weight, cols = piece(wup_v, j)[...].reshape(width, group), spans(j * group, group, 128)
+
+        def rows_of(i, _):
+            at = spans(i * span // 2, span // 2)
+            act, slope = gelu_both(dot(normed_two_v[at], weight))
+            act_v[at, cols] = act.astype(BF)
+            slope_v[at, cols] = slope.astype(BF)
+            return 0
+        return lax.fori_loop(0, 4, rows_of, 0)
+    lax.fori_loop(0, pieces, feed, 0)
     rounds.run()
-    lax.fori_loop(per, 2 * per, feed, 0)
-    inner.start(wup_v, wup_o)
-
+    lax.fori_loop(pieces, 2 * pieces, feed, 0)
     rounds.run()
 
+    down = [Scatter(wire, s, gdn_v, "yzx", ORDER_DOWN, core_dn, got_dn, sum_dn, part=part) for part in parts]
     deep = hidden // (2 * num_z)
 
     def down_grad(i, _):
-        grad = dot_rows(act_v[:, spans(i * deep, deep, deep)], cot[...]).astype(BF)
+        grad = dot_rows(act_v[:, spans(i * deep, deep, 128)], cot[...]).astype(BF)
         for h in range(2):
-            gdown_v[h, i // 2, i % 2] = grad[:, h * group : (h + 1) * group].reshape(2, deep // 2, group)
+            gdn_v[h, i // 2, i % 2] = grad[:, h * group : (h + 1) * group].reshape(2, deep // 2, group)
         return 0
     lax.fori_loop(0, 2 * num_z, down_grad, 0)
-    inner.start(gdown_v, gdown_o)
     rounds.run()
+    for g in down:
+        g.send_core()
     for g in g_down:
         g.done()
 
     def pre_grad(i, _):
-        at = spans(i * deep, deep, deep)
+        at = spans(i * deep, deep, 128)
         grad = sum(
             dot_cols(cot[:, h * group : (h + 1) * group], wdown_v[h, i // 2, i % 2].reshape(deep, group))
             for h in range(2)
@@ -803,127 +836,48 @@
         slope_v[:, at] = (slope_v[:, at].astype(F32) * grad).astype(BF)
         return 0
     lax.fori_loop(0, 2 * num_z, pre_grad, 0)
-    inner.start(slope_v, gpre_o)
-    for h in range(2):
-        cols = slice(h * group, (h + 1) * group)
-        out_v[:, cols] = (resid_v[:, cols] + dot(act_v[...], wdown_v[h].reshape(hidden, group))).astype(BF)
-    inner.start(out_v, out_o)
-    wire.drain()
-    inner.drain()
-
-
-def vm(shape, dtype=BF):
-    return pltpu.VMEM(tuple(shape), dtype)
-
-
-VMEM_SPEC, HBM_SPEC = pl.BlockSpec(memory_space=pltpu.VMEM), pl.BlockSpec(memory_space=pl.ANY)
-
-
-def forward(num_z, length, tokens, cot, w_in, w_out, w_up, w_down_t, kernel_t, gains, taps, twist, table):
-    rows, width = tokens.shape
-    group = width // 2
-    part = w_down_t.shape[1]
-    hidden = part * num_z * 2
-    sds = jax.ShapeDtypeStruct
-    axes = (2, num_z, 2, 2)
-    win = axes[1:] + (3, w_in.shape[0] // 2, group)
-    wout, wup, wdown = axes + (w_out.shape[0] // 2, group), axes + (w_up.shape[0] // 2, hidden // 2), axes + (part // 2, group)
-    kern = axes[1:] + (kernel_t.shape[1] // 2, group)
-    small = (4, 8, width // 4)
-    acts = dict(
-        proj=((3, length, group), BF), normed=((length, width), BF), spec=((2 * length, group), BF),
-        filt=((2 * length, group), BF), conv=((length, group), BF), gated=((2, rows, group), BF),
-        resid=((rows, width), F32), normed_two=((rows, width), BF), gpre=((rows, hidden), BF),
-    )
-    outs = [sds((rows, width), BF)] + [sds(w, BF) for w in (win, wout, wup, wdown, kern)] + [sds(small, F32)]
-    outs += [sds(*acts[k]) for k in acts]
-    act = lambda k: vm(*acts[k])
-    scratch = [vm(w) for w in (win, wout, wup, wdown, kern)] + [vm(small, F32)]
-    scratch += [vm((4, w_in.shape[0] // 2, w_in.shape[1])), vm((2, w_out.shape[0] // 2, w_out.shape[1])),
-                vm((2, w_up.shape[0] // 2, w_up.shape[1])), vm((2, part // 2, w_down_t.shape[0])),
-                vm((2, kernel_t.shape[1] // 2, kernel_t.shape[0])), vm(w_down_t.shape[::-1]), vm(kernel_t.shape[::-1])]
-    scratch += [vm(table.shape), act("proj"), vm((rows, width)), act("normed"), vm((length, group)), act("spec"),
-                act("filt"), vm((length, group)), vm((2 * length, group)), act("conv"), vm((length, group)),
-                act("gated"), act("resid"), act("normed_two"), act("gpre"), act("gpre"), vm(wdown), vm((rows, width))]
-    scratch += [pltpu.SemaphoreType.DMA((160,)), pltpu.SemaphoreType.DMA((160,)), pltpu.SemaphoreType.DMA((40,))]
-    return pl.pallas_call(
-        partial(forward_kernel, num_z, length),
-        out_shape=outs,
-        in_specs=[VMEM_SPEC] * 10 + [HBM_SPEC],
-        out_specs=[HBM_SPEC] * len(outs),
-        scratch_shapes=scratch,
-        compiler_params=pltpu.CompilerParams(collective_id=0, has_side_effects=True, vmem_limit_bytes=61 * 2**20),
-        cost_estimate=pl.CostEstimate(flops=17 * 10**9, bytes_accessed=50 * 10**6, transcendentals=2 * 10**6),
-    )(tokens, cot, w_in, w_out, w_up, w_down_t, kernel_t, gains, taps, twist, table)
-
-
-def backward_kernel(
-    num_z, length,
-    tok, cot, twist, small_v, table_h, win_h, wout_h, wup_h, gdown_h, kern_h, proj_h, normed_h, spec_h,
-    filt_h, conv_h, gated_h, resid_h, normed_two_h, gpre_h,
-    grad_in_o, gin_o, gout_o, gup_o, gdn_o, gains_o, gkern_o,
-    table_v, win_v, wout_v, wup_v, kern_v, proj_v, normed_v, spec_v, filt_v, conv_v,
-    gated_v, resid_v, normed_two_v, gpre_v,
-    gup_v, gdn_v, gkern_v,
-    core_in, core_out, core_up, core_dn, core_kern,
-    got_in, got_out, got_up, got_dn, got_kern,
-    sum_in, sum_out, sum_up, sum_dn, sum_kern,
-    ends_out, ends_up, ends_dn, ends_kern, swap_core, swap_y,
-    low_v, ggate_v, gch_v, gnorm_got, gain_v, gain_got,
-    send, recv, local,
-):
-    s = Spots(num_z)
-    z, x, y, c = s.z, s.x, s.y, s.c
-    wire, inner = Wire(send, recv, s), Local(local)
-    rows, width = tok.shape
-    group, span = width // 2, rows // 2
-    hidden = gpre_v.shape[1]
-    me = 2 * y + c
-    own_dn = [inner.start(gdown_h.at[i, :, :, c], gdn_v.at[i]) for i in range(2)]
-    loads = {}
-    for name, src, dst in (
-        ("gpre", gpre_h, gpre_v), ("wup", wup_h, wup_v), ("normed_two", normed_two_h, normed_two_v),
-        ("resid", resid_h, resid_v), ("wout", wout_h, wout_v), ("proj", proj_h, proj_v), ("conv", conv_h, conv_v),
-        ("gated", gated_h, gated_v), ("table", table_h, table_v), ("spec", spec_h, spec_v), ("filt", filt_h, filt_v),
-        ("kern", kern_h, kern_v), ("normed", normed_h, normed_v), ("win", win_h, win_v),
-    ):
-        loads[name] = inner.start(src, dst)
-
-    def need(*names):
-        for name in names:
-            inner.wait(loads[name])
-
-    s.meet()
-    block = width // (4 * num_z)
-    gout_v = wup_v.at[:, :, :, :, :, 0:group]
-    gin_v = win_v
-    down = [Scatter(wire, s, gdn_v, "yzx", ORDER_DOWN, core_dn, got_dn, sum_dn, away=gdown_h, part=part)
-            for part in row_parts(gdn_v.shape[-2])]
-    up = [Scatter(wire, s, gup_v, "yzx", ORDER_UP, core_up, got_up, sum_up, part=part)
-          for part in row_parts(gup_v.shape[-2])]
+    gpre_v = slope_v
+    down[0].go(0)
+    down[1].go(0)
+    wire.drain("normed")
+    out_v = low_v = normed_own
+
+    def down_out(i, _):
+        at, cols = spans((i % 2) * span, span), spans(i // 2 * group, group, 128)
+        grown = dot(act_v[at], wdown_v[i // 2].reshape(hidden, group))
+        out_v[at, cols] = (resid_v[at, cols] + grown).astype(BF)
+        return 0
+    lax.fori_loop(0, 4, down_out, 0)
+    store_out = inner.start(out_v, out_o)
+    down[2].go(0)
+
+    gnorm_got = [act_v.at[0:span, 0:width], act_v.at[span:, 0:width], act_v.at[0:span, width : 2 * width]]
+    gout_v, gup_v, gin_v = wup_v.at[:, :, :, :, 0:block], wdown_v, win_v
+    gch_v, gkern_v = sig_v, kern_v
+    ggate_v = gated_ch
+    up = [Scatter(wire, s, gup_v, "yzx", ORDER_UP, core_dn, got_up, sum_up, part=part) for part in parts]
     out = Scatter(wire, s, gout_v, "yzx", ORDER_OUT, core_out, got_out, sum_out)
     into = [Scatter(wire, s, gin_v, "zx", ("zx",), core_in, got_in, sum_in, part=(k,)) for k in range(3)]
     taps_grad = Scatter(wire, s, gkern_v, "zx", ("zx",), core_kern, got_kern, sum_kern)
-    for k in range(3):
-        down[k].send_core()
-    gains = jnp.concatenate([small_v[k] for k in range(4)], axis=-1)
-
-    need("gpre", "wup", "resid")
-    half = hidden // 2
-    grad = sum(
-        dot_cols(gpre_v[:, h * half : (h + 1) * half], wup_v[h].reshape(width, half)) for h in range(2)
-    )
-    normal, scale = norm_parts(resid_v[...])
-    part, gain_two = norm_back(normal, scale, grad, gains[1:2])
-    resid_v[...] = cot[...].astype(F32) + part
-    low_v[...] = resid_v[...].astype(BF)
-
-    for copy in own_dn:
-        inner.wait(copy)
-    down[0].go(0)
-    down[1].go(0)
-
-    need("wout")
+
+    inner.wait(store_out)
+
+    def norm_two_back(i, gain):
+        at = spans(i * span, span)
+
+        def up_back(j, total):
+            weight = piece(wup_v, j)[...].reshape(width, group)
+            return total + dot_cols(gpre_v[at, spans(j * group, group, 128)], weight)
+        grad = lax.fori_loop(0, 2 * pieces, up_back, jnp.zeros((span, width), F32))
+        normal, scale = norm_parts(resid_v[at])
+        part, more = norm_back(normal, scale, grad, gains[1:2])
+        part = cot[at].astype(F32) + part
+        resid_v[at] = part
+        low_v[at] = part.astype(BF)
+        return gain + more
+    gain_two = lax.fori_loop(0, 2, norm_two_back, jnp.zeros((1, width), F32))
+
+    wire.drain("gated")
     for h in range(2):
         grad = sum(
             dot_cols(
@@ -932,44 +886,41 @@
             )
             for k in range(2)
         )
-        ggate_v[h] = grad.astype(BF)
-    chunk, home = spans(me * span, span), spans(c * span, span)
+        ggate_v[h * rows : (h + 1) * rows] = grad.astype(BF)
     to_channels = [
-        wire.start(ggate_v.at[yy, spans(cc * span, span)], gch_v.at[chunk], peer)
+        wire.start(ggate_v.at[spans(yy * rows + cc * span, span)], gch_v.at[chunk], peer)
         for (yy, cc), peer in zip(s.group, s.mates)
     ]
-    gch_v[chunk] = ggate_v[y, home]
-
-    down[2].go(0)
-
-    need("normed_two")
-    wide = 256
-    per = hidden // 2 // wide
-
-    def up_grad(j, _):
-        grad = dot_rows(normed_two_v[...], gpre_v[:, spans(j * wide, wide, wide)]).astype(BF)
-        cols = spans((j % per) * wide, wide, wide)
-        gup_v[j // per, :, :, :, :, cols] = grad.reshape(num_z, 2, 2, block, wide)
-        return 0
-    lax.fori_loop(0, 2 * per, up_grad, 0)
-    for k in range(3):
-        up[k].send_core()
+    gch_v[chunk] = ggate_v[spans(y * rows + c * span, span)]
     down[0].go(1)
     down[1].go(1)
+
+    wire.drain("down")
+
+    def up_grad(j, _):
+        grad = dot_rows(normed_two_v[...], gpre_v[:, spans(j * group, group, 128)]).astype(BF)
+        piece(gup_v, j)[...] = grad.reshape(num_z, 2, 2, block, group)
+        return 0
+    lax.fori_loop(0, 2 * pieces, up_grad, 0)
+    arrived(to_channels[2:])
+    for g in up:
+        g.send_core()
+    down[2].go(1)
     up[0].go(0)
 
-    need("gated")
-    for h in range(2):
-        for k in range(2):
-            grad = dot_rows(gated_v[h], low_v[:, k * group : (k + 1) * group]).astype(BF)
-            gout_v[k, h * num_z // 2 : (h + 1) * num_z // 2] = grad.reshape(num_z // 2, 2, 2, block, group)
+    wire.drain("up")
+
+    def out_grad(i, _):
+        h, k = i // 2, i % 2
+        grad = dot_rows(gated_v[h], low_v[:, spans(k * group, group, 128)]).astype(BF)
+        gout_v[k, pl.ds(h * (num_z // 2), num_z // 2)] = grad.reshape(num_z // 2, 2, 2, block, group)
+        return 0
+    lax.fori_loop(0, 4, out_grad, 0)
     out.send_core()
-    down[2].go(1)
     down[0].go(2)
     up[1].go(0)
 
-    need("proj", "conv", "table", "spec", "filt")
-    arrived(to_channels)
+    arrived(to_channels[:2])
 
     def gate(i, _):
         at = spans(i * STEP, STEP, STEP)
@@ -997,7 +948,7 @@
     up[0].go(1)
     out.go(0)
 
-    def back(i, _):
+    def signal_back(i, _):
         at, imag = spans(i * STEP, STEP, STEP), spans(length + i * STEP, STEP, STEP)
         both = dot(table_v[at], filt_v[0:length]) + dot(table_v[imag], filt_v[length:])
         grad = (both * (1.0 / length)).astype(BF).astype(F32)
@@ -1005,9 +956,7 @@
         proj_v[0, at] = (grad * first).astype(BF)
         proj_v[1, at] = (grad * value).astype(BF)
         return 0
-    lax.fori_loop(0, length // STEP, back, 0)
-
-    need("normed", "win")
+    lax.fori_loop(0, length // STEP, signal_back, 0)
 
     def normed_grad(j):
         grad = sum(
@@ -1015,19 +964,27 @@
         )
         return grad.astype(BF)
 
-    to_owner = []
-    for i, ((yy, cc), peer) in enumerate(zip(s.group, s.mates)):
-        place = gpre_v.at[0:span, i * width : (i + 1) * width]
-        place[...] = normed_grad(2 * yy + cc)
-        to_owner.append(wire.start(place, gnorm_got.at[i], peer))
+    def owner_part(i, _):
+        yy, cc = (y + 1 - i // 2) % 2, (c + i // 2 + i) % 2
+        gpre_v[0:span, spans(i * width, width, 128)] = normed_grad(2 * yy + cc)
+        return 0
+    lax.fori_loop(0, 4, owner_part, 0)
+    to_owner = [
+        wire.start(gpre_v.at[0:span, i * width : (i + 1) * width], gnorm_got[i], peer)
+        for i, peer in enumerate(s.mates)
+    ]
     mine = gpre_v.at[0:span, 3 * width : 4 * width]
-    mine[...] = normed_grad(me)
 
     down[2].go(2)
     up[1].go(1)
-    for k in range(3):
+    wire.drain("in")
+
+    def in_grad(k, _):
         grad = dot_rows(normed_v[...], proj_v[k]).astype(BF)
         gin_v[:, :, :, k] = grad.reshape(num_z, 2, 2, block, group)
+        return 0
+    lax.fori_loop(0, 3, in_grad, 0)
+    for k in range(3):
         into[k].send_core()
     up[0].go(2)
     for k in range(3):
@@ -1035,15 +992,16 @@
     up[2].go(1)
     out.go(1)
 
-    need("kern")
-    taps = jnp.concatenate([small_v[2 * y], small_v[2 * y + 1]], axis=-1)[2:3]
-    tile = 128
-    for j in range(group // tile):
-        cols = slice(j * tile, (j + 1) * tile)
+    wire.drain("kern")
+
+    def taps_back(j, _):
+        cols = spans(j * tile, tile, tile)
         both = dot(table_v[0:length], spec_v[0:length, cols]) + dot(table_v[length:], spec_v[length:, cols])
-        grad = kernel_back(kern_v[:, :, :, :, cols].reshape(length, tile).astype(F32), taps[:, cols],
+        grad = kernel_back(kern_v[:, :, :, :, cols].reshape(length, tile).astype(F32), taps_v[:, cols],
                            both * (1.0 / length))
         gkern_v[:, :, :, :, cols] = grad.astype(BF).reshape(num_z, 2, 2, length // (4 * num_z), tile)
+        return 0
+    lax.fori_loop(0, group // tile, taps_back, 0)
     taps_grad.send_core()
     up[1].go(2)
     for k in range(3):
@@ -1053,18 +1011,20 @@
     out.go(2)
     for k in range(3):
         down[k].go(3)
-    trade_dn = Trade(wire, s, sum_dn, ends_dn)
+    trade_dn = Trade(wire, s, column_halves(sum_dn), ends_dn)
     taps_grad.go(1)
 
     arrived(to_owner)
-    across, diagonal, beside = (gnorm_got[i].astype(F32) for i in range(3))
-    here = mine[...].astype(F32) + across
-    there = beside + diagonal
-    first_rows, second_rows = jnp.where(c == 0, here, there), jnp.where(c == 0, there, here)
-    grad = jnp.concatenate([first_rows, second_rows], axis=0)
-    normal, scale = norm_parts(tok[...].astype(F32))
-    part, gain_one = norm_back(normal, scale, grad, gains[0:1])
-    low_v[...] = (resid_v[...] + part).astype(BF)
+
+    def norm_one_back(i, gain):
+        at, within = spans(i * tile, tile), spans(i % (span // tile) * tile, tile)
+        across, diagonal, beside, here = (ref[within].astype(F32) for ref in (*gnorm_got, mine))
+        grad = jnp.where(c == i // (span // tile), here + across, beside + diagonal)
+        normal, scale = norm_parts(tok[at].astype(F32))
+        part, more = norm_back(normal, scale, grad, gains[0:1])
+        low_v[at] = (resid_v[at] + part).astype(BF)
+        return gain + more
+    gain_one = lax.fori_loop(0, rows // tile, norm_one_back, jnp.zeros((1, width), F32))
     inner.start(low_v, grad_in_o)
 
     gain_v[0] = jnp.concatenate([gain_one, gain_two, jnp.zeros((6, width), F32)], axis=0)
@@ -1074,9 +1034,14 @@
     got = [wire.start(gain_v.at[1], gain_got.at[3], s.along["x"][0])]
     for k in range(3):
         up[k].go(3)
-    trade_up = Trade(wire, s, sum_up, ends_up)
+    rows_half = pieces // 2 * block
+    column_pieces = [
+        [sum_up[core * rows_half + q * block : core * rows_half + (q + 1) * block] for q in range(pieces // 2)]
+        for core in range(2)
+    ]
+    trade_up = Trade(wire, s, column_pieces, ends_up)
     out.go(3)
-    trade_out = Trade(wire, s, sum_out, ends_out)
+    trade_out = Trade(wire, s, column_halves(sum_out), ends_out)
     arrived(got)
     gain_v[2] = gain_v[1] + gain_got[3]
     got = [wire.start(gain_v.at[2], gain_got.at[3 + k], peer) for k, peer in zip(range(1, num_z), s.along["z"])]
@@ -1089,7 +1054,7 @@
     swaps = [wire.start(swap_y.at[0], swap_y.at[1], s.mates[0]), wire.start(swap_y.at[0], swap_y.at[2], s.mates[1]),
              wire.start(swap_core.at[0], swap_core.at[1], s.core)]
     taps_grad.go(2)
-    trade_kern = Trade(wire, s, sum_kern, ends_kern)
+    trade_kern = Trade(wire, s, column_halves(sum_kern), ends_kern)
     trade_dn.finish(gdn_o, turned=True)
     trade_up.finish(gup_o)
     trade_out.finish(gout_o)
@@ -1114,40 +1079,56 @@
     inner.drain()
 
 
-def backward(num_z, length, tokens, cot, twist, small_f, table, full):
+def vm(shape, dtype=BF):
+    return pltpu.VMEM(tuple(shape), dtype)
+
+
+VMEM_SPEC, HBM_SPEC = pl.BlockSpec(memory_space=pltpu.VMEM), pl.BlockSpec(memory_space=pl.ANY)
+
+
+def layer(num_z, length, tokens, cot, w_in, w_out, w_up, w_down_t, kernel_t, gains, taps, twist, table):
     rows, width = tokens.shape
     group = width // 2
+    part = w_down_t.shape[1]
+    hidden = part * num_z * 2
+    block = w_in.shape[0] // 2
     sds = jax.ShapeDtypeStruct
-    win, wout, wup, gdown, kern, proj, normed, spec, filt, conv, gated, resid, normed_two, gpre = full
-    like = lambda a: vm(a.shape, a.dtype)
-    weights = (win, wout, wup, gdown, kern)
-    blocks = [a.shape[-2:] for a in weights]
-    blocks[0] = win.shape[-3:]
-    counts = [7, 15, 15, 15, 7]
-    outs = [sds((rows, width), BF), sds((2 * win.shape[-2], width * 3 // 4), F32)]
-    outs += [sds((2 * w.shape[-2], w.shape[-1] // 2), F32) for w in (wout, wup)]
-    outs += [sds((gdown.shape[-1] // 2, 2 * gdown.shape[-2]), F32), sds((2, width // 4), F32)]
-    outs += [sds((kern.shape[-1] // 2, 2 * kern.shape[-2]), F32)]
-    scratch = [like(a) for a in (table, win, wout, wup, kern, proj, normed, spec, filt, conv, gated, resid,
-                                 normed_two, gpre)]
-    scratch += [like(wup), vm(gdown.shape[:3] + gdown.shape[4:]), like(kern)]
-    scratch += [vm(win.shape[:2] + win.shape[3:])] + [vm(w.shape[:3] + w.shape[4:]) for w in (wout, wup, gdown)]
-    scratch += [vm(kern.shape[:2] + kern.shape[3:])]
-    scratch += [vm((n,) + b) for n, b in zip(counts, blocks)] + [vm(b, F32) for b in blocks]
-    scratch += [vm((3, b[0], b[1] // 2), F32) for b in blocks[1:]]
-    scratch += [vm((2, 2) + blocks[0][1:]), vm((3,) + blocks[0][1:])]
-    scratch += [vm((rows, width)), vm((2, rows, group)), vm((length, group)), vm((3, rows // 2, width)),
-                vm((3, 8, width), F32), vm((3 + num_z, 8, width), F32)]
-    scratch += [pltpu.SemaphoreType.DMA((160,)), pltpu.SemaphoreType.DMA((160,)), pltpu.SemaphoreType.DMA((40,))]
+    axes = (2, num_z, 2, 2)
+    units = dict(
+        win=(3, block, group), wout=(block, group), wup=(hidden // width * block, group), wdown=(part // 2, group),
+        kern=(kernel_t.shape[1] // 2, group),
+    )
+    lead = {name: axes[1:] if name in ("win", "kern") else axes for name in units}
+    outs = [sds((rows, width), BF)] * 2
+    outs += [sds((w.shape[0], w.shape[1]), F32) for w in (w_in, w_out, w_up, w_down_t)]
+    outs += [sds((2, width // 4), F32), sds(kernel_t.shape, F32)]
+    channel = vm((length, group))
+    both = vm((2 * length, group))
+    token = vm((rows, width))
+    scratch = [vm(lead[name] + units[name]) for name in ("win", "wout", "wup", "wdown", "wdown", "kern")]
+    scratch += [vm((4, 8, width // 4), F32)]
+    scratch += [vm((4, block, w_in.shape[1])), vm((2, block, w_out.shape[1])), vm((2, block, w_up.shape[1])),
+                vm((2, part // 2, w_down_t.shape[0])), vm((2, kernel_t.shape[1] // 2, kernel_t.shape[0])),
+                vm(w_down_t.shape[::-1]), vm(kernel_t.shape[::-1])]
+    scratch += [vm(table.shape), vm((3, length, group)), token, vm((length, width)), channel, both, both, both, channel,
+                channel, vm((2, rows, group)), vm((rows, width), F32), token, vm((rows, hidden)), vm((rows, hidden))]
+    names = ("win", "wout", "wup", "wdown", "kern")
+    scratch += [vm(lead[name][:-1] + units[name]) for name in names if name != "wup"]
+    blocks = {name: math.prod(lead[name]) // 2 - 1 for name in names}
+    scratch += [vm((blocks[name],) + units[name]) for name in names] + [vm(units[name], F32) for name in names]
+    scratch += [vm((3, 1, block, group // 2), F32), vm((3, hidden // width // 2, block, group), F32),
+                vm((3, 1, part // 2, group // 2), F32), vm((3, 1, kernel_t.shape[1] // 2, group // 2), F32)]
+    scratch += [vm((2, 2, block, group)), vm((3, block, group)), vm((3, 8, width), F32), vm((3 + num_z, 8, width), F32)]
+    scratch += [pltpu.SemaphoreType.DMA((320,)), pltpu.SemaphoreType.DMA((320,)), pltpu.SemaphoreType.DMA((8,))]
     return pl.pallas_call(
-        partial(backward_kernel, num_z, length),
+        partial(layer_kernel, num_z, length),
         out_shape=outs,
-        in_specs=[VMEM_SPEC] * 4 + [HBM_SPEC] * 15,
-        out_specs=[HBM_SPEC] + [VMEM_SPEC] * 6,
+        in_specs=[VMEM_SPEC] * 10 + [HBM_SPEC],
+        out_specs=[HBM_SPEC] * 2 + [VMEM_SPEC] * 6,
         scratch_shapes=scratch,
-        compiler_params=pltpu.CompilerParams(collective_id=1, has_side_effects=True, vmem_limit_bytes=63 * 2**20),
-        cost_estimate=pl.CostEstimate(flops=17 * 10**9, bytes_accessed=50 * 10**6, transcendentals=2 * 10**6),
-    )(tokens, cot, twist, small_f, table, *full)
+        compiler_params=pltpu.CompilerParams(collective_id=0, has_side_effects=True, vmem_limit_bytes=63 * 2**20),
+        cost_estimate=pl.CostEstimate(flops=34 * 10**9, bytes_accessed=20 * 10**6, transcendentals=2 * 10**6),
+    )(tokens, cot, w_in, w_out, w_up, w_down_t, kernel_t, gains, taps, twist, table)
 
 
 def publish(*arrays):
@@ -1175,13 +1156,11 @@
         return general_body(tokens_in, w_in, w_out, w_up, w_down, norm_gains, kernel, taps, cotangent)
     width = tokens_in.shape[-1]
     length = kernel.shape[0] * num_dp
-    num_z = num_dp // 2
     table, twist = jnp.asarray(transform_table(length)), jnp.asarray(twist_table(length))
     tokens, cot = tokens_in.reshape(-1, width), cotangent.reshape(-1, width)
-    out, win, wout, wup, gdown, kern, small, *saved = forward(
-        num_z, length, tokens, cot, w_in, w_out, w_up, w_down.T, kernel.T, norm_gains, taps[None], twist, table)
-    results = backward(num_z, length, tokens, cot, twist, small, table, [win, wout, wup, gdown, kern, *saved])
-    out, grad_in, gin, gout, gup, gdn, gains, gkern = publish(out, *results)
+    results = layer(num_dp // 2, length, tokens, cot, w_in, w_out, w_up, w_down.T, kernel.T, norm_gains, taps[None],
+                    twist, table)
+    out, grad_in, gin, gout, gup, gdn, gains, gkern = publish(*results)
     return (out.reshape(tokens_in.shape), grad_in.reshape(tokens_in.shape), gin, gout, gup, gdn.T, gains, gkern.T)
 
 

time: 204 us -> 189 us (0.926)
  Pallas kernels: 203 us -> 187 us
    pallas_call x2 -> x1, Pallas kernels: 199 us -> 184 us  [layer(): pl.pallas_call(partial(layer_kernel, num_z, length), out_shape=outs, in_s...]
where the time goes in v5:
time: 189 us; the launch traced here: 188 us
  Pallas kernels  187 us (99%)
    pallas_call x1, Pallas kernels, layer(): pl.pallas_call(partial(layer_kernel, num_z, length), out_shape=outs, in_s...  184 us

profile of v5, /device:TPU:0, one launch (start us, length us, event | category | flops | bytes accessed | tf_op | source)
XLA Modules:
  0.0 187.9 jit_solution(18244300346395120128)
XLA Ops:
  0.6 184.0 %shard_map.170 = (bf16[512,768]{1,0:T(8,128)(2,1)}, bf16[512,768]{1,0:T(8,128)(2,1)}, f32[96,576]{1,0:T(8,128)}, f32[96,192]{1,0:T(8,128)}, f32[96,768]{1,0:T(8,...) custom-call(bf16[512,768]{1,0:T(8,128)(2,1)} %bitcast.9, bf16[512,768]{1,0:T(8,128)(2,1)} %bitcast.10, ...), custom_call_target="tpu_custom_call" | custom-call | flops 33999998976 | bytes 20000000 | tf_op jit(solution)/shard_map/pallas_call | solution.py:1123
  184.7 3.2 %shard_map.171 = (bf16[512,768]{1,0:T(8,128)(2,1)}, bf16[512,768]{1,0:T(8,128)(2,1)}, f32[96,576]{1,0:T(8,128)}, f32[96,192]{1,0:T(8,128)}, f32[96,768]{1,0:T(8,...) custom-call(bf16[512,768]{1,0:T(8,128)(2,1)} %get-tuple-element.24.refs_0_, ...), custom_call_target="tpu_custom_call" | custom-call | tf_op jit(solution)/shard_map/pallas_call | solution.py:1139

commit v6 on v5

--- a/solution.py
+++ b/solution.py
@@ -321,12 +321,12 @@
     def on(self, core):
         return (lambda body: body()) if core is None else pl.when(self.c == core)
 
+    def greet(self):
+        for peer in self.along["z"] + self.along["x"] + self.mates:
+            pl.semaphore_signal(pltpu.get_barrier_semaphore(), inc=1, device_id=peer, device_id_type=MESH)
+
     def meet(self):
-        barrier = pltpu.get_barrier_semaphore()
-        peers = self.along["z"] + self.along["x"] + self.mates
-        for peer in peers:
-            pl.semaphore_signal(barrier, inc=1, device_id=peer, device_id_type=MESH)
-        pl.semaphore_wait(barrier, len(peers))
+        pl.semaphore_wait(pltpu.get_barrier_semaphore(), len(self.along["z"] + self.along["x"] + self.mates))
 
 
 def both_cores(orders):
@@ -601,9 +601,12 @@
 
 
 ORDER_OUT = ("zxy", "zyx")
-ORDER_UP = ("zxy", "zyx")
+ORDER_UP = ("zxy", "yzx")
 ORDER_DOWN = ("zxy", "yzx")
-PARTS = 3
+BACK_OUT = ("zxy", "zyx")
+BACK_UP = ("zxy", "yzx")
+BACK_DOWN = ("zxy", "yzx")
+PARTS = 4
 STEP = 256
 
 
@@ -636,13 +639,21 @@
     kern[...] = kern_t[...].T
     small_v[me, 0:2] = gains_in[...].astype(F32)
     small_v[me, 2:3] = taps_in[...].astype(F32)
+    tile = 128
+
+    def norm_one(i, _):
+        at = spans(i * tile, tile)
+        resid_v[at], _ = norm_parts(tok[at].astype(F32))
+        return 0
+    s.greet()
+    lax.fori_loop(0, rows // tile, norm_one, 0)
     s.meet()
 
+    smalls = [wire.start(small_v.at[me], small_v.at[me], peer) for peer in s.mates]
     half = w_in.shape[0] // 2
     trade_in = [
         wire.start(w_in.at[spans(cc * half, half)], pre_in.at[me], peer) for (yy, cc), peer in zip(s.group, s.mates)
     ]
-    smalls = [wire.start(small_v.at[me], small_v.at[me], peer) for peer in s.mates]
     pairs = [(kern, pre_kern), (w_out, pre_out), (w_up, pre_up), (w_down, pre_down)]
     traded = []
     for src, pre in pairs:
@@ -667,6 +678,19 @@
         pre = pairs[i][1]
         return jnp.concatenate([pre[0], pre[1]], axis=-1)
 
+    arrived(smalls)
+    gains = jnp.concatenate([small_v[k] for k in range(4)], axis=-1)
+
+    def normed_rows(i, _):
+        at = spans(i * tile, tile)
+        normed_own[at] = (resid_v[at] * gains[0:1]).astype(BF)
+        return 0
+    lax.fori_loop(0, rows // tile, normed_rows, 0)
+    to_group = [
+        wire.start(normed_own.at[spans(cc * span, span)], normed_v.at[chunk], peer, buffer="normed")
+        for (yy, cc), peer in zip(s.group, s.mates)
+    ]
+    normed_v[chunk] = normed_own[home]
     arrived(trade_in)
     whole = jnp.concatenate([pre_in[k] for k in range(4)], axis=-1)
     for k in range(3):
@@ -675,21 +699,6 @@
         if k < 2:
             rounds.run()
 
-    arrived(smalls)
-    gains = jnp.concatenate([small_v[k] for k in range(4)], axis=-1)
-    tile = 128
-
-    def norm_one(i, _):
-        at = spans(i * tile, tile)
-        normed, _ = norm_parts(tok[at].astype(F32))
-        normed_own[at] = (normed * gains[0:1]).astype(BF)
-        return 0
-    lax.fori_loop(0, rows // tile, norm_one, 0)
-    to_group = [
-        wire.start(normed_own.at[spans(cc * span, span)], normed_v.at[chunk], peer, buffer="normed")
-        for (yy, cc), peer in zip(s.group, s.mates)
-    ]
-    normed_v[chunk] = normed_own[home]
     kern_v[z, x, c] = join(0)
     wout_v[y, z, x, c] = join(1)
     both = join(2)
@@ -790,29 +799,24 @@
         normed_two_v[at] = (normed * gains[1:2]).astype(BF)
         return 0
     lax.fori_loop(0, rows // tile, norm_two, 0)
-    rounds.run(2)
-    for g in g_up:
-        g.done()
 
     def piece(ref, j):
         return ref.at[j // pieces, :, :, :, spans((j % pieces) * block, block)]
 
-    def feed(j, _):
-        weight, cols = piece(wup_v, j)[...].reshape(width, group), spans(j * group, group, 128)
-
-        def rows_of(i, _):
-            at = spans(i * span // 2, span // 2)
-            act, slope = gelu_both(dot(normed_two_v[at], weight))
+    for q in range(pieces):
+        g_up[q].done()
+
+        def feed(i, _):
+            j = i // 2 * pieces + q
+            at, cols = spans(i % 2 * span, span), spans(j * group, group, 128)
+            act, slope = gelu_both(dot(normed_two_v[at], piece(wup_v, j)[...].reshape(width, group)))
             act_v[at, cols] = act.astype(BF)
             slope_v[at, cols] = slope.astype(BF)
             return 0
-        return lax.fori_loop(0, 4, rows_of, 0)
-    lax.fori_loop(0, pieces, feed, 0)
-    rounds.run()
-    lax.fori_loop(pieces, 2 * pieces, feed, 0)
-    rounds.run()
-
-    down = [Scatter(wire, s, gdn_v, "yzx", ORDER_DOWN, core_dn, got_dn, sum_dn, part=part) for part in parts]
+        lax.fori_loop(0, 4, feed, 0)
+        rounds.run()
+
+    down = [Scatter(wire, s, gdn_v, "yzx", BACK_DOWN, core_dn, got_dn, sum_dn, part=part) for part in parts]
     deep = hidden // (2 * num_z)
 
     def down_grad(i, _):
@@ -824,56 +828,47 @@
     rounds.run()
     for g in down:
         g.send_core()
+    rounds.run()
     for g in g_down:
         g.done()
+    down[0].go(0)
+    down[1].go(0)
 
     def pre_grad(i, _):
-        at = spans(i * deep, deep, 128)
+        at, cols = spans(i // num_z * span, span), spans(i % num_z * 2 * deep, 2 * deep, 128)
         grad = sum(
-            dot_cols(cot[:, h * group : (h + 1) * group], wdown_v[h, i // 2, i % 2].reshape(deep, group))
+            dot_cols(cot[at, h * group : (h + 1) * group], wdown_v[h, i % num_z].reshape(2 * deep, group))
             for h in range(2)
         )
-        slope_v[:, at] = (slope_v[:, at].astype(F32) * grad).astype(BF)
+        slope_v[at, cols] = (slope_v[at, cols].astype(F32) * grad).astype(BF)
         return 0
     lax.fori_loop(0, 2 * num_z, pre_grad, 0)
     gpre_v = slope_v
-    down[0].go(0)
-    down[1].go(0)
+    down[2].go(0)
+    down[3].go(0)
+
     wire.drain("normed")
-    out_v = low_v = normed_own
-
-    def down_out(i, _):
-        at, cols = spans((i % 2) * span, span), spans(i // 2 * group, group, 128)
-        grown = dot(act_v[at], wdown_v[i // 2].reshape(hidden, group))
-        out_v[at, cols] = (resid_v[at, cols] + grown).astype(BF)
-        return 0
-    lax.fori_loop(0, 4, down_out, 0)
-    store_out = inner.start(out_v, out_o)
-    down[2].go(0)
-
-    gnorm_got = [act_v.at[0:span, 0:width], act_v.at[span:, 0:width], act_v.at[0:span, width : 2 * width]]
-    gout_v, gup_v, gin_v = wup_v.at[:, :, :, :, 0:block], wdown_v, win_v
+    low_v = normed_own
+    gnorm_got = [[turned_v.at[(2 * i + h) * span : (2 * i + h + 1) * span] for h in range(2)] for i in range(3)]
+    gout_v, gup_v, gin_v = wdown_v.at[:, :, :, :, 0:block], wup_v, win_v
     gch_v, gkern_v = sig_v, kern_v
     ggate_v = gated_ch
-    up = [Scatter(wire, s, gup_v, "yzx", ORDER_UP, core_dn, got_up, sum_up, part=part) for part in parts]
-    out = Scatter(wire, s, gout_v, "yzx", ORDER_OUT, core_out, got_out, sum_out)
+    up = [Scatter(wire, s, gup_v, "yzx", BACK_UP, core_dn, got_up, sum_up, part=part) for part in parts]
+    out = Scatter(wire, s, gout_v, "yzx", BACK_OUT, core_out, got_out, sum_out)
     into = [Scatter(wire, s, gin_v, "zx", ("zx",), core_in, got_in, sum_in, part=(k,)) for k in range(3)]
     taps_grad = Scatter(wire, s, gkern_v, "zx", ("zx",), core_kern, got_kern, sum_kern)
 
-    inner.wait(store_out)
 
     def norm_two_back(i, gain):
         at = spans(i * span, span)
 
-        def up_back(j, total):
-            weight = piece(wup_v, j)[...].reshape(width, group)
-            return total + dot_cols(gpre_v[at, spans(j * group, group, 128)], weight)
-        grad = lax.fori_loop(0, 2 * pieces, up_back, jnp.zeros((span, width), F32))
+        grad = sum(
+            dot_cols(gpre_v[at, j * group : (j + 1) * group], piece(wup_v, j)[...].reshape(width, group))
+            for j in range(2 * pieces)
+        )
         normal, scale = norm_parts(resid_v[at])
         part, more = norm_back(normal, scale, grad, gains[1:2])
-        part = cot[at].astype(F32) + part
-        resid_v[at] = part
-        low_v[at] = part.astype(BF)
+        low_v[at] = (cot[at].astype(F32) + part).astype(BF)
         return gain + more
     gain_two = lax.fori_loop(0, 2, norm_two_back, jnp.zeros((1, width), F32))
 
@@ -892,23 +887,34 @@
         for (yy, cc), peer in zip(s.group, s.mates)
     ]
     gch_v[chunk] = ggate_v[spans(y * rows + c * span, span)]
-    down[0].go(1)
-    down[1].go(1)
-
-    wire.drain("down")
-
-    def up_grad(j, _):
+    wire.drain("up")
+
+    def up_grad(q, yy, _):
+        j = yy * pieces + q
         grad = dot_rows(normed_two_v[...], gpre_v[:, spans(j * group, group, 128)]).astype(BF)
         piece(gup_v, j)[...] = grad.reshape(num_z, 2, 2, block, group)
         return 0
-    lax.fori_loop(0, 2 * pieces, up_grad, 0)
-    arrived(to_channels[2:])
-    for g in up:
-        g.send_core()
-    down[2].go(1)
-    up[0].go(0)
-
-    wire.drain("up")
+
+    for q in range(pieces):
+        lax.fori_loop(0, 2, partial(up_grad, q), 0)
+        if q == 0:
+            arrived(to_channels[2:])
+        up[q].send_core()
+        if q % 2:
+            down[q - 1].go(1)
+            down[q].go(1)
+            up[q - 1].go(0)
+
+    def down_out(i, _):
+        at = spans(i * span, span)
+        grown = jnp.concatenate([dot(act_v[at], wdown_v[h].reshape(hidden, group)) for h in range(2)], axis=-1)
+        act_v[at, 0:width] = (resid_v[at] + grown).astype(BF)
+        return 0
+    lax.fori_loop(0, 2, down_out, 0)
+    inner.start(act_v.at[:, 0:width], out_o)
+    up[1].go(0)
+    up[3].go(0)
+    wire.drain("down")
 
     def out_grad(i, _):
         h, k = i // 2, i % 2
@@ -918,7 +924,7 @@
     lax.fori_loop(0, 4, out_grad, 0)
     out.send_core()
     down[0].go(2)
-    up[1].go(0)
+    down[1].go(2)
 
     arrived(to_channels[:2])
 
@@ -929,6 +935,13 @@
         proj_v[2, at] = (grad * conv_v[at].astype(F32)).astype(BF)
         return 0
     lax.fori_loop(0, length // STEP, gate, 0)
+
+    wire.drain("in")
+
+    def in_grad(k):
+        grad = dot_rows(normed_v[...], proj_v[k]).astype(BF)
+        gin_v[:, :, :, k] = grad.reshape(num_z, 2, 2, block, group)
+        into[k].send_core()
 
     def turn(i, _):
         real, imag = spans(i * STEP, STEP, STEP), spans(length + i * STEP, STEP, STEP)
@@ -943,9 +956,10 @@
         spec_v[imag] = (im_k * cosine + re_k * sine).astype(BF)
         return 0
     lax.fori_loop(0, length // STEP, turn, 0)
-    down[1].go(2)
-    up[2].go(0)
+    down[2].go(2)
+    down[3].go(2)
     up[0].go(1)
+    up[1].go(1)
     out.go(0)
 
     def signal_back(i, _):
@@ -958,38 +972,30 @@
         return 0
     lax.fori_loop(0, length // STEP, signal_back, 0)
 
-    def normed_grad(j):
+    def part_at(j, h):
+        return gpre_v.at[spans(j % 2 * span, span), spans(j // 2 * width + h * group, group, 128)]
+
+    to_owner = []
+    for h in range(2):
         grad = sum(
-            dot_cols(proj_v[k, spans(j * span, span)], win_v[:, :, :, k].reshape(width, group)) for k in range(3)
-        )
-        return grad.astype(BF)
-
-    def owner_part(i, _):
-        yy, cc = (y + 1 - i // 2) % 2, (c + i // 2 + i) % 2
-        gpre_v[0:span, spans(i * width, width, 128)] = normed_grad(2 * yy + cc)
-        return 0
-    lax.fori_loop(0, 4, owner_part, 0)
-    to_owner = [
-        wire.start(gpre_v.at[0:span, i * width : (i + 1) * width], gnorm_got[i], peer)
-        for i, peer in enumerate(s.mates)
-    ]
-    mine = gpre_v.at[0:span, 3 * width : 4 * width]
-
-    down[2].go(2)
-    up[1].go(1)
-    wire.drain("in")
-
-    def in_grad(k, _):
-        grad = dot_rows(normed_v[...], proj_v[k]).astype(BF)
-        gin_v[:, :, :, k] = grad.reshape(num_z, 2, 2, block, group)
-        return 0
-    lax.fori_loop(0, 3, in_grad, 0)
+            dot_cols(proj_v[k], win_v[h * num_z // 2 : (h + 1) * num_z // 2, :, :, k].reshape(group, group))
+            for k in range(3)
+        ).astype(BF)
+        for j in range(4):
+            part_at(j, h)[...] = grad[j * span : (j + 1) * span]
+        to_owner += [
+            wire.start(partial(part_at, 2 * yy + cc, h), gnorm_got[i][h], peer)
+            for i, ((yy, cc), peer) in enumerate(zip(s.group, s.mates))
+        ]
+
+    up[2].go(1)
+    up[3].go(1)
     for k in range(3):
-        into[k].send_core()
+        in_grad(k)
     up[0].go(2)
     for k in range(3):
         into[k].go(0)
-    up[2].go(1)
+    up[1].go(2)
     out.go(1)
 
     wire.drain("kern")
@@ -1003,26 +1009,29 @@
         return 0
     lax.fori_loop(0, group // tile, taps_back, 0)
     taps_grad.send_core()
-    up[1].go(2)
     for k in range(3):
         into[k].go(1)
     taps_grad.go(0)
     up[2].go(2)
-    out.go(2)
-    for k in range(3):
+    up[3].go(2)
+    for k in range(4):
         down[k].go(3)
     trade_dn = Trade(wire, s, column_halves(sum_dn), ends_dn)
     taps_grad.go(1)
+    out.go(2)
 
     arrived(to_owner)
 
     def norm_one_back(i, gain):
         at, within = spans(i * tile, tile), spans(i % (span // tile) * tile, tile)
-        across, diagonal, beside, here = (ref[within].astype(F32) for ref in (*gnorm_got, mine))
+        across, diagonal, beside = (
+            jnp.concatenate([ref[within].astype(F32) for ref in pair], axis=-1) for pair in gnorm_got
+        )
+        here = jnp.concatenate([part_at(me, h)[within].astype(F32) for h in range(2)], axis=-1)
         grad = jnp.where(c == i // (span // tile), here + across, beside + diagonal)
         normal, scale = norm_parts(tok[at].astype(F32))
         part, more = norm_back(normal, scale, grad, gains[0:1])
-        low_v[at] = (resid_v[at] + part).astype(BF)
+        low_v[at] = (low_v[at].astype(F32) + part).astype(BF)
         return gain + more
     gain_one = lax.fori_loop(0, rows // tile, norm_one_back, jnp.zeros((1, width), F32))
     inner.start(low_v, grad_in_o)
@@ -1032,7 +1041,7 @@
     arrived(got)
     gain_v[1] = gain_v[0] + gain_got[0] + gain_got[1] + gain_got[2]
     got = [wire.start(gain_v.at[1], gain_got.at[3], s.along["x"][0])]
-    for k in range(3):
+    for k in range(4):
         up[k].go(3)
     rows_half = pieces // 2 * block
     column_pieces = [
@@ -1126,7 +1135,7 @@
         in_specs=[VMEM_SPEC] * 10 + [HBM_SPEC],
         out_specs=[HBM_SPEC] * 2 + [VMEM_SPEC] * 6,
         scratch_shapes=scratch,
-        compiler_params=pltpu.CompilerParams(collective_id=0, has_side_effects=True, vmem_limit_bytes=63 * 2**20),
+        compiler_params=pltpu.CompilerParams(collective_id=0, has_side_effects=True, vmem_limit_bytes=67 * 10**6),
         cost_estimate=pl.CostEstimate(flops=34 * 10**9, bytes_accessed=20 * 10**6, transcendentals=2 * 10**6),
     )(tokens, cot, w_in, w_out, w_up, w_down_t, kernel_t, gains, taps, twist, table)
 

time: 189 us -> 174 us (0.921)
  Pallas kernels: 187 us -> 174 us
    pallas_call x1, Pallas kernels: 184 us -> 170 us  [layer(): pl.pallas_call(partial(layer_kernel, num_z, length), out_shape=outs, in_s...]
where the time goes in v6:
time: 174 us
  Pallas kernels  174 us (100%)
    pallas_call x1, Pallas kernels, layer(): pl.pallas_call(partial(layer_kernel, num_z, length), out_shape=outs, in_s...  170 us

profile of v6, /device:TPU:0, one launch (start us, length us, event | category | flops | bytes accessed | tf_op | source)
XLA Modules:
  0.0 174.3 jit_solution(12025516514650201106)
XLA Ops:
  0.6 170.4 %shard_map.170 = (bf16[512,768]{1,0:T(8,128)(2,1)}, bf16[512,768]{1,0:T(8,128)(2,1)}, f32[96,576]{1,0:T(8,128)}, f32[96,192]{1,0:T(8,128)}, f32[96,768]{1,0:T(8,...) custom-call(bf16[512,768]{1,0:T(8,128)(2,1)} %bitcast.9, bf16[512,768]{1,0:T(8,128)(2,1)} %bitcast.10, ...), custom_call_target="tpu_custom_call" | custom-call | flops 33999998976 | bytes 20000000 | tf_op jit(solution)/shard_map/pallas_call | solution.py:1132
  171.1 3.2 %shard_map.171 = (bf16[512,768]{1,0:T(8,128)(2,1)}, bf16[512,768]{1,0:T(8,128)(2,1)}, f32[96,576]{1,0:T(8,128)}, f32[96,192]{1,0:T(8,128)}, f32[96,768]{1,0:T(8,...) custom-call(bf16[512,768]{1,0:T(8,128)(2,1)} %get-tuple-element.24.refs_0_, ...), custom_call_target="tpu_custom_call" | custom-call | tf_op jit(solution)/shard_map/pallas_call | solution.py:1148

commit v7 on v6

--- a/solution.py
+++ b/solution.py
@@ -925,6 +925,7 @@
     out.send_core()
     down[0].go(2)
     down[1].go(2)
+    out.go(0)
 
     arrived(to_channels[:2])
 
@@ -960,7 +961,6 @@
     down[3].go(2)
     up[0].go(1)
     up[1].go(1)
-    out.go(0)
 
     def signal_back(i, _):
         at, imag = spans(i * STEP, STEP, STEP), spans(length + i * STEP, STEP, STEP)
@@ -995,14 +995,29 @@
     up[0].go(2)
     for k in range(3):
         into[k].go(0)
+
+    def gain_part(j, total):
+        grad = jnp.concatenate([part_at(j, h)[...].astype(F32) for h in range(2)], axis=-1)
+        return total + jnp.sum(grad * normed_v[spans(j * span, span)].astype(F32), axis=0, keepdims=True)
+    gain_one = lax.fori_loop(0, 4, gain_part, jnp.zeros((1, width), F32)) / gains[0:1]
+    gain_v[0] = jnp.concatenate([gain_one, gain_two, jnp.zeros((6, width), F32)], axis=0)
+    gain_got_one = [wire.start(gain_v.at[0], gain_got.at[k], peer) for k, peer in enumerate(s.mates)]
     up[1].go(2)
     out.go(1)
 
     wire.drain("kern")
 
+    def taps_signal(i, _):
+        at, imag = spans(i * STEP, STEP, STEP), spans(length + i * STEP, STEP, STEP)
+        both = dot(table_v[at], spec_v[0:length]) + dot(table_v[imag], spec_v[length:])
+        resid_v[spans(i % tall * STEP, STEP, STEP), spans(i // tall * group, group, 128)] = both
+        return 0
+    tall = rows // STEP
+    lax.fori_loop(0, length // STEP, taps_signal, 0)
+
     def taps_back(j, _):
         cols = spans(j * tile, tile, tile)
-        both = dot(table_v[0:length], spec_v[0:length, cols]) + dot(table_v[length:], spec_v[length:, cols])
+        both = jnp.concatenate([resid_v[:, cols], resid_v[:, spans(group + j * tile, tile, tile)]], axis=0)
         grad = kernel_back(kern_v[:, :, :, :, cols].reshape(length, tile).astype(F32), taps_v[:, cols],
                            both * (1.0 / length))
         gkern_v[:, :, :, :, cols] = grad.astype(BF).reshape(num_z, 2, 2, length // (4 * num_z), tile)
@@ -1014,15 +1029,12 @@
     taps_grad.go(0)
     up[2].go(2)
     up[3].go(2)
-    for k in range(4):
-        down[k].go(3)
-    trade_dn = Trade(wire, s, column_halves(sum_dn), ends_dn)
-    taps_grad.go(1)
-    out.go(2)
-
     arrived(to_owner)
-
-    def norm_one_back(i, gain):
+    arrived(gain_got_one)
+    gain_v[1] = gain_v[0] + gain_got[0] + gain_got[1] + gain_got[2]
+    got = [wire.start(gain_v.at[1], gain_got.at[3], s.along["x"][0])]
+
+    def norm_one_back(i, _):
         at, within = spans(i * tile, tile), spans(i % (span // tile) * tile, tile)
         across, diagonal, beside = (
             jnp.concatenate([ref[within].astype(F32) for ref in pair], axis=-1) for pair in gnorm_got
@@ -1030,17 +1042,18 @@
         here = jnp.concatenate([part_at(me, h)[within].astype(F32) for h in range(2)], axis=-1)
         grad = jnp.where(c == i // (span // tile), here + across, beside + diagonal)
         normal, scale = norm_parts(tok[at].astype(F32))
-        part, more = norm_back(normal, scale, grad, gains[0:1])
+        part, _ = norm_back(normal, scale, grad, gains[0:1])
         low_v[at] = (low_v[at].astype(F32) + part).astype(BF)
-        return gain + more
-    gain_one = lax.fori_loop(0, rows // tile, norm_one_back, jnp.zeros((1, width), F32))
+        return 0
+    lax.fori_loop(0, rows // tile, norm_one_back, 0)
     inner.start(low_v, grad_in_o)
 
-    gain_v[0] = jnp.concatenate([gain_one, gain_two, jnp.zeros((6, width), F32)], axis=0)
-    got = [wire.start(gain_v.at[0], gain_got.at[k], peer) for k, peer in enumerate(s.mates)]
-    arrived(got)
-    gain_v[1] = gain_v[0] + gain_got[0] + gain_got[1] + gain_got[2]
-    got = [wire.start(gain_v.at[1], gain_got.at[3], s.along["x"][0])]
+    for k in range(4):
+        down[k].go(3)
+    trade_dn = Trade(wire, s, column_halves(sum_dn), ends_dn)
+    taps_grad.go(1)
+    out.go(2)
+
     for k in range(4):
         up[k].go(3)
     rows_half = pieces // 2 * block
@@ -1048,12 +1061,12 @@
         [sum_up[core * rows_half + q * block : core * rows_half + (q + 1) * block] for q in range(pieces // 2)]
         for core in range(2)
     ]
+    arrived(got)
+    gain_v[2] = gain_v[1] + gain_got[3]
+    got = [wire.start(gain_v.at[2], gain_got.at[3 + k], peer) for k, peer in zip(range(1, num_z), s.along["z"])]
     trade_up = Trade(wire, s, column_pieces, ends_up)
     out.go(3)
     trade_out = Trade(wire, s, column_halves(sum_out), ends_out)
-    arrived(got)
-    gain_v[2] = gain_v[1] + gain_got[3]
-    got = [wire.start(gain_v.at[2], gain_got.at[3 + k], peer) for k, peer in zip(range(1, num_z), s.along["z"])]
 
     for k in range(3):
         into[k].go(2)

time: 174 us -> 173 us (level)
  Pallas kernels: 174 us -> 172 us
where the time goes in v7:
time: 173 us
  Pallas kernels  172 us (99%)
    pallas_call x1, Pallas kernels, layer(): pl.pallas_call(partial(layer_kernel, num_z, length), out_shape=outs, in_s...  169 us

profile of v7, /device:TPU:0, one launch (start us, length us, event | category | flops | bytes accessed | tf_op | source)
XLA Modules:
  0.0 172.6 jit_solution(5285245551187616312)
XLA Ops:
  0.6 168.7 %shard_map.170 = (bf16[512,768]{1,0:T(8,128)(2,1)}, bf16[512,768]{1,0:T(8,128)(2,1)}, f32[96,576]{1,0:T(8,128)}, f32[96,192]{1,0:T(8,128)}, f32[96,768]{1,0:T(8,...) custom-call(bf16[512,768]{1,0:T(8,128)(2,1)} %bitcast.9, bf16[512,768]{1,0:T(8,128)(2,1)} %bitcast.10, ...), custom_call_target="tpu_custom_call" | custom-call | flops 33999998976 | bytes 20000000 | tf_op jit(solution)/shard_map/pallas_call | solution.py:1145
  169.4 3.2 %shard_map.171 = (bf16[512,768]{1,0:T(8,128)(2,1)}, bf16[512,768]{1,0:T(8,128)(2,1)}, f32[96,576]{1,0:T(8,128)}, f32[96,192]{1,0:T(8,128)}, f32[96,768]{1,0:T(8,...) custom-call(bf16[512,768]{1,0:T(8,128)(2,1)} %get-tuple-element.24.refs_0_, ...), custom_call_target="tpu_custom_call" | custom-call | tf_op jit(solution)/shard_map/pallas_call | solution.py:1161

commit v8 on v7

--- a/solution.py
+++ b/solution.py
@@ -831,8 +831,8 @@
     rounds.run()
     for g in g_down:
         g.done()
-    down[0].go(0)
-    down[1].go(0)
+    for g in down:
+        g.go(0)
 
     def pre_grad(i, _):
         at, cols = spans(i // num_z * span, span), spans(i % num_z * 2 * deep, 2 * deep, 128)
@@ -844,8 +844,6 @@
         return 0
     lax.fori_loop(0, 2 * num_z, pre_grad, 0)
     gpre_v = slope_v
-    down[2].go(0)
-    down[3].go(0)
 
     wire.drain("normed")
     low_v = normed_own
@@ -1154,15 +1152,26 @@
 
 
 def publish(*arrays):
+    count = len(arrays)
+
     def copy_all(*refs):
-        for src, dst in zip(refs[: len(arrays)], refs[len(arrays) :]):
-            dst[...] = src[...]
+        held, sems = refs[2 * count : 3 * count], refs[3 * count]
+        loads = [pltpu.make_async_copy(refs[i], held[i], sems.at[0, i]) for i in range(count)]
+        stores = [pltpu.make_async_copy(held[i], refs[count + i], sems.at[1, i]) for i in range(count)]
+        for load in loads:
+            load.start()
+        for load, store in zip(loads, stores):
+            load.wait()
+            store.start()
+        for store in stores:
+            store.wait()
 
     return pl.pallas_call(
         copy_all,
         out_shape=[jax.ShapeDtypeStruct(a.shape, a.dtype) for a in arrays],
-        in_specs=[VMEM_SPEC] * len(arrays),
-        out_specs=[VMEM_SPEC] * len(arrays),
+        in_specs=[HBM_SPEC] * count,
+        out_specs=[HBM_SPEC] * count,
+        scratch_shapes=[vm(a.shape, a.dtype) for a in arrays] + [pltpu.SemaphoreType.DMA((2, count))],
     )(*arrays)
 
 

time: 173 us -> 172 us (level)
  no operation moved by 1% of the time
where the time goes in v8:
time: 172 us
  Pallas kernels  171 us (99%)
    pallas_call x1, Pallas kernels, layer(): pl.pallas_call(partial(layer_kernel, num_z, length), out_shape=outs, in_s...  169 us

profile of v8, /device:TPU:0, one launch (start us, length us, event | category | flops | bytes accessed | tf_op | source)
XLA Modules:
  0.0 172.3 jit_solution(4406148966234481414)
XLA Ops:
  0.6 168.7 %shard_map.170 = (bf16[512,768]{1,0:T(8,128)(2,1)}, bf16[512,768]{1,0:T(8,128)(2,1)}, f32[96,576]{1,0:T(8,128)}, f32[96,192]{1,0:T(8,128)}, f32[96,768]{1,0:T(8,...) custom-call(bf16[512,768]{1,0:T(8,128)(2,1)} %bitcast.9, bf16[512,768]{1,0:T(8,128)(2,1)} %bitcast.10, ...), custom_call_target="tpu_custom_call" | custom-call | flops 33999998976 | bytes 20000000 | tf_op jit(solution)/shard_map/pallas_call | solution.py:1143
  169.4 2.7 %shard_map.171 = (bf16[512,768]{1,0:T(8,128)(2,1)}, bf16[512,768]{1,0:T(8,128)(2,1)}, f32[96,576]{1,0:T(8,128)}, f32[96,192]{1,0:T(8,128)}, f32[96,768]{1,0:T(8,...) custom-call(bf16[512,768]{1,0:T(8,128)(2,1)} %get-tuple-element.24.refs_0_, ...), custom_call_target="tpu_custom_call" | custom-call | tf_op jit(solution)/shard_map/pallas_call | solution.py:1169
